TPU v7x, 256 devices: a whole 4x4x8 slice. The times are simulated.
256 devices in a mesh: dp: 32 (over x, z_lo, y), tensor: 8 (over z_hi, core).
Axes of the slice: x: 4, y: 4, z: 8 (z_hi: 4, z_lo: 2; z = z_hi * 2 + z_lo), core: 2. Of those that a mesh axis runs over, the one named last changes fastest.
Arguments:
- activations: bfloat16 [32768, 28672], P('dp', 'tensor'), may hold values from -6 to 6
- out_grads: bfloat16 [32768, 8192], P('dp', 'tensor'), may hold values from -6 to 6
- proj_in: bfloat16 [28672, 64], P('tensor'), may hold values from -0.03125 to 0.03125
- proj_out: bfloat16 [8192, 64], P('tensor'), may hold values from -0.0625 to 0.0625
- doc_ids: int32 [32, 1024], P('dp'), may hold values from 0 to 3, never falling along the last dimension, each value on 1 to 512 neighbouring positions
- queries: bfloat16 [8192, 4096], P(('dp', 'tensor')), may hold values from -0.005859375 to 0.005859375
- block_owner: int32 [32], replicated, may hold values from 0 to 31, each once
Outputs:
- scores: float32 [8192, 128], P(('dp', 'tensor'))
Inputs may be any that keep to these rules, and one draw needn't show every extreme that they name: `doc_ids`: each index of dp holds 4 documents as runs of consecutive tokens in rising order, each of 1 to 512 tokens, one of exactly that many. `block_owner`: a permutation.
All inputs are finite; a program needn't handle non-finite values.
Results may differ from a plain program's by a relative error of at most 0.0029.
Values may be sent and summed in bfloat16 or wider, within the bound.
No kernel may reach another device: no remote copies, remote signals or barrier semaphores. Data moves between devices by JAX's collectives and lax.ppermute only.
A program may use at most 64 MiB of HBM per device.

v0:
```python
import jax
import jax.numpy as jnp
from jax import lax
from jax.sharding import PartitionSpec as P

RANK = 64
DOCS_DEV = 4


def doc_features(in_proj, out_proj, labels_now):
    labels = jnp.arange(DOCS_DEV, dtype=jnp.int32)
    onehot = (labels_now[None, :] == labels[:, None]).astype(jnp.float32)
    weighted = onehot[:, :, None] * out_proj[None, :, :]
    features = jnp.einsum("dti,tj->dij", weighted, in_proj, precision=lax.Precision.HIGHEST)
    return features.reshape(DOCS_DEV, RANK * RANK)


def score_all(queries, doc_feat):
    return lax.dot_general(
        queries,
        lax.all_gather(doc_feat, "dp", axis=0, tiled=True),
        (((1,), (1,)), ((), ())),
        preferred_element_type=jnp.float32,
    )


def shards(activations, out_grads, proj_in, proj_out, doc_ids, queries, block_owner):
    part_in = jnp.dot(activations, proj_in, preferred_element_type=jnp.float32)
    part_out = jnp.dot(out_grads, proj_out, preferred_element_type=jnp.float32)
    labels_now = doc_ids[0]
    in_proj, out_proj = lax.psum((part_in, part_out), "tensor")
    doc_feat = doc_features(in_proj, out_proj, labels_now).astype(jnp.bfloat16)
    stored = score_all(queries, doc_feat)
    gathered = lax.all_gather(stored, "dp", axis=0, tiled=True)
    owner = block_owner[lax.axis_index("dp")]
    block_rows = stored.shape[0]
    return lax.dynamic_slice_in_dim(gathered, owner * block_rows, block_rows, 0)


def solution(mesh):
    placed = (
        P("dp", "tensor"),
        P("dp", "tensor"),
        P("tensor", None),
        P("tensor", None),
        P("dp", None),
        P(("dp", "tensor"), None),
        P(),
    )
    return jax.shard_map(
        shards, mesh=mesh, in_specs=placed, out_specs=P(("dp", "tensor"), None), check_vma=False
    )
```

profile of v0, /device:TPU:8, one launch (start us, length us, event | category | flops | bytes accessed | tf_op | source)
XLA Modules:
  0.0 336.2 jit_solution(2644003999269660165)
XLA Ops:
  6.5 0.0 copy-start
  6.5 0.0 copy-start.2
  6.5 0.0 copy-start.3
  6.5 0.0 copy-start.1
  6.5 0.0 all-reduce.3.cloned.1.call-start
  6.6 1.5 copy-done
  8.1 2.4 fusion.5
  10.5 6.1 %fusion.6 = f32[1024,64]{0,1:T(8,128)} fusion(bf16[1024,3584]{1,0:T(8,128)(2,1)} %param.7, bf16[3584,64]{0,1:T(8,128)(2,1)} %param.9), kind=kOutput, calls=%fused_computation.10 | convolution fusion | flops 469762048 | bytes 8060928 | tf_op jit(solution)/shard_map/dot_general | solution.py:28
  16.6 0.0 all-reduce.3.cloned.1.call-update
  16.7 0.0 all-gather.3.cloned.1.call-start
  16.7 0.0 copy-done.2
  16.7 77.1 %all-reduce.3.cloned.1.call-done = (f32[1024,64]{0,1:T(8,128)}, f32[1024,64]{0,1:T(8,128)}) async-done(((f32[1024,64]{0,1:T(8,128)}, f32[1024,64]{0,1:T(8,128)}), (f32[1024,64]{0,1:T(8,128)}, f32[1024,64]{0,1:T(8,128)})) %all-reduce.3.cloned.1.call-update) | async-done | bytes 524304 | tf_op jit(solution)/shard_map/psum | solution.py:31
  93.8 2.0 convolution_convert_fusion
  95.8 0.7 reshape.26
  96.5 0.0 all-gather.3.cloned.1.call-update
  96.6 0.0 copy-done.3
  96.6 0.6 dynamic_slice.6
  97.8 150.3 %all-gather.3.cloned.1.call-done = bf16[32,4,4096]{2,1,0:T(4,128)(2,1)} async-done(((bf16[1,4,4096]{2,1,0:T(4,128)(2,1)}), bf16[32,4,4096]{2,1,0:T(4,128)(2,1)}) %all-gather.3.cloned.1.call-update) | async-done | bytes 1048592 | tf_op jit(solution)/shard_map/all_gather | solution.py:21
  248.1 1.3 reshape.27
  249.4 0.0 copy-done.1
  249.5 0.4 convolution_bitcast_fusion
  249.9 78.9 %all_gather.7 = f32[1024,128]{1,0:T(8,128)S(1)} all-gather(f32[32,128]{1,0:T(8,128)S(1)} %convolution_bitcast_fusion), channel_id=1, replica_groups=mesh['dp'=32,'tensor'=8] {'dp'}, dimensions={0}, use_global_device_ids=true | all-gather | bytes 540672 | tf_op jit(solution)/shard_map/all_gather | solution.py:34
  328.8 0.6 constant_dynamic-slice_fusion
  (1 shorter events, 0.0 us)
Async XLA Ops:
  6.5 1.6 copy-start
  6.5 10.2 %copy-start.2 = (s32[1,1024]{1,0:T(1,128)S(1)}, s32[1,1024]{1,0:T(1,128)}, u32[]{:S(2)}) copy-start(s32[1,1024]{1,0:T(1,128)} %param.11) | copy-start | bytes 12292
  6.5 90.0 %copy-start.3 = (s32[32]{0:T(128)S(1)}, s32[32]{0:T(128)}, u32[]{:S(2)}) copy-start(s32[32]{0:T(128)} %param.13) | copy-start | bytes 388
  6.5 242.9 %copy-start.1 = (bf16[32,4096]{1,0:T(8,128)(2,1)S(1)}, bf16[32,4096]{1,0:T(8,128)(2,1)}, u32[]{:S(2)}) copy-start(bf16[32,4096]{1,0:T(8,128)(2,1)} %param.12) | copy-start | bytes 786436
  6.5 87.3 %all-reduce.3.cloned.1.call-start = ((), (), s32[]{:S(2)}) async-start(), calls=%async_computation.1 | async-start | bytes 1048576 | tf_op jit(solution)/shard_map/psum | solution.py:31
  16.7 231.4 %all-gather.3.cloned.1.call-start = ((), (), s32[]{:S(2)}) async-start(), calls=%async_computation | async-start | bytes 1081344 | tf_op jit(solution)/shard_map/all_gather | solution.py:21
Sparse Core Ops, SparseCore 0:
  16.8 76.9 all-reduce.2
  96.7 151.3 all-gather.2
where the time goes:
time: 341 us; the launch traced here: 336 us
  waiting for transfers between devices  227 us (67%)
  blocking collectives  78.9 us (23%)
  between operations  14.1 us (4%)
  matrix products  10.9 us (3%)
  local copies, waits for them, and re-layouts  4.81 us (1%)
    all_gather x1, waiting for transfers between devices, score_all(): lax.all_gather(doc_feat, 'dp', axis=0, tiled=True)  150 us
    all_gather x1, blocking collectives, shards(): gathered = lax.all_gather(stored, 'dp', axis=0, tiled=True)  78.9 us
    psum x1, waiting for transfers between devices, shards(): in_proj, out_proj = lax.psum((part_in, part_out), 'tensor')  77.1 us
  transfers between devices with their start and end apart: 2, of which 2 were waited for; matrix products, arithmetic and copies ran while one was open for 0% of the time, Pallas kernels for 0%

commit v1 on v0

v1 whole, which is shorter than its diff:
```python
import jax
import jax.numpy as jnp
from jax import lax
from jax.sharding import PartitionSpec as P

RANK = 64
DOCS_DEV = 4
N_DP = 32
HALF = RANK // 2


def swap(value, bits):
    return lax.ppermute(value, "tensor", [(i, i ^ bits) for i in range(8)])


def pick(first, low, high):
    return jnp.where(first, low, high), jnp.where(first, high, low)


def shards(activations, out_grads, proj_in, proj_out, doc_ids, queries, block_owner):
    me = lax.axis_index("tensor")
    core0, chip = (me & 1) == 0, me >> 1
    row0, col0 = (chip >> 1) == 0, (chip & 1) == 0

    cut = queries.reshape(32, 2, 2, 16, 2, HALF)
    mine, other = pick(core0, cut[:, :, 0], cut[:, :, 1])
    got = swap(other, 1)
    rows0 = jnp.where(core0, mine, got)
    rows1 = jnp.where(core0, got, mine)
    q = jnp.stack([rows0, rows1]).reshape(64, 2, 16, 2, HALF).transpose(0, 1, 3, 2, 4).reshape(64, 2048)

    part_out = jnp.dot(out_grads, proj_out, preferred_element_type=jnp.float32).T
    part_in = jnp.dot(activations, proj_in, preferred_element_type=jnp.float32).T
    part = jnp.concatenate([part_out.reshape(2, HALF, -1), part_in.reshape(2, HALF, -1)])
    half = part.shape[-1] // 2
    keep, send = pick(core0, part[..., :half], part[..., half:])
    total = keep + swap(send, 1)
    out_keep, out_other = pick(row0, total[0], total[1])
    in_keep, in_other = pick(col0, total[2], total[3])
    far = swap(jnp.stack([out_other, in_keep]), 4)
    near = swap(jnp.stack([out_keep, in_other]), 2)
    last = swap(jnp.stack([out_other, in_other]), 6)
    out_proj, in_proj = (jnp.stack([out_keep, in_keep]) + near) + (far + last)

    ids = doc_ids[0]
    labels_now = jnp.where(core0, ids[:half], ids[half:])
    labels = jnp.arange(DOCS_DEV, dtype=jnp.int32)
    onehot = (labels_now[None, :] == labels[:, None]).astype(jnp.float32)
    weighted = onehot[:, None, :] * out_proj[None]
    feat = jnp.einsum("dit,jt->dij", weighted, in_proj, precision=lax.Precision.HIGHEST)
    keep, send = pick(core0, feat[:, :16], feat[:, 16:])
    block = (keep + swap(send, 1)).astype(jnp.bfloat16).reshape(DOCS_DEV, 512)

    groups = [[p * 8 + 2 * b + c for p in range(N_DP) for b in range(4)] for c in range(2)]
    everyone = jnp.broadcast_to(block, (4 * N_DP, DOCS_DEV, 512))
    feats = lax.all_to_all(everyone, ("dp", "tensor"), 0, 0, axis_index_groups=groups)
    feats = feats.reshape(N_DP, 4, DOCS_DEV, 512).transpose(0, 2, 1, 3).reshape(N_DP * DOCS_DEV, 2048)
    scored = lax.dot_general(q, feats, (((1,), (1,)), ((), ())), preferred_element_type=jnp.float32)
    keep, send = pick(core0, scored[:32], scored[32:])
    stored = (keep + swap(send, 1)).astype(jnp.bfloat16)

    blocks = lax.all_to_all(jnp.broadcast_to(stored, (N_DP,) + stored.shape), "dp", 0, 0)
    owner = block_owner[lax.axis_index("dp")]
    return lax.dynamic_index_in_dim(blocks, owner, 0, keepdims=False).astype(jnp.float32)


def solution(mesh):
    placed = (
        P("dp", "tensor"),
        P("dp", "tensor"),
        P("tensor", None),
        P("tensor", None),
        P("dp", None),
        P(("dp", "tensor"), None),
        P(),
    )
    return jax.shard_map(
        shards, mesh=mesh, in_specs=placed, out_specs=P(("dp", "tensor"), None), check_vma=False
    )
```

time: 341 us -> 84.5 us (0.25); the launches traced: 336 us -> 84 us
  waiting for transfers between devices: 227 us -> 34.4 us
  blocking collectives: 78.9 us -> 0 us
  starting transfers between devices: 0.08 us -> 28.3 us
  between operations: 14.1 us -> 2.2 us
  other arithmetic: 0.01 us -> 4.13 us
    all_gather x1 -> x0, waiting for transfers between devices: 150 us -> none  [score_all(): lax.all_gather(doc_feat, 'dp', axis=0, tiled=True)]
    all_gather x1 -> x0, blocking collectives: 78.9 us -> none  [shards(): gathered = lax.all_gather(stored, 'dp', axis=0, tiled=True)]
    psum x1 -> x0, waiting for transfers between devices: 77.1 us -> none  [shards(): in_proj, out_proj = lax.psum((part_in, part_out), 'tensor')]
    all_to_all x0 -> x2, starting transfers between devices: none -> 19 us  [the longest x1 13.6 us: shards(): lax.all_to_all(everyone, ('dp', 'tensor'), 0, 0, axis_index_groups=groups)]
    ppermute x0 -> x7, waiting for transfers between devices: none -> 17.3 us  [swap(): return lax.ppermute(value, 'tensor', [(i, i ^ bits) for i in range(8)])]
    all_to_all x0 -> x2, waiting for transfers between devices: none -> 17.1 us  [the longest x1 11 us: shards(): lax.all_to_all(everyone, ('dp', 'tensor'), 0, 0, axis_index_groups=groups)]
    ppermute x0 -> x7, starting transfers between devices: none -> 9.3 us  [swap(): return lax.ppermute(value, 'tensor', [(i, i ^ bits) for i in range(8)])]
    unnamed x10 -> x11, local copies, waits for them, and re-layouts: 3.62 us -> 0.12 us
  transfers between devices with their start and end apart: 2 -> 9, of which waited for: 2 -> 9; matrix products, arithmetic and copies ran while one was open for 0% -> 8% of each run, Pallas kernels for 0% -> 0%
where the time goes in v1:
time: 84.5 us; the launch traced here: 84 us
  waiting for transfers between devices  34.4 us (41%)
  starting transfers between devices  28.3 us (33%)
  matrix products  8.13 us (10%)
  local copies, waits for them, and re-layouts  6.79 us (8%)
  other arithmetic  4.13 us (5%)
  between operations  2.2 us (3%)
    ppermute x7, waiting for transfers between devices, swap(): return lax.ppermute(value, 'tensor', [(i, i ^ bits) for i in range(8)])  17.3 us
    all_to_all x1, starting transfers between devices, shards(): lax.all_to_all(everyone, ('dp', 'tensor'), 0, 0, axis_index_groups=groups)  13.6 us
    all_to_all x1, waiting for transfers between devices, shards(): lax.all_to_all(everyone, ('dp', 'tensor'), 0, 0, axis_index_groups=groups)  11 us
    ppermute x7, starting transfers between devices, swap(): return lax.ppermute(value, 'tensor', [(i, i ^ bits) for i in range(8)])  9.3 us
    all_to_all x1, waiting for transfers between devices, shards(): lax.all_to_all(jnp.broadcast_to(stored, (N_DP,) + stored.shape), 'dp', 0, 0)  6.11 us
    dot_general x1, matrix products, shards(): jnp.dot(activations, proj_in, preferred_element_type=jnp.float32)  5.67 us
    all_to_all x1, starting transfers between devices, shards(): lax.all_to_all(jnp.broadcast_to(stored, (N_DP,) + stored.shape), 'dp', 0, 0)  5.39 us
    another operation x2, other arithmetic, shards(): jnp.stack([rows0, rows1]).reshape(64, 2, 16, 2, HALF)  2.75 us
  transfers between devices with their start and end apart: 9, of which 9 were waited for; matrix products, arithmetic and copies ran while one was open for 8% of the time, Pallas kernels for 0%

profile of v1, /device:TPU:8, one launch (start us, length us, event | category | flops | bytes accessed | tf_op | source)
XLA Modules:
  0.0 84.0 jit_solution(17929132129733679781)
XLA Ops:
  0.0 0.0 copy-start
  0.0 0.0 copy-start.2
  0.0 0.0 copy-start.3
  0.0 0.0 copy-start.1
  0.0 5.7 %fusion.13 = f32[64,1024]{1,0:T(8,128)S(1)} fusion(bf16[3584,64]{0,1:T(8,128)(2,1)} %param.9, bf16[1024,3584]{1,0:T(8,128)(2,1)} %param.7), kind=kOutput, calls=%fused_computation.40 | convolution fusion | flops 469762048 | bytes 8060928 | tf_op jit(solution)/shard_map/dot_general | solution.py:33
  5.7 0.0 copy-done
  5.7 0.0 copy-done.2
  5.7 0.8 fusion.12
  6.5 0.1 collective-permute-start.1
  6.6 0.0 copy-done.3
  6.7 1.5 %collective-permute-done.1 = f32[4,32,512]{2,1,0:T(8,128)S(1)} collective-permute-done((f32[4,32,512]{2,1,0:T(8,128)S(1)}, f32[4,32,512]{2,1,0:T(8,128)S(1)}, u32[]{:S(2)}, u32[]{:S(2)}) %collective-permute-start.1) | collective-permute-done | bytes 262176 | tf_op jit(solution)/shard_map/ppermute | solution.py:13
  8.2 0.1 select_add_fusion
  8.3 3.4 %collective-permute-start.2 = (f32[2,32,512]{2,1,0:T(8,128)S(1)}, f32[2,32,512]{2,1,0:T(8,128)S(1)}, u32[]{:S(2)}, u32[]{:S(2)}) collective-permute-start(f32[2,32,512]{2,1,0:T(8,128)S(1)} %get-tuple-element.13), channel_id=1, source_target_pairs={{0,2},{1,3},{2,0},{3,1},{4,6},{5,7},{6,4},{7,5},{8,10},{9,11},{10,... | collective-permute-start | bytes 393224 | tf_op jit(solution)/shard_map/ppermute | solution.py:13
  11.6 5.4 %collective-permute-start.3 = (f32[2,32,512]{2,1,0:T(8,128)S(1)}, f32[2,32,512]{2,1,0:T(8,128)S(1)}, u32[]{:S(2)}, u32[]{:S(2)}) collective-permute-start(f32[2,32,512]{2,1,0:T(8,128)S(1)} %get-tuple-element.12), channel_id=1, source_target_pairs={{0,4},{1,5},{2,6},{3,7},{4,0},{5,1},{6,2},{7,3},{8,12},{9,13},{10,... | collective-permute-start | bytes 393224 | tf_op jit(solution)/shard_map/ppermute | solution.py:13
  17.0 0.0 collective-permute-start.4
  17.0 1.2 %collective-permute-done.2 = f32[2,32,512]{2,1,0:T(8,128)S(1)} collective-permute-done((f32[2,32,512]{2,1,0:T(8,128)S(1)}, f32[2,32,512]{2,1,0:T(8,128)S(1)}, u32[]{:S(2)}, u32[]{:S(2)}) %collective-permute-start.2) | collective-permute-done | bytes 131104 | tf_op jit(solution)/shard_map/ppermute | solution.py:13
  18.3 8.5 %collective-permute-done.3 = f32[2,32,512]{2,1,0:T(8,128)S(1)} collective-permute-done((f32[2,32,512]{2,1,0:T(8,128)S(1)}, f32[2,32,512]{2,1,0:T(8,128)S(1)}, u32[]{:S(2)}, u32[]{:S(2)}) %collective-permute-start.3) | collective-permute-done | bytes 131104 | tf_op jit(solution)/shard_map/ppermute | solution.py:13
  26.8 1.8 %collective-permute-done.4 = f32[2,32,512]{2,1,0:T(8,128)S(1)} collective-permute-done((f32[2,32,512]{2,1,0:T(8,128)S(1)}, f32[2,32,512]{2,1,0:T(8,128)S(1)}, u32[]{:S(2)}, u32[]{:S(2)}) %collective-permute-start.4) | collective-permute-done | bytes 131104 | tf_op jit(solution)/shard_map/ppermute | solution.py:13
  28.6 0.4 fusion.5
  29.0 0.1 collective-permute-start.5
  29.1 1.2 %collective-permute-done.5 = f32[4,16,32]{2,1,0:T(8,128)S(1)} collective-permute-done((f32[4,16,32]{2,1,0:T(8,128)S(1)}, f32[4,16,32]{2,1,0:T(8,128)S(1)}, u32[]{:S(2)}, u32[]{:S(2)}) %collective-permute-start.5) | collective-permute-done | bytes 8224 | tf_op jit(solution)/shard_map/ppermute | solution.py:13
  30.3 0.1 reshape.56
  30.4 0.0 copy-start.4
  30.4 1.0 %broadcast_in_dim.4 = bf16[128,4,512]{2,1,0:T(4,128)(2,1)} broadcast(bf16[4,512]{1,0:T(4,128)(2,1)S(1)} %reshape.56), dimensions={1,2} | broadcast | bytes 528384 | tf_op jit(solution)/shard_map/broadcast_in_dim | solution.py:55
  31.4 13.6 %all-to-all-start = ((bf16[128,4,512]{2,1,0:T(4,128)(2,1)}), bf16[128,4,512]{2,1,0:T(4,128)(2,1)}, u32[]{:S(2)}, u32[]{:S(2)}) async-start(bf16[128,4,512]{2,1,0:T(4,128)(2,1)} %broadcast_in_dim.4), calls=%async_computation | async-start | bytes 1048576 | tf_op jit(solution)/shard_map/all_to_all | solution.py:56
  45.0 0.0 copy-done.1
  45.0 0.8 reshape.51
  45.8 0.5 fusion.3
  46.3 0.3 collective-permute-start
  46.6 1.9 %collective-permute-done = bf16[32,2,16,2,32]{4,3,2,1,0:T(2,128)(2,1)S(1)} collective-permute-done((bf16[32,2,16,2,32]{4,3,2,1,0:T(2,128)(2,1)S(1)}, bf16[32,2,16,2,32]{4,3,2,1,0:T(2,128)(2,1)S(1)}, u32[]{:S(2)}, u32[]{:S(2)}) %collective-permute-start) | collective-permute-done | bytes 131104 | tf_op jit(solution)/shard_map/ppermute | solution.py:13
  48.5 1.0 %fusion = (bf16[1,32,2,16,2,32]{5,4,3,2,1,0:T(2,128)(2,1)S(1)}, bf16[1,32,2,16,2,32]{5,4,3,2,1,0:T(2,128)(2,1)S(1)}) fusion(bf16[32,2,16,2,32]{4,3,2,1,0:T(2,128)(2,1)S(1)} %collective-permute-done, pred[]{:T(512)S(6)} %eq.28, bf16[32,2,2,16,2,32]{5,4,3,2,1,0:T(2,128)(2,1)S(1)} %reshape.51), kind=kLoop, calls=%fused_computation.5 | loop fusion | flops 196608 | bytes 656384 | tf_op jit(solution)/shard_map/stack | solution.py:30
  49.5 1.8 %pad_maximum_fusion = bf16[2,32,2,16,2,32]{5,4,3,2,1,0:T(2,128)(2,1)S(1)} fusion(bf16[1,32,2,16,2,32]{5,4,3,2,1,0:T(2,128)(2,1)S(1)} %get-tuple-element.6, bf16[1,32,2,16,2,32]{5,4,3,2,1,0:T(2,128)(2,1)S(1)} %get-tuple-element.5), kind=kLoop, calls=%fused_computation.1 | loop fusion | flops 131072 | bytes 524288 | tf_op jit(solution)/shard_map/stack | solution.py:30
  51.3 2.2 %copy.23 = bf16[64,2,16,2,32]{0,4,2,3,1:T(8,128)(2,1)} copy(bf16[64,2,16,2,32]{4,3,2,1,0:T(2,128)(2,1)S(1)} %bitcast.59) | data formatting | bytes 524288 | tf_op jit(solution)/shard_map/reshape | solution.py:30
  53.5 11.0 %all-to-all-done = bf16[128,4,512]{2,1,0:T(4,128)(2,1)} async-done(((bf16[128,4,512]{2,1,0:T(4,128)(2,1)}), bf16[128,4,512]{2,1,0:T(4,128)(2,1)}, u32[]{:S(2)}, u32[]{:S(2)}) %all-to-all-start) | async-done | bytes 524320 | tf_op jit(solution)/shard_map/all_to_all | solution.py:56
  64.5 1.3 %copy.22 = bf16[32,4,4,512]{3,2,1,0:T(4,128)(2,1)S(1)} copy(bf16[32,4,4,512]{3,1,2,0:T(4,128)(2,1)} %bitcast.17) | data formatting | bytes 1048576 | tf_op jit(solution)/shard_map/transpose | solution.py:57
  65.8 0.1 copy.25
  65.9 1.3 %fusion.14 = f32[64,128]{1,0:T(8,128)S(1)} fusion(bf16[64,2048]{0,1:T(8,128)(2,1)} %bitcast.64, bf16[128,2048]{1,0:T(8,128)(2,1)S(1)} %bitcast.65), kind=kOutput, calls=%fused_computation.41 | convolution fusion | flops 33554432 | bytes 819200 | tf_op jit(solution)/shard_map/dot_general | solution.py:58
  67.3 0.1 collective-permute-start.6
  67.4 1.2 %collective-permute-done.6 = f32[32,128]{1,0:T(8,128)S(1)} collective-permute-done((f32[32,128]{1,0:T(8,128)S(1)}, f32[32,128]{1,0:T(8,128)S(1)}, u32[]{:S(2)}, u32[]{:S(2)}) %collective-permute-start.6) | collective-permute-done | bytes 16416 | tf_op jit(solution)/shard_map/ppermute | solution.py:13
  68.5 0.7 broadcast_in_dim.10
  69.3 5.4 %all-to-all-start.1 = ((bf16[32,32,128]{2,1,0:T(8,128)(2,1)}), bf16[32,32,128]{2,1,0:T(8,128)(2,1)S(1)}, u32[]{:S(2)}, u32[]{:S(2)}) async-start(bf16[32,32,128]{2,1,0:T(8,128)(2,1)} %broadcast_in_dim.10), calls=%async_computation.1 | async-start | bytes 524288 | tf_op jit(solution)/shard_map/all_to_all | solution.py:62
  74.7 0.0 copy-done.4
  74.7 0.6 dynamic_slice.7
  77.2 6.1 %all-to-all-done.1 = bf16[32,32,128]{2,1,0:T(8,128)(2,1)S(1)} async-done(((bf16[32,32,128]{2,1,0:T(8,128)(2,1)}), bf16[32,32,128]{2,1,0:T(8,128)(2,1)S(1)}, u32[]{:S(2)}, u32[]{:S(2)}) %all-to-all-start.1) | async-done | bytes 262176 | tf_op jit(solution)/shard_map/all_to_all | solution.py:62
  83.3 0.6 bitcast_convert_fusion
  (11 shorter events, 0.2 us)
Async XLA Ops:
  0.0 5.7 %copy-start = (bf16[1024,1024]{1,0:T(8,128)(2,1)S(1)}, bf16[1024,1024]{1,0:T(8,128)(2,1)}, u32[]{:S(2)}) copy-start(bf16[1024,1024]{1,0:T(8,128)(2,1)} %param.8) | copy-start | bytes 6291460
  0.0 5.7 %copy-start.2 = (bf16[1024,64]{0,1:T(8,128)(2,1)S(1)}, bf16[1024,64]{0,1:T(8,128)(2,1)}, u32[]{:S(2)}) copy-start(bf16[1024,64]{0,1:T(8,128)(2,1)} %param.10) | copy-start | bytes 393220
  0.0 6.6 %copy-start.3 = (s32[1,1024]{1,0:T(1,128)S(1)}, s32[1,1024]{1,0:T(1,128)}, u32[]{:S(2)}) copy-start(s32[1,1024]{1,0:T(1,128)} %param.11) | copy-start | bytes 12292
  0.0 45.0 %copy-start.1 = (bf16[32,4096]{1,0:T(8,128)(2,1)S(1)}, bf16[32,4096]{1,0:T(8,128)(2,1)}, u32[]{:S(2)}) copy-start(bf16[32,4096]{1,0:T(8,128)(2,1)} %param.12) | copy-start | bytes 786436
  6.5 1.6 %collective-permute-start.1 = (f32[4,32,512]{2,1,0:T(8,128)S(1)}, f32[4,32,512]{2,1,0:T(8,128)S(1)}, u32[]{:S(2)}, u32[]{:S(2)}) collective-permute-start(f32[4,32,512]{2,1,0:T(8,128)S(1)} %broadcast_select_fusion.3), channel_id=1, source_target_pairs={{0,1},{1,0},{2,3},{3,2},{4,5},{5,4},{6,7},{7,6},{8,9},{9,8},{10,11... | collective-permute-start | bytes 786440 | tf_op jit(solution)/shard_map/ppermute | solution.py:13
  8.3 10.0 %collective-permute-start.2 = (f32[2,32,512]{2,1,0:T(8,128)S(1)}, f32[2,32,512]{2,1,0:T(8,128)S(1)}, u32[]{:S(2)}, u32[]{:S(2)}) collective-permute-start(f32[2,32,512]{2,1,0:T(8,128)S(1)} %get-tuple-element.13), channel_id=1, source_target_pairs={{0,2},{1,3},{2,0},{3,1},{4,6},{5,7},{6,4},{7,5},{8,10},{9,11},{10,... | collective-permute-start | bytes 393224 | tf_op jit(solution)/shard_map/ppermute | solution.py:13
  11.6 15.1 %collective-permute-start.3 = (f32[2,32,512]{2,1,0:T(8,128)S(1)}, f32[2,32,512]{2,1,0:T(8,128)S(1)}, u32[]{:S(2)}, u32[]{:S(2)}) collective-permute-start(f32[2,32,512]{2,1,0:T(8,128)S(1)} %get-tuple-element.12), channel_id=1, source_target_pairs={{0,4},{1,5},{2,6},{3,7},{4,0},{5,1},{6,2},{7,3},{8,12},{9,13},{10,... | collective-permute-start | bytes 393224 | tf_op jit(solution)/shard_map/ppermute | solution.py:13
  17.0 11.5 %collective-permute-start.4 = (f32[2,32,512]{2,1,0:T(8,128)S(1)}, f32[2,32,512]{2,1,0:T(8,128)S(1)}, u32[]{:S(2)}, u32[]{:S(2)}) collective-permute-start(f32[2,32,512]{2,1,0:T(8,128)S(1)} %get-tuple-element.11), channel_id=1, source_target_pairs={{0,6},{1,7},{2,4},{3,5},{4,2},{5,3},{6,0},{7,1},{8,14},{9,15},{10,... | collective-permute-start | bytes 393224 | tf_op jit(solution)/shard_map/ppermute | solution.py:13
  29.0 1.3 %collective-permute-start.5 = (f32[4,16,32]{2,1,0:T(8,128)S(1)}, f32[4,16,32]{2,1,0:T(8,128)S(1)}, u32[]{:S(2)}, u32[]{:S(2)}) collective-permute-start(f32[4,16,32]{2,1,0:T(8,128)S(1)} %slice_select_fusion.4), channel_id=1, source_target_pairs={{0,1},{1,0},{2,3},{3,2},{4,5},{5,4},{6,7},{7,6},{8,9},{9,8},{10,11... | collective-permute-start | bytes 24584 | tf_op jit(solution)/shard_map/ppermute | solution.py:13
  30.4 44.3 %copy-start.4 = (s32[32]{0:T(128)S(1)}, s32[32]{0:T(128)}, u32[]{:S(2)}) copy-start(s32[32]{0:T(128)} %param.13) | copy-start | bytes 388
  31.4 33.1 %all-to-all-start = ((bf16[128,4,512]{2,1,0:T(4,128)(2,1)}), bf16[128,4,512]{2,1,0:T(4,128)(2,1)}, u32[]{:S(2)}, u32[]{:S(2)}) async-start(bf16[128,4,512]{2,1,0:T(4,128)(2,1)} %broadcast_in_dim.4), calls=%async_computation | async-start | bytes 1048576 | tf_op jit(solution)/shard_map/all_to_all | solution.py:56
  46.3 2.2 %collective-permute-start = (bf16[32,2,16,2,32]{4,3,2,1,0:T(2,128)(2,1)S(1)}, bf16[32,2,16,2,32]{4,3,2,1,0:T(2,128)(2,1)S(1)}, u32[]{:S(2)}, u32[]{:S(2)}) collective-permute-start(bf16[32,2,16,2,32]{4,3,2,1,0:T(2,128)(2,1)S(1)} %fusion.3), channel_id=1, source_target_pairs={{0,1},{1,0},{2,3},{3,2},{4,5},{5,4},{6,7},{7,6},{8,9},{9,8},{10,11... | collective-permute-start | bytes 393224 | tf_op jit(solution)/shard_map/ppermute | solution.py:13
  67.3 1.3 %collective-permute-start.6 = (f32[32,128]{1,0:T(8,128)S(1)}, f32[32,128]{1,0:T(8,128)S(1)}, u32[]{:S(2)}, u32[]{:S(2)}) collective-permute-start(f32[32,128]{1,0:T(8,128)S(1)} %slice_select_fusion.5), channel_id=1, source_target_pairs={{0,1},{1,0},{2,3},{3,2},{4,5},{5,4},{6,7},{7,6},{8,9},{9,8},{10,11... | collective-permute-start | bytes 49160 | tf_op jit(solution)/shard_map/ppermute | solution.py:13
  69.3 14.1 %all-to-all-start.1 = ((bf16[32,32,128]{2,1,0:T(8,128)(2,1)}), bf16[32,32,128]{2,1,0:T(8,128)(2,1)S(1)}, u32[]{:S(2)}, u32[]{:S(2)}) async-start(bf16[32,32,128]{2,1,0:T(8,128)(2,1)} %broadcast_in_dim.10), calls=%async_computation.1 | async-start | bytes 524288 | tf_op jit(solution)/shard_map/all_to_all | solution.py:62

commit v2 on v1

--- a/solution.py
+++ b/solution.py
@@ -22,24 +22,20 @@
     core0, chip = (me & 1) == 0, me >> 1
     row0, col0 = (chip >> 1) == 0, (chip & 1) == 0
 
-    cut = queries.reshape(32, 2, 2, 16, 2, HALF)
-    mine, other = pick(core0, cut[:, :, 0], cut[:, :, 1])
-    got = swap(other, 1)
-    rows0 = jnp.where(core0, mine, got)
-    rows1 = jnp.where(core0, got, mine)
-    q = jnp.stack([rows0, rows1]).reshape(64, 2, 16, 2, HALF).transpose(0, 1, 3, 2, 4).reshape(64, 2048)
-
     part_out = jnp.dot(out_grads, proj_out, preferred_element_type=jnp.float32).T
     part_in = jnp.dot(activations, proj_in, preferred_element_type=jnp.float32).T
     part = jnp.concatenate([part_out.reshape(2, HALF, -1), part_in.reshape(2, HALF, -1)])
     half = part.shape[-1] // 2
     keep, send = pick(core0, part[..., :half], part[..., half:])
     total = keep + swap(send, 1)
+    queries, total = lax.optimization_barrier((queries, total))
+    cut = queries.reshape(32, 2, 2, 16, 2, HALF).transpose(1, 4, 2, 0, 3, 5).reshape(8, 32, 512)
     out_keep, out_other = pick(row0, total[0], total[1])
     in_keep, in_other = pick(col0, total[2], total[3])
     far = swap(jnp.stack([out_other, in_keep]), 4)
     near = swap(jnp.stack([out_keep, in_other]), 2)
     last = swap(jnp.stack([out_other, in_other]), 6)
+    near, far, last, cut = lax.optimization_barrier((near, far, last, cut))
     out_proj, in_proj = (jnp.stack([out_keep, in_keep]) + near) + (far + last)
 
     ids = doc_ids[0]
@@ -51,13 +47,13 @@
     keep, send = pick(core0, feat[:, :16], feat[:, 16:])
     block = (keep + swap(send, 1)).astype(jnp.bfloat16).reshape(DOCS_DEV, 512)
 
-    groups = [[p * 8 + 2 * b + c for p in range(N_DP) for b in range(4)] for c in range(2)]
-    everyone = jnp.broadcast_to(block, (4 * N_DP, DOCS_DEV, 512))
-    feats = lax.all_to_all(everyone, ("dp", "tensor"), 0, 0, axis_index_groups=groups)
-    feats = feats.reshape(N_DP, 4, DOCS_DEV, 512).transpose(0, 2, 1, 3).reshape(N_DP * DOCS_DEV, 2048)
+    block, cut = lax.optimization_barrier((block, cut))
+    feats = lax.all_to_all(jnp.broadcast_to(block, (N_DP, DOCS_DEV, 512)), "dp", 0, 0)
+    feats = feats.reshape(N_DP * DOCS_DEV, 512)
+    q = lax.all_to_all(cut, "tensor", 0, 0).reshape(256, 512)
     scored = lax.dot_general(q, feats, (((1,), (1,)), ((), ())), preferred_element_type=jnp.float32)
-    keep, send = pick(core0, scored[:32], scored[32:])
-    stored = (keep + swap(send, 1)).astype(jnp.bfloat16)
+    parts = lax.all_to_all(scored.reshape(8, 32, N_DP * DOCS_DEV), "tensor", 0, 0)
+    stored = jnp.sum(parts, axis=0).astype(jnp.bfloat16)
 
     blocks = lax.all_to_all(jnp.broadcast_to(stored, (N_DP,) + stored.shape), "dp", 0, 0)
     owner = block_owner[lax.axis_index("dp")]

time: 84.5 us -> 96.2 us (1.14)
  blocking collectives: 0 us -> 28.3 us
  starting transfers between devices: 28.3 us -> 19.9 us
  waiting for transfers between devices: 34.4 us -> 27.1 us
  other arithmetic: 4.13 us -> 2.53 us
  local copies, waits for them, and re-layouts: 6.79 us -> 7.93 us
    all_to_all x0 -> x2, blocking collectives: none -> 28.3 us  [the longest x1 16.2 us: shards(): lax.all_to_all(jnp.broadcast_to(block, (N_DP, DOCS_DEV, 512)), 'dp', 0, 0)]
    ppermute x7 -> x5, waiting for transfers between devices: 17.3 us -> 9.46 us  [swap(): return lax.ppermute(value, 'tensor', [(i, i ^ bits) for i in range(8)])]
    all_to_all x1, starting transfers between devices: 13.6 us -> 5.94 us  [shards(): q = lax.all_to_all(cut, 'tensor', 0, 0).reshape(256, 512)]
    another operation x2 -> x0, other arithmetic: 2.75 us -> none  [shards(): jnp.stack([rows0, rows1]).reshape(64, 2, 16, 2, HALF)]
    reshape x2 -> x4, local copies, waits for them, and re-layouts: 2.99 us -> 4.88 us  [the longest x3 4.84 us: shards(): queries.reshape(32, 2, 2, 16, 2, HALF).transpose(1, 4, 2, 0, 3, 5)]
    unnamed x11 -> x8, local copies, waits for them, and re-layouts: 0.12 us -> 1.59 us
    transpose x1 -> x0, local copies, waits for them, and re-layouts: 1.29 us -> none  [shards(): feats.reshape(N_DP, 4, DOCS_DEV, 512).transpose(0, 2, 1, 3)]
    dot_general x1, matrix products: 1.35 us -> 0.22 us  [shards(): lax.dot_general(q, feats, (((1,), (1,)), ((), ())), preferred_element_typ...]
  transfers between devices with their start and end apart: 9 -> 7, of which waited for: 9 -> 6; matrix products, arithmetic and copies ran while one was open for 8% -> 6% of each run, Pallas kernels for 0% -> 0%
where the time goes in v2:
time: 96.2 us; the launch traced here: 95.7 us
  blocking collectives  28.3 us (29%)
  waiting for transfers between devices  27.1 us (28%)
  starting transfers between devices  19.9 us (21%)
  local copies, waits for them, and re-layouts  7.93 us (8%)
  matrix products  7.79 us (8%)
  other arithmetic  2.53 us (3%)
  between operations  2.11 us (2%)
    all_to_all x1, blocking collectives, shards(): lax.all_to_all(jnp.broadcast_to(block, (N_DP, DOCS_DEV, 512)), 'dp', 0, 0)  16.2 us
    all_to_all x1, blocking collectives, shards(): lax.all_to_all(scored.reshape(8, 32, N_DP * DOCS_DEV), 'tensor', 0, 0)  12.2 us
    all_to_all x1, waiting for transfers between devices, shards(): q = lax.all_to_all(cut, 'tensor', 0, 0).reshape(256, 512)  12 us
    ppermute x5, waiting for transfers between devices, swap(): return lax.ppermute(value, 'tensor', [(i, i ^ bits) for i in range(8)])  9.46 us
    ppermute x5, starting transfers between devices, swap(): return lax.ppermute(value, 'tensor', [(i, i ^ bits) for i in range(8)])  8.85 us
    all_to_all x1, starting transfers between devices, shards(): q = lax.all_to_all(cut, 'tensor', 0, 0).reshape(256, 512)  5.94 us
    all_to_all x1, waiting for transfers between devices, shards(): lax.all_to_all(jnp.broadcast_to(stored, (N_DP,) + stored.shape), 'dp', 0, 0)  5.7 us
    dot_general x1, matrix products, shards(): jnp.dot(activations, proj_in, preferred_element_type=jnp.float32)  5.56 us
  transfers between devices with their start and end apart: 7, of which 6 were waited for; matrix products, arithmetic and copies ran while one was open for 6% of the time, Pallas kernels for 0%

profile of v2, /device:TPU:8, one launch (start us, length us, event | category | flops | bytes accessed | tf_op | source)
XLA Modules:
  0.0 95.7 jit_solution(1197378080231912524)
XLA Ops:
  0.0 0.0 copy-start
  0.0 0.0 copy-start.2
  0.0 0.0 copy-start.1
  0.0 1.6 %copy-done = bf16[1024,1024]{1,0:T(8,128)(2,1)S(1)} copy-done((bf16[1024,1024]{1,0:T(8,128)(2,1)S(1)}, bf16[1024,1024]{1,0:T(8,128)(2,1)}, u32[]{:S(2)}) %copy-start) | copy-done | bytes 2097176
  1.6 1.7 %fusion.8 = f32[64,1024]{1,0:T(8,128)S(1)} fusion(bf16[1024,64]{0,1:T(8,128)(2,1)} %param.10, bf16[1024,1024]{1,0:T(8,128)(2,1)S(1)} %copy-done), kind=kOutput, calls=%fused_computation.29 | convolution fusion | flops 134217728 | bytes 2490368 | tf_op jit(solution)/shard_map/dot_general | solution.py:25
  3.3 5.6 %fusion.9 = f32[64,1024]{1,0:T(8,128)S(1)} fusion(bf16[3584,64]{0,1:T(8,128)(2,1)} %param.9, bf16[1024,3584]{1,0:T(8,128)(2,1)} %param.7), kind=kOutput, calls=%fused_computation.30 | convolution fusion | flops 469762048 | bytes 8060928 | tf_op jit(solution)/shard_map/dot_general | solution.py:26
  8.8 0.0 copy-start.3
  8.9 0.1 collective-permute-start
  9.0 0.0 copy-done.2
  9.0 1.5 %collective-permute-done = f32[4,32,512]{2,1,0:T(8,128)S(1)} collective-permute-done((f32[4,32,512]{2,1,0:T(8,128)S(1)}, f32[4,32,512]{2,1,0:T(8,128)S(1)}, u32[]{:S(2)}, u32[]{:S(2)}) %collective-permute-start) | collective-permute-done | bytes 262176 | tf_op jit(solution)/shard_map/ppermute | solution.py:13
  10.5 0.1 select_add_fusion
  10.6 0.8 pad_maximum_fusion.4
  11.3 3.3 %collective-permute-start.1 = (f32[2,32,512]{2,1,0:T(8,128)}, f32[2,32,512]{2,1,0:T(8,128)S(1)}, u32[]{:S(2)}, u32[]{:S(2)}) collective-permute-start(f32[2,32,512]{2,1,0:T(8,128)} %get-tuple-element.27), channel_id=1, source_target_pairs={{0,2},{1,3},{2,0},{3,1},{4,6},{5,7},{6,4},{7,5},{8,10},{9,11},{10,... | collective-permute-start | bytes 393224 | tf_op jit(solution)/shard_map/ppermute | solution.py:13
  14.6 5.4 %collective-permute-start.2 = (f32[2,32,512]{2,1,0:T(8,128)}, f32[2,32,512]{2,1,0:T(8,128)}, u32[]{:S(2)}, u32[]{:S(2)}) collective-permute-start(f32[2,32,512]{2,1,0:T(8,128)} %get-tuple-element.26), channel_id=1, source_target_pairs={{0,4},{1,5},{2,6},{3,7},{4,0},{5,1},{6,2},{7,3},{8,12},{9,13},{10,... | collective-permute-start | bytes 393224 | tf_op jit(solution)/shard_map/ppermute | solution.py:13
  20.0 0.0 collective-permute-start.3
  20.0 0.0 copy-done.1
  20.0 1.8 %reshape.47 = bf16[32,2,2,16,2,32]{5,4,3,2,1,0:T(2,128)(2,1)} reshape(bf16[32,4096]{1,0:T(8,128)(2,1)S(1)} %copy-done.1) | data formatting | bytes 524288 | tf_op jit(solution)/shard_map/reshape | solution.py:32
  21.8 1.4 %copy.10 = bf16[32,2,2,16,2,32]{5,3,0,2,4,1:T(8,128)(2,1)S(1)} copy(bf16[32,2,2,16,2,32]{5,4,3,2,1,0:T(2,128)(2,1)} %reshape.47) | data formatting | bytes 524288 | tf_op jit(solution)/shard_map/reshape | solution.py:32
  23.2 1.7 %reshape.48 = bf16[8,32,512]{2,1,0:T(8,128)(2,1)} reshape(bf16[2,2,2,32,16,32]{5,4,3,2,1,0:T(8,128)(2,1)S(1)} %bitcast.24) | data formatting | bytes 524288 | tf_op jit(solution)/shard_map/reshape | solution.py:32
  24.9 0.0 collective-permute-done.1
  24.9 5.8 %collective-permute-done.2 = f32[2,32,512]{2,1,0:T(8,128)} collective-permute-done((f32[2,32,512]{2,1,0:T(8,128)}, f32[2,32,512]{2,1,0:T(8,128)}, u32[]{:S(2)}, u32[]{:S(2)}) %collective-permute-start.2) | collective-permute-done | bytes 131104 | tf_op jit(solution)/shard_map/ppermute | solution.py:13
  30.7 1.0 %collective-permute-done.3 = f32[2,32,512]{2,1,0:T(8,128)} collective-permute-done((f32[2,32,512]{2,1,0:T(8,128)S(1)}, f32[2,32,512]{2,1,0:T(8,128)}, u32[]{:S(2)}, u32[]{:S(2)}) %collective-permute-start.3) | collective-permute-done | bytes 131104 | tf_op jit(solution)/shard_map/ppermute | solution.py:13
  31.7 1.0 %fusion.4 = f32[2,32,512]{2,1,0:T(8,128)S(1)} fusion(f32[2,32,512]{2,1,0:T(8,128)S(1)} %collective-permute-done.1, f32[1,32,512]{2,1,0:T(8,128)S(1)} %get-tuple-element.22, f32[1,32,512]{2,1,0:T(8,128)S(1)} %get-tuple-element.24, f32[2,32,512]{2,1,0:T(8,128)} %collective-permute-done.2, f32[2,32,512]{2,1,0:T(8,128)} %collective-permute-done.3), kind=kLoop, calls=%fused_computation.13 | loop fusion | flops 131072 | bytes 655360 | tf_op jit(solution)/shard_map/add | solution.py:39
  32.7 0.4 fusion.1
  33.0 0.1 collective-permute-start.4
  33.1 1.2 %collective-permute-done.4 = f32[4,16,32]{2,1,0:T(8,128)S(1)} collective-permute-done((f32[4,16,32]{2,1,0:T(8,128)S(1)}, f32[4,16,32]{2,1,0:T(8,128)S(1)}, u32[]{:S(2)}, u32[]{:S(2)}) %collective-permute-start.4) | collective-permute-done | bytes 8224 | tf_op jit(solution)/shard_map/ppermute | solution.py:13
  34.4 0.1 reshape.49
  34.5 16.2 %all_to_all.20 = bf16[32,4,512]{2,1,0:T(4,128)(2,1)S(1)} all-to-all(bf16[32,4,512]{2,1,0:T(4,128)(2,1)S(1)} %broadcast_in_dim.4), channel_id=1, replica_groups=mesh['dp'=32,'tensor'=8] {'dp'}, dimensions={0} | all-to-all | bytes 262144 | tf_op jit(solution)/shard_map/all_to_all | solution.py:51
  50.7 5.9 %all-to-all-start = ((bf16[8,32,512]{2,1,0:T(8,128)(2,1)}), bf16[8,32,512]{2,1,0:T(8,128)(2,1)S(1)}, u32[]{:S(2)}, u32[]{:S(2)}) async-start(bf16[8,32,512]{2,1,0:T(8,128)(2,1)} %reshape.48), calls=%async_computation | async-start | bytes 524288 | tf_op jit(solution)/shard_map/all_to_all | solution.py:53
  56.6 12.0 %all-to-all-done = bf16[8,32,512]{2,1,0:T(8,128)(2,1)S(1)} async-done(((bf16[8,32,512]{2,1,0:T(8,128)(2,1)}), bf16[8,32,512]{2,1,0:T(8,128)(2,1)S(1)}, u32[]{:S(2)}, u32[]{:S(2)}) %all-to-all-start) | async-done | bytes 262176 | tf_op jit(solution)/shard_map/all_to_all | solution.py:53
  68.6 0.2 fusion.10
  68.8 12.2 %all_to_all.21 = f32[8,32,128]{2,1,0:T(8,128)S(1)} all-to-all(f32[8,32,128]{2,1,0:T(8,128)S(1)} %fusion.10), channel_id=1, replica_groups=mesh['dp'=32,'tensor'=8] {'tensor'}, dimensions={0} | all-to-all | bytes 262144 | tf_op jit(solution)/shard_map/all_to_all | solution.py:55
  81.0 0.7 broadcast_in_dim.10
  81.8 5.1 %all-to-all-start.3 = ((bf16[32,32,128]{2,1,0:T(8,128)(2,1)}), bf16[32,32,128]{2,1,0:T(8,128)(2,1)S(1)}, u32[]{:S(2)}, u32[]{:S(2)}) async-start(bf16[32,32,128]{2,1,0:T(8,128)(2,1)} %broadcast_in_dim.10), calls=%async_computation.3 | async-start | bytes 524288 | tf_op jit(solution)/shard_map/all_to_all | solution.py:58
  86.9 0.0 copy-done.3
  86.9 0.6 dynamic_slice.7
  89.4 5.7 %all-to-all-done.3 = bf16[32,32,128]{2,1,0:T(8,128)(2,1)S(1)} async-done(((bf16[32,32,128]{2,1,0:T(8,128)(2,1)}), bf16[32,32,128]{2,1,0:T(8,128)(2,1)S(1)}, u32[]{:S(2)}, u32[]{:S(2)}) %all-to-all-start.3) | async-done | bytes 262176 | tf_op jit(solution)/shard_map/all_to_all | solution.py:58
  95.1 0.6 bitcast_convert_fusion
  (10 shorter events, 0.2 us)
Async XLA Ops:
  0.0 1.6 %copy-start = (bf16[1024,1024]{1,0:T(8,128)(2,1)S(1)}, bf16[1024,1024]{1,0:T(8,128)(2,1)}, u32[]{:S(2)}) copy-start(bf16[1024,1024]{1,0:T(8,128)(2,1)} %param.8) | copy-start | bytes 6291460
  0.0 9.0 %copy-start.2 = (s32[1,1024]{1,0:T(1,128)S(1)}, s32[1,1024]{1,0:T(1,128)}, u32[]{:S(2)}) copy-start(s32[1,1024]{1,0:T(1,128)} %param.11) | copy-start | bytes 12292
  0.0 20.0 %copy-start.1 = (bf16[32,4096]{1,0:T(8,128)(2,1)S(1)}, bf16[32,4096]{1,0:T(8,128)(2,1)}, u32[]{:S(2)}) copy-start(bf16[32,4096]{1,0:T(8,128)(2,1)} %param.12) | copy-start | bytes 786436
  8.8 78.1 %copy-start.3 = (s32[32]{0:T(128)S(1)}, s32[32]{0:T(128)}, u32[]{:S(2)}) copy-start(s32[32]{0:T(128)} %param.13) | copy-start | bytes 388
  8.9 1.6 %collective-permute-start = (f32[4,32,512]{2,1,0:T(8,128)S(1)}, f32[4,32,512]{2,1,0:T(8,128)S(1)}, u32[]{:S(2)}, u32[]{:S(2)}) collective-permute-start(f32[4,32,512]{2,1,0:T(8,128)S(1)} %broadcast_select_fusion), channel_id=1, source_target_pairs={{0,1},{1,0},{2,3},{3,2},{4,5},{5,4},{6,7},{7,6},{8,9},{9,8},{10,11... | collective-permute-start | bytes 786440 | tf_op jit(solution)/shard_map/ppermute | solution.py:13
  11.3 13.5 %collective-permute-start.1 = (f32[2,32,512]{2,1,0:T(8,128)}, f32[2,32,512]{2,1,0:T(8,128)S(1)}, u32[]{:S(2)}, u32[]{:S(2)}) collective-permute-start(f32[2,32,512]{2,1,0:T(8,128)} %get-tuple-element.27), channel_id=1, source_target_pairs={{0,2},{1,3},{2,0},{3,1},{4,6},{5,7},{6,4},{7,5},{8,10},{9,11},{10,... | collective-permute-start | bytes 393224 | tf_op jit(solution)/shard_map/ppermute | solution.py:13
  14.6 16.1 %collective-permute-start.2 = (f32[2,32,512]{2,1,0:T(8,128)}, f32[2,32,512]{2,1,0:T(8,128)}, u32[]{:S(2)}, u32[]{:S(2)}) collective-permute-start(f32[2,32,512]{2,1,0:T(8,128)} %get-tuple-element.26), channel_id=1, source_target_pairs={{0,4},{1,5},{2,6},{3,7},{4,0},{5,1},{6,2},{7,3},{8,12},{9,13},{10,... | collective-permute-start | bytes 393224 | tf_op jit(solution)/shard_map/ppermute | solution.py:13
  20.0 11.6 %collective-permute-start.3 = (f32[2,32,512]{2,1,0:T(8,128)S(1)}, f32[2,32,512]{2,1,0:T(8,128)}, u32[]{:S(2)}, u32[]{:S(2)}) collective-permute-start(f32[2,32,512]{2,1,0:T(8,128)S(1)} %get-tuple-element.25), channel_id=1, source_target_pairs={{0,6},{1,7},{2,4},{3,5},{4,2},{5,3},{6,0},{7,1},{8,14},{9,15},{10,... | collective-permute-start | bytes 393224 | tf_op jit(solution)/shard_map/ppermute | solution.py:13
  33.0 1.3 %collective-permute-start.4 = (f32[4,16,32]{2,1,0:T(8,128)S(1)}, f32[4,16,32]{2,1,0:T(8,128)S(1)}, u32[]{:S(2)}, u32[]{:S(2)}) collective-permute-start(f32[4,16,32]{2,1,0:T(8,128)S(1)} %slice_select_fusion.4), channel_id=1, source_target_pairs={{0,1},{1,0},{2,3},{3,2},{4,5},{5,4},{6,7},{7,6},{8,9},{9,8},{10,11... | collective-permute-start | bytes 24584 | tf_op jit(solution)/shard_map/ppermute | solution.py:13
  50.7 18.0 %all-to-all-start = ((bf16[8,32,512]{2,1,0:T(8,128)(2,1)}), bf16[8,32,512]{2,1,0:T(8,128)(2,1)S(1)}, u32[]{:S(2)}, u32[]{:S(2)}) async-start(bf16[8,32,512]{2,1,0:T(8,128)(2,1)} %reshape.48), calls=%async_computation | async-start | bytes 524288 | tf_op jit(solution)/shard_map/all_to_all | solution.py:53
  81.8 13.4 %all-to-all-start.3 = ((bf16[32,32,128]{2,1,0:T(8,128)(2,1)}), bf16[32,32,128]{2,1,0:T(8,128)(2,1)S(1)}, u32[]{:S(2)}, u32[]{:S(2)}) async-start(bf16[32,32,128]{2,1,0:T(8,128)(2,1)} %broadcast_in_dim.10), calls=%async_computation.3 | async-start | bytes 524288 | tf_op jit(solution)/shard_map/all_to_all | solution.py:58

commit v3 on v0

v3 whole, which is shorter than its diff:
```python
import jax
import jax.numpy as jnp
from jax import lax
from jax.experimental import pallas as pl
from jax.experimental.pallas import tpu as pltpu
from jax.sharding import PartitionSpec as P

RANK = 64
DOCS_DEV = 4
N_DP = 32
DOCS = N_DP * DOCS_DEV
TOKENS = 1024
STEP = 256
NT = (((1,), (1,)), ((), ()))


def swap(value, bits):
    return lax.ppermute(value, "tensor", [(i, i ^ bits) for i in range(8)])


def pick(first, low, high):
    return jnp.where(first, low, high), jnp.where(first, high, low)


def project_kernel(out_grads, activations, proj_out, proj_in, part):
    from_out = lax.dot_general(out_grads[...], proj_out[...], NT, preferred_element_type=jnp.float32)
    from_in = lax.dot_general(activations[...], proj_in[...], NT, preferred_element_type=jnp.float32)
    part[...] = jnp.concatenate([from_out, from_in], axis=1)


def project(out_grads, activations, proj_out, proj_in):
    d, ff = out_grads.shape[1], activations.shape[1]
    return pl.pallas_call(
        project_kernel,
        grid=(TOKENS // STEP,),
        in_specs=[
            pl.BlockSpec((STEP, d), lambda i: (i, 0)),
            pl.BlockSpec((STEP, ff), lambda i: (i, 0)),
            pl.BlockSpec((RANK, d), lambda i: (0, 0)),
            pl.BlockSpec((RANK, ff), lambda i: (0, 0)),
        ],
        out_specs=pl.BlockSpec((STEP, 2 * RANK), lambda i: (i, 0)),
        out_shape=jax.ShapeDtypeStruct((TOKENS, 2 * RANK), jnp.float32),
        compiler_params=pltpu.CompilerParams(vmem_limit_bytes=60 << 20),
        name="project",
    )(out_grads, activations, proj_out, proj_in)


def features_kernel(ids, p, p_more, q, q_more, feat):
    both = jnp.concatenate([p[...] + p_more[...], q[...] + q_more[...]], axis=0)
    out_t = both.T[:RANK]
    weighted = jnp.concatenate([jnp.where(ids[...] == d, out_t, 0.0) for d in range(DOCS_DEV)], axis=0)
    feat[...] = jnp.dot(
        weighted, both[:, RANK:], precision=lax.Precision.HIGHEST, preferred_element_type=jnp.float32
    )


def features(ids, p, p_more, q, q_more):
    return pl.pallas_call(
        features_kernel,
        out_shape=jax.ShapeDtypeStruct((DOCS_DEV * RANK, RANK), jnp.float32),
        compiler_params=pltpu.CompilerParams(vmem_limit_bytes=16 << 20),
        name="features",
    )(ids, p, p_more, q, q_more)


def score_kernel(mine, got, feats, scored):
    half = feats.shape[1]
    rows = jnp.concatenate([mine[:, :half], got[:, :half], mine[:, half:], got[:, half:]], axis=0)
    every = lax.dot_general(rows, feats[...], NT, preferred_element_type=jnp.float32)
    source = lax.broadcasted_iota(jnp.int32, (2 * DOCS, DOCS), 0)
    doc = lax.broadcasted_iota(jnp.int32, (2 * DOCS, DOCS), 1)
    first = (doc >> 2) * 8 + (doc & 3)
    count = rows.shape[0] // 2
    scored[...] = jnp.dot(
        every[:count], (source == first).astype(jnp.float32), precision=lax.Precision.HIGHEST,
        preferred_element_type=jnp.float32,
    ) + jnp.dot(
        every[count:], (source == first + 4).astype(jnp.float32), precision=lax.Precision.HIGHEST,
        preferred_element_type=jnp.float32,
    )


def score(mine, got, feats):
    return pl.pallas_call(
        score_kernel,
        out_shape=jax.ShapeDtypeStruct((2 * mine.shape[0], DOCS), jnp.float32),
        compiler_params=pltpu.CompilerParams(vmem_limit_bytes=16 << 20),
        name="score",
    )(mine, got, feats)


def shards(activations, out_grads, proj_in, proj_out, doc_ids, queries, block_owner):
    core0 = (lax.axis_index("tensor") & 1) == 0
    half = TOKENS // 2

    part = project(out_grads, activations, proj_out.T, proj_in.T)
    keep, send = pick(core0, part[:half], part[half:])
    total = keep + swap(send, 1)
    p, q = total[: half // 2], total[half // 2 :]
    p, q = p + swap(p, 6), q + swap(q, 2)
    p_more, q_more = swap(p, 2), swap(q, 6)

    columns = queries.shape[1] // 2
    mine, other = pick(core0, queries[:, :columns], queries[:, columns:])
    got = swap(other, 1)

    ids = jnp.where(core0, doc_ids[:, :half], doc_ids[:, half:])
    feat = features(ids, p, p_more, q, q_more).reshape(DOCS_DEV, 2, RANK // 2, RANK)
    keep, send = pick(core0, feat[:, 0], feat[:, 1])
    block = (keep + swap(send, 1)).astype(jnp.bfloat16)
    block = block.reshape(DOCS_DEV, 2, columns // 2).transpose(1, 0, 2).reshape(2 * DOCS_DEV, columns // 2)

    everyone = jnp.broadcast_to(block, (N_DP,) + block.shape)
    feats = lax.all_to_all(everyone, "dp", 0, 0).reshape(2 * DOCS, columns // 2)
    scored = score(mine, got, feats)
    rows = queries.shape[0]
    stored = (scored[:rows] + swap(scored[rows:], 1)).astype(jnp.bfloat16)

    blocks = lax.all_to_all(jnp.broadcast_to(stored, (N_DP,) + stored.shape), "dp", 0, 0)
    owner = block_owner[lax.axis_index("dp")]
    return lax.dynamic_index_in_dim(blocks, owner, 0, keepdims=False).astype(jnp.float32)


def solution(mesh):
    placed = (
        P("dp", "tensor"),
        P("dp", "tensor"),
        P("tensor", None),
        P("tensor", None),
        P("dp", None),
        P(("dp", "tensor"), None),
        P(),
    )
    return jax.shard_map(
        shards, mesh=mesh, in_specs=placed, out_specs=P(("dp", "tensor"), None), check_vma=False
    )
```

time: 341 us -> 75.4 us (0.22); the launches traced: 336 us -> 74.8 us
  waiting for transfers between devices: 227 us -> 35.5 us
  blocking collectives: 78.9 us -> 0 us
  starting transfers between devices: 0.08 us -> 23.8 us
  between operations: 14.1 us -> 2.09 us
  matrix products: 10.9 us -> 0 us
  Pallas kernels: 0 us -> 8.27 us
    all_gather x1 -> x0, waiting for transfers between devices: 150 us -> none  [score_all(): lax.all_gather(doc_feat, 'dp', axis=0, tiled=True)]
    all_gather x1 -> x0, blocking collectives: 78.9 us -> none  [shards(): gathered = lax.all_gather(stored, 'dp', axis=0, tiled=True)]
    psum x1 -> x0, waiting for transfers between devices: 77.1 us -> none  [shards(): in_proj, out_proj = lax.psum((part_in, part_out), 'tensor')]
    ppermute x0 -> x8, waiting for transfers between devices: none -> 19.9 us  [swap(): return lax.ppermute(value, 'tensor', [(i, i ^ bits) for i in range(8)])]
    all_to_all x0 -> x2, waiting for transfers between devices: none -> 15.6 us  [the longest x1 9.56 us: shards(): feats = lax.all_to_all(everyone, 'dp', 0, 0).reshape(2 * DOCS, columns // 2)]
    all_to_all x0 -> x2, starting transfers between devices: none -> 13.7 us  [the longest x1 8.82 us: shards(): feats = lax.all_to_all(everyone, 'dp', 0, 0).reshape(2 * DOCS, columns // 2)]
    dot_general x4 -> x0, matrix products: 10.9 us -> none  [the longest x1 6.13 us: shards(): part_in = jnp.dot(activations, proj_in, preferred_element_type=jnp.float32)]
    ppermute x0 -> x8, starting transfers between devices: none -> 10.1 us  [swap(): return lax.ppermute(value, 'tensor', [(i, i ^ bits) for i in range(8)])]
  transfers between devices with their start and end apart: 2 -> 10, of which waited for: 2 -> 10; matrix products, arithmetic and copies ran while one was open for 0% -> 1% of each run, Pallas kernels for 0% -> 0%
where the time goes in v3:
time: 75.4 us; the launch traced here: 74.8 us
  waiting for transfers between devices  35.5 us (47%)
  starting transfers between devices  23.8 us (32%)
  Pallas kernels  8.27 us (11%)
  other arithmetic  2.83 us (4%)
  local copies, waits for them, and re-layouts  2.32 us (3%)
  between operations  2.09 us (3%)
    ppermute x8, waiting for transfers between devices, swap(): return lax.ppermute(value, 'tensor', [(i, i ^ bits) for i in range(8)])  19.9 us
    ppermute x8, starting transfers between devices, swap(): return lax.ppermute(value, 'tensor', [(i, i ^ bits) for i in range(8)])  10.1 us
    all_to_all x1, waiting for transfers between devices, shards(): feats = lax.all_to_all(everyone, 'dp', 0, 0).reshape(2 * DOCS, columns // 2)  9.56 us
    all_to_all x1, starting transfers between devices, shards(): feats = lax.all_to_all(everyone, 'dp', 0, 0).reshape(2 * DOCS, columns // 2)  8.82 us
    pallas_call x1, Pallas kernels, project(): pl.pallas_call(project_kernel, grid=(TOKENS // STEP,), in_specs=[pl.Block...  6.87 us
    all_to_all x1, waiting for transfers between devices, shards(): lax.all_to_all(jnp.broadcast_to(stored, (N_DP,) + stored.shape), 'dp', 0, 0)  6.09 us
    all_to_all x1, starting transfers between devices, shards(): lax.all_to_all(jnp.broadcast_to(stored, (N_DP,) + stored.shape), 'dp', 0, 0)  4.86 us
  transfers between devices with their start and end apart: 10, of which 10 were waited for; matrix products, arithmetic and copies ran while one was open for 1% of the time, Pallas kernels for 0%

profile of v3, /device:TPU:8, one launch (start us, length us, event | category | flops | bytes accessed | tf_op | source)
XLA Modules:
  0.0 74.8 jit_solution(12167186318670561839)
XLA Ops:
  0.0 0.0 copy-start.1
  0.0 0.0 copy-start
  0.0 0.0 copy-start.2
  0.0 6.9 %project.1 = f32[1024,128]{1,0:T(8,128)} custom-call(bf16[1024,1024]{1,0:T(8,128)(2,1)} %out_grads.1, bf16[1024,3584]{1,0:T(8,128)(2,1)} %activations.1, bf16[64,1024]{1,0:T(8,128)(2,1)} %bitcast.35, bf16[64,3584]{1,0:T(8,128)(2,1)} %bitcast.34), custom_call_target="tpu_custom_call" | custom-call | tf_op jit(solution)/shard_map/project/pallas_call | solution.py:33
  6.9 1.1 %slice_select_fusion = f32[512,128]{1,0:T(8,128)S(1)} fusion(f32[1024,128]{1,0:T(8,128)} %project.1, pred[]{:T(512)S(6)} %eq.3), kind=kLoop, calls=%fused_computation.1 | loop fusion | flops 65536 | bytes 786433 | tf_op jit(solution)/shard_map/jit(_where)/select_n | solution.py:22
  7.9 0.1 collective-permute-start.1
  8.0 1.5 %collective-permute-done.1 = f32[512,128]{1,0:T(8,128)S(1)} collective-permute-done((f32[512,128]{1,0:T(8,128)S(1)}, f32[512,128]{1,0:T(8,128)S(1)}, u32[]{:S(2)}, u32[]{:S(2)}) %collective-permute-start.1) | collective-permute-done | bytes 262176 | tf_op jit(solution)/shard_map/ppermute | solution.py:18
  9.6 1.1 %select_add_fusion = f32[512,128]{1,0:T(8,128)S(1)} fusion(f32[512,128]{1,0:T(8,128)S(1)} %collective-permute-done.1, f32[1024,128]{1,0:T(8,128)} %project.1, pred[]{:T(512)S(6)} %eq.3), kind=kLoop, calls=%fused_computation | loop fusion | flops 131072 | bytes 1048577 | tf_op jit(solution)/shard_map/add | solution.py:99
  10.7 6.4 %collective-permute-start.2 = (f32[256,128]{1,0:T(8,128)S(1)}, f32[256,128]{1,0:T(8,128)S(1)}, u32[]{:S(2)}, u32[]{:S(2)}) collective-permute-start(f32[256,128]{1,0:T(8,128)S(1)} %get-tuple-element.8), channel_id=1, source_target_pairs={{0,6},{1,7},{2,4},{3,5},{4,2},{5,3},{6,0},{7,1},{8,14},{9,15},{10,... | collective-permute-start | bytes 393224 | tf_op jit(solution)/shard_map/ppermute | solution.py:18
  17.1 1.4 %collective-permute-start.4 = (f32[256,128]{1,0:T(8,128)S(1)}, f32[256,128]{1,0:T(8,128)S(1)}, u32[]{:S(2)}, u32[]{:S(2)}) collective-permute-start(f32[256,128]{1,0:T(8,128)S(1)} %get-tuple-element.7), channel_id=1, source_target_pairs={{0,2},{1,3},{2,0},{3,1},{4,6},{5,7},{6,4},{7,5},{8,10},{9,11},{10,... | collective-permute-start | bytes 393224 | tf_op jit(solution)/shard_map/ppermute | solution.py:18
  18.5 4.4 %collective-permute-done.2 = f32[256,128]{1,0:T(8,128)S(1)} collective-permute-done((f32[256,128]{1,0:T(8,128)S(1)}, f32[256,128]{1,0:T(8,128)S(1)}, u32[]{:S(2)}, u32[]{:S(2)}) %collective-permute-start.2) | collective-permute-done | bytes 131104 | tf_op jit(solution)/shard_map/ppermute | solution.py:18
  23.0 3.1 %collective-permute-done.4 = f32[256,128]{1,0:T(8,128)S(1)} collective-permute-done((f32[256,128]{1,0:T(8,128)S(1)}, f32[256,128]{1,0:T(8,128)S(1)}, u32[]{:S(2)}, u32[]{:S(2)}) %collective-permute-start.4) | collective-permute-done | bytes 131104 | tf_op jit(solution)/shard_map/ppermute | solution.py:18
  26.1 1.1 %collective-permute-start.3 = (f32[256,128]{1,0:T(8,128)S(1)}, f32[256,128]{1,0:T(8,128)S(1)}, u32[]{:S(2)}, u32[]{:S(2)}) collective-permute-start(f32[256,128]{1,0:T(8,128)S(1)} %get-tuple-element.6.p), channel_id=1, source_target_pairs={{0,2},{1,3},{2,0},{3,1},{4,6},{5,7},{6,4},{7,5},{8,10},{9,11},{10,... | collective-permute-start | bytes 393224 | tf_op jit(solution)/shard_map/ppermute | solution.py:18
  27.1 0.8 %collective-permute-start.5 = (f32[256,128]{1,0:T(8,128)S(1)}, f32[256,128]{1,0:T(8,128)S(1)}, u32[]{:S(2)}, u32[]{:S(2)}) collective-permute-start(f32[256,128]{1,0:T(8,128)S(1)} %get-tuple-element.5.q), channel_id=1, source_target_pairs={{0,6},{1,7},{2,4},{3,5},{4,2},{5,3},{6,0},{7,1},{8,14},{9,15},{10,... | collective-permute-start | bytes 393224 | tf_op jit(solution)/shard_map/ppermute | solution.py:18
  28.0 0.0 copy-done.1
  28.0 5.7 %collective-permute-done.3.p_more = f32[256,128]{1,0:T(8,128)S(1)} collective-permute-done((f32[256,128]{1,0:T(8,128)S(1)}, f32[256,128]{1,0:T(8,128)S(1)}, u32[]{:S(2)}, u32[]{:S(2)}) %collective-permute-start.3) | collective-permute-done | bytes 131104 | tf_op jit(solution)/shard_map/ppermute | solution.py:18
  33.7 1.4 %collective-permute-done.5.q_more = f32[256,128]{1,0:T(8,128)S(1)} collective-permute-done((f32[256,128]{1,0:T(8,128)S(1)}, f32[256,128]{1,0:T(8,128)S(1)}, u32[]{:S(2)}, u32[]{:S(2)}) %collective-permute-start.5) | collective-permute-done | bytes 131104 | tf_op jit(solution)/shard_map/ppermute | solution.py:18
  35.1 0.7 features.1
  35.8 0.1 collective-permute-start.6
  35.9 1.2 %collective-permute-done.6 = f32[4,32,64]{2,1,0:T(8,128)S(1)} collective-permute-done((f32[4,32,64]{2,1,0:T(8,128)S(1)}, f32[4,32,64]{2,1,0:T(8,128)S(1)}, u32[]{:S(2)}, u32[]{:S(2)}) %collective-permute-start.6) | collective-permute-done | bytes 32800 | tf_op jit(solution)/shard_map/ppermute | solution.py:18
  37.2 0.1 reshape.19
  37.3 0.9 %broadcast_in_dim.6 = bf16[32,8,1024]{2,1,0:T(8,128)(2,1)} broadcast(bf16[8,1024]{1,0:T(8,128)(2,1)S(1)} %reshape.20), dimensions={1,2} | broadcast | bytes 540672 | tf_op jit(solution)/shard_map/broadcast_in_dim | solution.py:114
  38.2 8.8 %all-to-all-start = ((bf16[32,8,1024]{2,1,0:T(8,128)(2,1)}), bf16[32,8,1024]{2,1,0:T(8,128)(2,1)S(1)}, u32[]{:S(2)}, u32[]{:S(2)}) async-start(bf16[32,8,1024]{2,1,0:T(8,128)(2,1)} %broadcast_in_dim.6), calls=%async_computation | async-start | bytes 1048576 | tf_op jit(solution)/shard_map/all_to_all | solution.py:115
  47.0 0.0 copy-done
  47.0 0.1 collective-permute-start
  47.1 1.3 %collective-permute-done.got = bf16[32,2048]{1,0:T(8,128)(2,1)S(1)} collective-permute-done((bf16[32,2048]{1,0:T(8,128)(2,1)S(1)}, bf16[32,2048]{1,0:T(8,128)(2,1)S(1)}, u32[]{:S(2)}, u32[]{:S(2)}) %collective-permute-start) | collective-permute-done | bytes 131104 | tf_op jit(solution)/shard_map/ppermute | solution.py:18
  48.5 9.6 %all-to-all-done = bf16[32,8,1024]{2,1,0:T(8,128)(2,1)S(1)} async-done(((bf16[32,8,1024]{2,1,0:T(8,128)(2,1)}), bf16[32,8,1024]{2,1,0:T(8,128)(2,1)S(1)}, u32[]{:S(2)}, u32[]{:S(2)}) %all-to-all-start) | async-done | bytes 524320 | tf_op jit(solution)/shard_map/all_to_all | solution.py:115
  58.0 0.7 score.1
  58.7 0.1 collective-permute-start.7
  58.8 1.2 %collective-permute-done.7 = f32[32,128]{1,0:T(8,128)S(1)} collective-permute-done((f32[32,128]{1,0:T(8,128)S(1)}, f32[32,128]{1,0:T(8,128)S(1)}, u32[]{:S(2)}, u32[]{:S(2)}) %collective-permute-start.7) | collective-permute-done | bytes 16416 | tf_op jit(solution)/shard_map/ppermute | solution.py:18
  60.0 0.7 broadcast_in_dim.7
  60.7 4.9 %all-to-all-start.1 = ((bf16[32,32,128]{2,1,0:T(8,128)(2,1)}), bf16[32,32,128]{2,1,0:T(8,128)(2,1)S(1)}, u32[]{:S(2)}, u32[]{:S(2)}) async-start(bf16[32,32,128]{2,1,0:T(8,128)(2,1)} %broadcast_in_dim.7), calls=%async_computation.1 | async-start | bytes 524288 | tf_op jit(solution)/shard_map/all_to_all | solution.py:120
  65.6 0.0 copy-done.2
  65.6 0.6 dynamic_slice.7
  68.1 6.1 %all-to-all-done.1 = bf16[32,32,128]{2,1,0:T(8,128)(2,1)S(1)} async-done(((bf16[32,32,128]{2,1,0:T(8,128)(2,1)}), bf16[32,32,128]{2,1,0:T(8,128)(2,1)S(1)}, u32[]{:S(2)}, u32[]{:S(2)}) %all-to-all-start.1) | async-done | bytes 262176 | tf_op jit(solution)/shard_map/all_to_all | solution.py:120
  74.2 0.6 bitcast_convert_fusion
  (10 shorter events, 0.1 us)
Async XLA Ops:
  0.0 28.0 %copy-start.1 = (s32[1,1024]{1,0:T(1,128)S(1)}, s32[1,1024]{1,0:T(1,128)}, u32[]{:S(2)}) copy-start(s32[1,1024]{1,0:T(1,128)} %param.11) | copy-start | bytes 12292
  0.0 47.0 %copy-start = (bf16[32,4096]{1,0:T(8,128)(2,1)S(1)}, bf16[32,4096]{1,0:T(8,128)(2,1)}, u32[]{:S(2)}) copy-start(bf16[32,4096]{1,0:T(8,128)(2,1)} %param.12) | copy-start | bytes 786436
  0.0 65.6 %copy-start.2 = (s32[32]{0:T(128)S(1)}, s32[32]{0:T(128)}, u32[]{:S(2)}) copy-start(s32[32]{0:T(128)} %param.13) | copy-start | bytes 388
  7.9 1.6 %collective-permute-start.1 = (f32[512,128]{1,0:T(8,128)S(1)}, f32[512,128]{1,0:T(8,128)S(1)}, u32[]{:S(2)}, u32[]{:S(2)}) collective-permute-start(f32[512,128]{1,0:T(8,128)S(1)} %slice_select_fusion), channel_id=1, source_target_pairs={{0,1},{1,0},{2,3},{3,2},{4,5},{5,4},{6,7},{7,6},{8,9},{9,8},{10,11... | collective-permute-start | bytes 786440 | tf_op jit(solution)/shard_map/ppermute | solution.py:18
  10.7 12.3 %collective-permute-start.2 = (f32[256,128]{1,0:T(8,128)S(1)}, f32[256,128]{1,0:T(8,128)S(1)}, u32[]{:S(2)}, u32[]{:S(2)}) collective-permute-start(f32[256,128]{1,0:T(8,128)S(1)} %get-tuple-element.8), channel_id=1, source_target_pairs={{0,6},{1,7},{2,4},{3,5},{4,2},{5,3},{6,0},{7,1},{8,14},{9,15},{10,... | collective-permute-start | bytes 393224 | tf_op jit(solution)/shard_map/ppermute | solution.py:18
  17.1 9.0 %collective-permute-start.4 = (f32[256,128]{1,0:T(8,128)S(1)}, f32[256,128]{1,0:T(8,128)S(1)}, u32[]{:S(2)}, u32[]{:S(2)}) collective-permute-start(f32[256,128]{1,0:T(8,128)S(1)} %get-tuple-element.7), channel_id=1, source_target_pairs={{0,2},{1,3},{2,0},{3,1},{4,6},{5,7},{6,4},{7,5},{8,10},{9,11},{10,... | collective-permute-start | bytes 393224 | tf_op jit(solution)/shard_map/ppermute | solution.py:18
  26.1 7.6 %collective-permute-start.3 = (f32[256,128]{1,0:T(8,128)S(1)}, f32[256,128]{1,0:T(8,128)S(1)}, u32[]{:S(2)}, u32[]{:S(2)}) collective-permute-start(f32[256,128]{1,0:T(8,128)S(1)} %get-tuple-element.6.p), channel_id=1, source_target_pairs={{0,2},{1,3},{2,0},{3,1},{4,6},{5,7},{6,4},{7,5},{8,10},{9,11},{10,... | collective-permute-start | bytes 393224 | tf_op jit(solution)/shard_map/ppermute | solution.py:18
  27.1 7.9 %collective-permute-start.5 = (f32[256,128]{1,0:T(8,128)S(1)}, f32[256,128]{1,0:T(8,128)S(1)}, u32[]{:S(2)}, u32[]{:S(2)}) collective-permute-start(f32[256,128]{1,0:T(8,128)S(1)} %get-tuple-element.5.q), channel_id=1, source_target_pairs={{0,6},{1,7},{2,4},{3,5},{4,2},{5,3},{6,0},{7,1},{8,14},{9,15},{10,... | collective-permute-start | bytes 393224 | tf_op jit(solution)/shard_map/ppermute | solution.py:18
  35.8 1.3 %collective-permute-start.6 = (f32[4,32,64]{2,1,0:T(8,128)S(1)}, f32[4,32,64]{2,1,0:T(8,128)S(1)}, u32[]{:S(2)}, u32[]{:S(2)}) collective-permute-start(f32[4,32,64]{2,1,0:T(8,128)S(1)} %select_bitcast_fusion), channel_id=1, source_target_pairs={{0,1},{1,0},{2,3},{3,2},{4,5},{5,4},{6,7},{7,6},{8,9},{9,8},{10,11... | collective-permute-start | bytes 98312 | tf_op jit(solution)/shard_map/ppermute | solution.py:18
  38.2 19.9 %all-to-all-start = ((bf16[32,8,1024]{2,1,0:T(8,128)(2,1)}), bf16[32,8,1024]{2,1,0:T(8,128)(2,1)S(1)}, u32[]{:S(2)}, u32[]{:S(2)}) async-start(bf16[32,8,1024]{2,1,0:T(8,128)(2,1)} %broadcast_in_dim.6), calls=%async_computation | async-start | bytes 1048576 | tf_op jit(solution)/shard_map/all_to_all | solution.py:115
  47.0 1.4 %collective-permute-start = (bf16[32,2048]{1,0:T(8,128)(2,1)S(1)}, bf16[32,2048]{1,0:T(8,128)(2,1)S(1)}, u32[]{:S(2)}, u32[]{:S(2)}) collective-permute-start(bf16[32,2048]{1,0:T(8,128)(2,1)S(1)} %get-tuple-element.9), channel_id=1, source_target_pairs={{0,1},{1,0},{2,3},{3,2},{4,5},{5,4},{6,7},{7,6},{8,9},{9,8},{10,11... | collective-permute-start | bytes 393224 | tf_op jit(solution)/shard_map/ppermute | solution.py:18
  58.7 1.3 %collective-permute-start.7 = (f32[32,128]{1,0:T(8,128)S(1)}, f32[32,128]{1,0:T(8,128)S(1)}, u32[]{:S(2)}, u32[]{:S(2)}) collective-permute-start(f32[32,128]{1,0:T(8,128)S(1)} %slice.55), channel_id=1, source_target_pairs={{0,1},{1,0},{2,3},{3,2},{4,5},{5,4},{6,7},{7,6},{8,9},{9,8},{10,11... | collective-permute-start | bytes 49160 | tf_op jit(solution)/shard_map/ppermute | solution.py:18
  60.7 13.5 %all-to-all-start.1 = ((bf16[32,32,128]{2,1,0:T(8,128)(2,1)}), bf16[32,32,128]{2,1,0:T(8,128)(2,1)S(1)}, u32[]{:S(2)}, u32[]{:S(2)}) async-start(bf16[32,32,128]{2,1,0:T(8,128)(2,1)} %broadcast_in_dim.7), calls=%async_computation.1 | async-start | bytes 524288 | tf_op jit(solution)/shard_map/all_to_all | solution.py:120

commit v4 on v3

v4 whole, which is shorter than its diff:
```python
import jax
import jax.numpy as jnp
from jax import lax
from jax.experimental import pallas as pl
from jax.experimental.pallas import tpu as pltpu
from jax.sharding import PartitionSpec as P

RANK = 64
DOCS_DEV = 4
N_DP = 32
DOCS = N_DP * DOCS_DEV
TOKENS = 1024
STEP = 256
NT = (((1,), (1,)), ((), ()))


def swap(value, even, odd):
    return lax.ppermute(value, "tensor", [(i, i ^ (odd if i & 1 else even)) for i in range(8)])


def pick(first, low, high):
    return jnp.where(first, low, high), jnp.where(first, high, low)


def project_kernel(out_grads, activations, proj_out, proj_in, send, keep, grads, acts, raw_out, raw_in, wide_out, wide_in, sem):
    blocks = TOKENS // STEP
    first = jnp.where((lax.axis_index("tensor") & 1) == 0, TOKENS // 2, 0)

    def rows(block):
        start = first + block * STEP
        return pl.ds(pl.multiple_of(jnp.where(start >= TOKENS, start - TOKENS, start), STEP), STEP)

    def copies(block):
        here = pl.ds(pl.multiple_of(block * STEP, STEP), STEP)
        return (
            pltpu.make_async_copy(out_grads.at[rows(block)], grads.at[here], sem.at[2 + 2 * block]),
            pltpu.make_async_copy(activations.at[rows(block)], acts.at[here], sem.at[3 + 2 * block]),
        )

    weights = (
        pltpu.make_async_copy(proj_out, raw_out, sem.at[0]),
        pltpu.make_async_copy(proj_in, raw_in, sem.at[1]),
    )
    for copy in weights:
        copy.start()
    for block in range(blocks):
        for copy in copies(block):
            copy.start()
    for copy in weights:
        copy.wait()
    wide_out[...] = jnp.concatenate([raw_out[...], jnp.zeros_like(raw_out)], axis=0).T
    wide_in[...] = jnp.concatenate([jnp.zeros_like(raw_in), raw_in[...]], axis=0).T

    def run(block, target):
        here = pl.ds(pl.multiple_of(block * STEP, STEP), STEP)
        there = pl.ds(pl.multiple_of(block % (blocks // 2) * STEP, STEP), STEP)
        for copy in copies(block):
            copy.wait()
        target[there] = jnp.dot(grads[here], wide_out[...], preferred_element_type=jnp.float32) + jnp.dot(
            acts[here], wide_in[...], preferred_element_type=jnp.float32
        )

    @pl.loop(0, blocks // 2)
    def _(block):
        run(block, send)

    @pl.loop(blocks // 2, blocks)
    def _(block):
        run(block, keep)


def project(out_grads, activations, proj_out, proj_in):
    d, ff = out_grads.shape[1], activations.shape[1]
    half = pltpu.VMEM((TOKENS // 2, 2 * RANK), jnp.float32)
    args = [pltpu.with_memory_space_constraint(x, pltpu.HBM) for x in (out_grads, activations, proj_out, proj_in)]
    return pl.pallas_call(
        project_kernel,
        in_specs=[pl.BlockSpec(memory_space=pltpu.HBM)] * 4,
        out_specs=[pl.BlockSpec(memory_space=pltpu.VMEM)] * 2,
        out_shape=[half, half],
        scratch_shapes=[
            pltpu.VMEM((TOKENS, d), jnp.bfloat16),
            pltpu.VMEM((TOKENS, ff), jnp.bfloat16),
            pltpu.VMEM((RANK, d), jnp.bfloat16),
            pltpu.VMEM((RANK, ff), jnp.bfloat16),
            pltpu.VMEM((d, 2 * RANK), jnp.bfloat16),
            pltpu.VMEM((ff, 2 * RANK), jnp.bfloat16),
            pltpu.SemaphoreType.DMA((2 + 2 * (TOKENS // STEP),)),
        ],
        compiler_params=pltpu.CompilerParams(vmem_limit_bytes=40 << 20),
        name="project",
    )(*args)


def features_kernel(ids, total, more, feat):
    both = total[...] + more[...]
    out_t = both.T[:RANK]
    weighted = jnp.concatenate([jnp.where(ids[...] == d, out_t, 0.0) for d in range(DOCS_DEV)], axis=0)
    feat[...] = jnp.dot(
        weighted, both[:, RANK:], precision=lax.Precision.HIGHEST, preferred_element_type=jnp.float32
    )


def features(ids, total, more):
    return pl.pallas_call(
        features_kernel,
        out_shape=jax.ShapeDtypeStruct((DOCS_DEV * RANK, RANK), jnp.float32),
        compiler_params=pltpu.CompilerParams(vmem_limit_bytes=16 << 20),
        name="features",
    )(ids, total, more)


def score_kernel(mine, got, feats, scored):
    half = feats.shape[1]
    rows = jnp.concatenate([mine[:, :half], got[:, :half], mine[:, half:], got[:, half:]], axis=0)
    every = lax.dot_general(rows, feats[...], NT, preferred_element_type=jnp.float32)
    source = lax.broadcasted_iota(jnp.int32, (2 * DOCS, DOCS), 0)
    doc = lax.broadcasted_iota(jnp.int32, (2 * DOCS, DOCS), 1)
    first = (doc >> 2) * 8 + (doc & 3)
    count = rows.shape[0] // 2
    scored[...] = jnp.dot(
        every[:count], (source == first).astype(jnp.float32), precision=lax.Precision.HIGHEST,
        preferred_element_type=jnp.float32,
    ) + jnp.dot(
        every[count:], (source == first + 4).astype(jnp.float32), precision=lax.Precision.HIGHEST,
        preferred_element_type=jnp.float32,
    )


def score(mine, got, feats):
    return pl.pallas_call(
        score_kernel,
        out_shape=jax.ShapeDtypeStruct((2 * mine.shape[0], DOCS), jnp.float32),
        compiler_params=pltpu.CompilerParams(vmem_limit_bytes=16 << 20),
        name="score",
    )(mine, got, feats)


def spread_kernel(block, everyone):
    everyone[...] = jnp.broadcast_to(block[...], everyone.shape)


def spread(block):
    return pl.pallas_call(
        spread_kernel,
        out_specs=pl.BlockSpec(memory_space=pltpu.VMEM),
        out_shape=pltpu.VMEM((N_DP,) + block.shape, block.dtype),
        compiler_params=pltpu.CompilerParams(vmem_limit_bytes=8 << 20),
        name="spread",
    )(block)


def shards(activations, out_grads, proj_in, proj_out, doc_ids, queries, block_owner):
    core0 = (lax.axis_index("tensor") & 1) == 0
    half = TOKENS // 2

    send, keep = project(out_grads, activations, proj_out.T, proj_in.T)
    total = keep + swap(send, 1, 1)
    total = total + swap(total, 2, 6)
    more = swap(total, 6, 2)

    columns = queries.shape[1] // 2
    mine, other = pick(core0, queries[:, :columns], queries[:, columns:])
    got = swap(other, 1, 1)

    ids = jnp.where(core0, doc_ids[:, :half], doc_ids[:, half:])
    here = lax.axis_index("dp")
    owner = lax.dynamic_slice(block_owner, (here,), (1,), allow_negative_indices=False)[0] & (N_DP - 1)
    more, mine, got, owner = lax.optimization_barrier((more, mine, got, owner))
    feat = features(ids, total, more).reshape(DOCS_DEV, 2, RANK // 2, RANK)
    keep, send = pick(core0, feat[:, 0], feat[:, 1])
    block = (keep + swap(send, 1, 1)).astype(jnp.bfloat16)
    block = block.reshape(DOCS_DEV, 2, columns // 2).transpose(1, 0, 2).reshape(2 * DOCS_DEV, columns // 2)

    feats = lax.all_to_all(spread(block), "dp", 0, 0).reshape(2 * DOCS, columns // 2)
    scored = score(mine, got, feats)
    rows = queries.shape[0]
    stored = (scored[:rows] + swap(scored[rows:], 1, 1)).astype(jnp.bfloat16)

    blocks = lax.all_to_all(spread(stored), "dp", 0, 0)
    picked = lax.dynamic_slice(blocks, (owner, 0, 0), (1,) + stored.shape, allow_negative_indices=False)
    return picked[0].astype(jnp.float32)


def solution(mesh):
    placed = (
        P("dp", "tensor"),
        P("dp", "tensor"),
        P("tensor", None),
        P("tensor", None),
        P("dp", None),
        P(("dp", "tensor"), None),
        P(),
    )
    return jax.shard_map(
        shards, mesh=mesh, in_specs=placed, out_specs=P(("dp", "tensor"), None), check_vma=False
    )
```

time: 75.4 us -> 67.1 us (0.89)
  blocking collectives: 0 us -> 31.6 us
  waiting for transfers between devices: 35.5 us -> 16.7 us
  starting transfers between devices: 23.8 us -> 9.66 us
  other arithmetic: 2.83 us -> 0.73 us
  Pallas kernels: 8.27 us -> 6.57 us
  local copies, waits for them, and re-layouts: 2.32 us -> 0.72 us
  between operations: 2.09 us -> 0.79 us
    all_to_all x0 -> x2, blocking collectives: none -> 31.6 us  [the longest x1 18.4 us: shards(): lax.all_to_all(spread(block), 'dp', 0, 0).reshape(2 * DOCS, columns // 2)]
    all_to_all x2 -> x0, waiting for transfers between devices: 15.6 us -> none  [the longest x1 9.56 us: shards(): feats = lax.all_to_all(everyone, 'dp', 0, 0).reshape(2 * DOCS, columns // 2)]
    all_to_all x2 -> x0, starting transfers between devices: 13.7 us -> none  [the longest x1 8.82 us: shards(): feats = lax.all_to_all(everyone, 'dp', 0, 0).reshape(2 * DOCS, columns // 2)]
    ppermute x8 -> x6, waiting for transfers between devices: 19.9 us -> 16.7 us  [swap(): lax.ppermute(value, 'tensor', [(i, i ^ (odd if i & 1 else even)) for i in...]
    pallas_call x1 -> x3, Pallas kernels: 6.87 us -> 5.16 us  [the longest x1 5.07 us: project(): pl.pallas_call(project_kernel, in_specs=[pl.BlockSpec(memory_space=pltpu....]
    broadcast_in_dim x2 -> x0, local copies, waits for them, and re-layouts: 1.58 us -> none  [the longest x1 0.85 us: shards(): everyone = jnp.broadcast_to(block, (N_DP,) + block.shape)]
    select_n x3 -> x2, other arithmetic: 1.09 us -> 0.03 us  [pick(): return (jnp.where(first, low, high), jnp.where(first, high, low))]
    add x2, other arithmetic: 1.11 us -> 0.06 us  [the longest x1 0.03 us: shards(): total = keep + swap(send, 1, 1)]
  transfers between devices with their start and end apart: 10 -> 6, of which waited for: 10 -> 6; matrix products, arithmetic and copies ran while one was open for 1% -> 1% of each run, Pallas kernels for 0% -> 0%
where the time goes in v4:
time: 67.1 us; the launch traced here: 66.7 us
  blocking collectives  31.6 us (47%)
  waiting for transfers between devices  16.7 us (25%)
  starting transfers between devices  9.66 us (14%)
  Pallas kernels  6.57 us (10%)
  between operations  0.79 us (1%)
  other arithmetic  0.73 us (1%)
  local copies, waits for them, and re-layouts  0.72 us (1%)
    all_to_all x1, blocking collectives, shards(): lax.all_to_all(spread(block), 'dp', 0, 0).reshape(2 * DOCS, columns // 2)  18.4 us
    ppermute x6, waiting for transfers between devices, swap(): lax.ppermute(value, 'tensor', [(i, i ^ (odd if i & 1 else even)) for i in...  16.7 us
    all_to_all x1, blocking collectives, shards(): blocks = lax.all_to_all(spread(stored), 'dp', 0, 0)  13.2 us
    ppermute x6, starting transfers between devices, swap(): lax.ppermute(value, 'tensor', [(i, i ^ (odd if i & 1 else even)) for i in...  9.66 us
    pallas_call x1, Pallas kernels, project(): pl.pallas_call(project_kernel, in_specs=[pl.BlockSpec(memory_space=pltpu....  5.07 us
  transfers between devices with their start and end apart: 6, of which 6 were waited for; matrix products, arithmetic and copies ran while one was open for 1% of the time, Pallas kernels for 0%

profile of v4, /device:TPU:8, one launch (start us, length us, event | category | flops | bytes accessed | tf_op | source)
XLA Modules:
  0.0 66.7 jit_solution(13802173926452718281)
XLA Ops:
  0.0 0.0 copy-start
  0.0 0.0 copy-start.2
  0.0 0.0 copy-start.1
  0.0 5.1 %project.1 = (f32[512,128]{1,0:T(8,128)S(1)}, f32[512,128]{1,0:T(8,128)S(1)}) custom-call(bf16[1024,1024]{1,0:T(8,128)(2,1)} %out_grads.1, bf16[1024,3584]{1,0:T(8,128)(2,1)} %activations.1, bf16[64,1024]{1,0:T(8,128)(2,1)} %bitcast.31, bf16[64,3584]{1,0:T(8,128)(2,1)} %bitcast.30), custom_call_target="tpu_custom_call" | custom-call | tf_op jit(solution)/shard_map/project/pallas_call | solution.py:76
  5.1 0.1 collective-permute-start
  5.2 1.5 %collective-permute-done = f32[512,128]{1,0:T(8,128)S(1)} collective-permute-done((f32[512,128]{1,0:T(8,128)S(1)}, f32[512,128]{1,0:T(8,128)S(1)}, u32[]{:S(2)}, u32[]{:S(2)}) %collective-permute-start) | collective-permute-done | bytes 262176 | tf_op jit(solution)/shard_map/ppermute | solution.py:18
  6.7 3.4 %collective-permute-start.1 = (f32[512,128]{1,0:T(8,128)S(1)}, f32[512,128]{1,0:T(8,128)S(1)}, u32[]{:S(2)}, u32[]{:S(2)}) collective-permute-start(f32[512,128]{1,0:T(8,128)S(1)} %add.12), channel_id=1, source_target_pairs={{0,2},{1,7},{2,0},{3,5},{4,6},{5,3},{6,4},{7,1},{8,10},{9,15},{10,... | collective-permute-start | bytes 786440 | tf_op jit(solution)/shard_map/ppermute | solution.py:18
  10.1 7.3 %collective-permute-done.1 = f32[512,128]{1,0:T(8,128)S(1)} collective-permute-done((f32[512,128]{1,0:T(8,128)S(1)}, f32[512,128]{1,0:T(8,128)S(1)}, u32[]{:S(2)}, u32[]{:S(2)}) %collective-permute-start.1) | collective-permute-done | bytes 262176 | tf_op jit(solution)/shard_map/ppermute | solution.py:18
  17.4 5.9 %collective-permute-start.2 = (f32[512,128]{1,0:T(8,128)S(1)}, f32[512,128]{1,0:T(8,128)S(1)}, u32[]{:S(2)}, u32[]{:S(2)}) collective-permute-start(f32[512,128]{1,0:T(8,128)S(1)} %add.13.total), channel_id=1, source_target_pairs={{0,6},{1,3},{2,4},{3,1},{4,2},{5,7},{6,0},{7,5},{8,14},{9,11},{10,... | collective-permute-start | bytes 786440 | tf_op jit(solution)/shard_map/ppermute | solution.py:18
  23.3 0.0 copy-done
  23.4 0.1 collective-permute-start.3
  23.5 0.0 copy-done.2
  23.5 0.6 dynamic_slice.6
  24.7 0.0 copy-done.1
  24.7 0.1 collective-permute-done.3.got
  24.8 5.4 %collective-permute-done.2.more = f32[512,128]{1,0:T(8,128)S(1)} collective-permute-done((f32[512,128]{1,0:T(8,128)S(1)}, f32[512,128]{1,0:T(8,128)S(1)}, u32[]{:S(2)}, u32[]{:S(2)}) %collective-permute-start.2) | collective-permute-done | bytes 262176 | tf_op jit(solution)/shard_map/ppermute | solution.py:18
  30.2 0.7 %features.1 = f32[256,64]{1,0:T(8,128)S(1)} custom-call(s32[1,512]{1,0:T(1,128)S(1)} %broadcast_select_fusion.2.ids, f32[512,128]{1,0:T(8,128)S(1)} %add.13.total, f32[512,128]{1,0:T(8,128)S(1)} %collective-permute-done.2.more), custom_call_target="tpu_custom_call" | custom-call | tf_op jit(solution)/shard_map/features/pallas_call | solution.py:105
  31.0 0.1 collective-permute-start.4
  31.1 1.2 %collective-permute-done.4 = f32[4,32,64]{2,1,0:T(8,128)S(1)} collective-permute-done((f32[4,32,64]{2,1,0:T(8,128)S(1)}, f32[4,32,64]{2,1,0:T(8,128)S(1)}, u32[]{:S(2)}, u32[]{:S(2)}) %collective-permute-start.4) | collective-permute-done | bytes 32800 | tf_op jit(solution)/shard_map/ppermute | solution.py:18
  32.3 0.1 reshape.21
  32.5 0.1 spread.2
  32.5 18.4 %all_to_all.10 = bf16[32,8,1024]{2,1,0:T(8,128)(2,1)S(1)} all-to-all(bf16[32,8,1024]{2,1,0:T(8,128)(2,1)S(1)} %spread.2), channel_id=1, replica_groups=mesh['dp'=32,'tensor'=8] {'dp'}, dimensions={0} | all-to-all | bytes 1048576 | tf_op jit(solution)/shard_map/all_to_all | solution.py:175
  50.9 0.7 %score.1 = f32[64,128]{1,0:T(8,128)S(1)} custom-call(bf16[32,2048]{1,0:T(8,128)(2,1)S(1)} %get-tuple-element.13.mine, bf16[32,2048]{1,0:T(8,128)(2,1)S(1)} %collective-permute-done.3.got, bf16[256,1024]{1,0:T(8,128)(2,1)S(1)} %bitcast.27), custom_call_target="tpu_custom_call" | custom-call | tf_op jit(solution)/shard_map/score/pallas_call | solution.py:131
  51.6 0.1 collective-permute-start.5
  51.7 1.2 %collective-permute-done.5 = f32[32,128]{1,0:T(8,128)S(1)} collective-permute-done((f32[32,128]{1,0:T(8,128)S(1)}, f32[32,128]{1,0:T(8,128)S(1)}, u32[]{:S(2)}, u32[]{:S(2)}) %collective-permute-start.5) | collective-permute-done | bytes 16416 | tf_op jit(solution)/shard_map/ppermute | solution.py:18
  52.9 13.2 %all_to_all.11 = bf16[32,32,128]{2,1,0:T(8,128)(2,1)S(1)} all-to-all(bf16[32,32,128]{2,1,0:T(8,128)(2,1)S(1)} %spread.3), channel_id=1, replica_groups=mesh['dp'=32,'tensor'=8] {'dp'}, dimensions={0} | all-to-all | bytes 524288 | tf_op jit(solution)/shard_map/all_to_all | solution.py:180
  66.1 0.6 bitcast_convert_fusion
  (11 shorter events, 0.2 us)
Async XLA Ops:
  0.0 23.3 %copy-start = (bf16[32,4096]{1,0:T(8,128)(2,1)S(1)}, bf16[32,4096]{1,0:T(8,128)(2,1)}, u32[]{:S(2)}) copy-start(bf16[32,4096]{1,0:T(8,128)(2,1)} %param.12) | copy-start | bytes 786436
  0.0 23.5 %copy-start.2 = (s32[32]{0:T(128)S(1)}, s32[32]{0:T(128)}, u32[]{:S(2)}) copy-start(s32[32]{0:T(128)} %param.13) | copy-start | bytes 388
  0.0 24.7 %copy-start.1 = (s32[1,1024]{1,0:T(1,128)S(1)}, s32[1,1024]{1,0:T(1,128)}, u32[]{:S(2)}) copy-start(s32[1,1024]{1,0:T(1,128)} %param.11) | copy-start | bytes 12292
  5.1 1.6 %collective-permute-start = (f32[512,128]{1,0:T(8,128)S(1)}, f32[512,128]{1,0:T(8,128)S(1)}, u32[]{:S(2)}, u32[]{:S(2)}) collective-permute-start(f32[512,128]{1,0:T(8,128)S(1)} %get-tuple-element.12), channel_id=1, source_target_pairs={{0,1},{1,0},{2,3},{3,2},{4,5},{5,4},{6,7},{7,6},{8,9},{9,8},{10,11... | collective-permute-start | bytes 786440 | tf_op jit(solution)/shard_map/ppermute | solution.py:18
  6.7 10.6 %collective-permute-start.1 = (f32[512,128]{1,0:T(8,128)S(1)}, f32[512,128]{1,0:T(8,128)S(1)}, u32[]{:S(2)}, u32[]{:S(2)}) collective-permute-start(f32[512,128]{1,0:T(8,128)S(1)} %add.12), channel_id=1, source_target_pairs={{0,2},{1,7},{2,0},{3,5},{4,6},{5,3},{6,4},{7,1},{8,10},{9,15},{10,... | collective-permute-start | bytes 786440 | tf_op jit(solution)/shard_map/ppermute | solution.py:18
  17.4 12.8 %collective-permute-start.2 = (f32[512,128]{1,0:T(8,128)S(1)}, f32[512,128]{1,0:T(8,128)S(1)}, u32[]{:S(2)}, u32[]{:S(2)}) collective-permute-start(f32[512,128]{1,0:T(8,128)S(1)} %add.13.total), channel_id=1, source_target_pairs={{0,6},{1,3},{2,4},{3,1},{4,2},{5,7},{6,0},{7,5},{8,14},{9,11},{10,... | collective-permute-start | bytes 786440 | tf_op jit(solution)/shard_map/ppermute | solution.py:18
  23.4 1.4 %collective-permute-start.3 = (bf16[32,2048]{1,0:T(8,128)(2,1)S(1)}, bf16[32,2048]{1,0:T(8,128)(2,1)S(1)}, u32[]{:S(2)}, u32[]{:S(2)}) collective-permute-start(bf16[32,2048]{1,0:T(8,128)(2,1)S(1)} %get-tuple-element.17), channel_id=1, source_target_pairs={{0,1},{1,0},{2,3},{3,2},{4,5},{5,4},{6,7},{7,6},{8,9},{9,8},{10,11... | collective-permute-start | bytes 393224 | tf_op jit(solution)/shard_map/ppermute | solution.py:18
  31.0 1.3 %collective-permute-start.4 = (f32[4,32,64]{2,1,0:T(8,128)S(1)}, f32[4,32,64]{2,1,0:T(8,128)S(1)}, u32[]{:S(2)}, u32[]{:S(2)}) collective-permute-start(f32[4,32,64]{2,1,0:T(8,128)S(1)} %select_bitcast_fusion), channel_id=1, source_target_pairs={{0,1},{1,0},{2,3},{3,2},{4,5},{5,4},{6,7},{7,6},{8,9},{9,8},{10,11... | collective-permute-start | bytes 98312 | tf_op jit(solution)/shard_map/ppermute | solution.py:18
  51.6 1.3 %collective-permute-start.5 = (f32[32,128]{1,0:T(8,128)S(1)}, f32[32,128]{1,0:T(8,128)S(1)}, u32[]{:S(2)}, u32[]{:S(2)}) collective-permute-start(f32[32,128]{1,0:T(8,128)S(1)} %slice.35), channel_id=1, source_target_pairs={{0,1},{1,0},{2,3},{3,2},{4,5},{5,4},{6,7},{7,6},{8,9},{9,8},{10,11... | collective-permute-start | bytes 49160 | tf_op jit(solution)/shard_map/ppermute | solution.py:18

commit v5 on v4

v5 whole, which is shorter than its diff:
```python
import jax
import jax.numpy as jnp
from jax import lax
from jax.experimental import pallas as pl
from jax.experimental.pallas import tpu as pltpu
from jax.sharding import PartitionSpec as P

RANK = 64
DOCS_DEV = 4
N_DP = 32
DOCS = N_DP * DOCS_DEV
Y = 4
TOKENS = 1024
STEP = 256
NT = (((1,), (1,)), ((), ()))


def swap(value, even, odd):
    return lax.ppermute(value, "tensor", [(i, i ^ (odd if i & 1 else even)) for i in range(8)])


def pick(first, low, high):
    return jnp.where(first, low, high), jnp.where(first, high, low)


def token_block(ref, block):
    return ref.at[pl.ds(pl.multiple_of(block * STEP, STEP), STEP)]


def project_block(grads, acts, wide_out, wide_in, block, target):
    here = pl.ds(pl.multiple_of(block * STEP, STEP), STEP)
    target[here] = jnp.dot(grads[here], wide_out[...], preferred_element_type=jnp.float32) + jnp.dot(
        acts[here], wide_in[...], preferred_element_type=jnp.float32
    )


def project_sent_kernel(
    out_grads, activations, proj_out, proj_in, send, grads_kept, acts_kept, wide_out, wide_in, grads, acts, raw_out, raw_in, sem
):
    blocks = TOKENS // STEP // 2
    core = lax.axis_index("tensor") & 1

    def copies(half, block, to_grads, to_acts, base):
        return (
            pltpu.make_async_copy(
                token_block(out_grads, half * blocks + block), token_block(to_grads, block), sem.at[base + 2 * block]
            ),
            pltpu.make_async_copy(
                token_block(activations, half * blocks + block), token_block(to_acts, block), sem.at[base + 2 * block + 1]
            ),
        )

    weights = (
        pltpu.make_async_copy(proj_out, raw_out, sem.at[0]),
        pltpu.make_async_copy(proj_in, raw_in, sem.at[1]),
    )
    later = [copy for block in range(blocks) for copy in copies(core, block, grads_kept, acts_kept, 2 + 2 * blocks)]
    for copy in weights:
        copy.start()
    for block in range(blocks):
        for copy in copies(1 - core, block, grads, acts, 2):
            copy.start()
    for copy in later:
        copy.start()
    for copy in weights:
        copy.wait()
    wide_out[...] = jnp.concatenate([raw_out[...], jnp.zeros_like(raw_out)], axis=0).T
    wide_in[...] = jnp.concatenate([jnp.zeros_like(raw_in), raw_in[...]], axis=0).T

    @pl.loop(0, blocks)
    def _(block):
        for copy in copies(1 - core, block, grads, acts, 2):
            copy.wait()
        project_block(grads, acts, wide_out, wide_in, block, send)

    for copy in later:
        copy.wait()


def project_kept_kernel(grads, acts, wide_out, wide_in, keep):
    @pl.loop(0, TOKENS // STEP // 2)
    def _(block):
        project_block(grads, acts, wide_out, wide_in, block, keep)


def project(out_grads, activations, proj_out, proj_in, meanwhile):
    d, ff = out_grads.shape[1], activations.shape[1]
    half = TOKENS // 2
    in_vmem, in_hbm = pl.BlockSpec(memory_space=pltpu.VMEM), pl.BlockSpec(memory_space=pltpu.HBM)
    args = [pltpu.with_memory_space_constraint(x, pltpu.HBM) for x in (out_grads, activations, proj_out, proj_in)]
    send, *rest = pl.pallas_call(
        project_sent_kernel,
        in_specs=[in_hbm] * 4,
        out_specs=[in_vmem] * 5,
        out_shape=[
            pltpu.VMEM((half, 2 * RANK), jnp.float32),
            pltpu.VMEM((half, d), jnp.bfloat16),
            pltpu.VMEM((half, ff), jnp.bfloat16),
            pltpu.VMEM((d, 2 * RANK), jnp.bfloat16),
            pltpu.VMEM((ff, 2 * RANK), jnp.bfloat16),
        ],
        scratch_shapes=[
            pltpu.VMEM((half, d), jnp.bfloat16),
            pltpu.VMEM((half, ff), jnp.bfloat16),
            pltpu.VMEM((RANK, d), jnp.bfloat16),
            pltpu.VMEM((RANK, ff), jnp.bfloat16),
            pltpu.SemaphoreType.DMA((2 + 2 * (TOKENS // STEP),)),
        ],
        compiler_params=pltpu.CompilerParams(vmem_limit_bytes=24 << 20),
        name="project_sent",
    )(*args)
    got = meanwhile(send)
    keep = pl.pallas_call(
        project_kept_kernel,
        in_specs=[in_vmem] * 4,
        out_specs=in_vmem,
        out_shape=pltpu.VMEM((half, 2 * RANK), jnp.float32),
        compiler_params=pltpu.CompilerParams(vmem_limit_bytes=24 << 20),
        cost_estimate=pl.CostEstimate(
            flops=2 * half * (d + ff) * 2 * RANK, bytes_accessed=2 * half * (d + ff), transcendentals=0
        ),
        name="project_kept",
    )(*rest)
    return keep, got


def features_kernel(ids, total, more, feat):
    both = total[...] + more[...]
    out_t = both.T[:RANK]
    weighted = jnp.concatenate([jnp.where(ids[...] == d, out_t, 0.0) for d in range(DOCS_DEV)], axis=0)
    feat[...] = jnp.dot(
        weighted, both[:, RANK:], precision=lax.Precision.HIGHEST, preferred_element_type=jnp.float32
    )


def features(ids, total, more):
    return pl.pallas_call(
        features_kernel,
        out_shape=jax.ShapeDtypeStruct((DOCS_DEV * RANK, RANK), jnp.float32),
        compiler_params=pltpu.CompilerParams(vmem_limit_bytes=16 << 20),
        name="features",
    )(ids, total, more)


def score_kernel(feats, *refs):
    queries, (keep, send, rows) = refs[:-3], refs[-3:]
    half, count = feats.shape[1], feats.shape[0] // 2
    each = queries[0].shape[1]
    here = lax.axis_index("dp") & (Y - 1)
    for step, q in enumerate(queries):
        for h in range(2):
            for core in range(2):
                start = ((2 * h + core) * Y + (here ^ step)) * each
                rows[pl.ds(pl.multiple_of(start, each), each)] = q[core, :, h * half : (h + 1) * half]
    every = lax.dot_general(feats[...], rows[...], NT, preferred_element_type=jnp.float32)
    doc = lax.broadcasted_iota(jnp.int32, (count, 2 * count), 0)
    source = lax.broadcasted_iota(jnp.int32, (count, 2 * count), 1)
    first = (doc >> 2) * 8 + (doc & 3)
    width = rows.shape[0] // 2
    scored = jnp.dot(
        (source == first).astype(jnp.float32), every[:, :width], precision=lax.Precision.HIGHEST,
        preferred_element_type=jnp.float32,
    ) + jnp.dot(
        (source == first + 4).astype(jnp.float32), every[:, width:], precision=lax.Precision.HIGHEST,
        preferred_element_type=jnp.float32,
    )
    keep[...] = scored[:, : width // 2]
    send[...] = scored[:, width // 2 :]


def score(feats, queries):
    out = jax.ShapeDtypeStruct((feats.shape[0] // 2, len(queries) * queries[0].shape[1]), jnp.float32)
    return pl.pallas_call(
        score_kernel,
        out_shape=[out, out],
        scratch_shapes=[pltpu.VMEM((4 * len(queries) * queries[0].shape[1], feats.shape[1]), feats.dtype)],
        compiler_params=pltpu.CompilerParams(vmem_limit_bytes=16 << 20),
        name="score",
    )(feats, *queries)


def place_kernel(owner, blocks, scores, wide):
    lanes, rows = blocks.shape[2], scores.shape[0]
    block = owner[0]
    line = blocks[pl.ds(block & ~(Y - 1), Y)].reshape(DOCS, lanes)
    row = lax.broadcasted_iota(jnp.int32, (DOCS, DOCS), 0)
    column = lax.broadcasted_iota(jnp.int32, (DOCS, DOCS), 1)
    spot = column == ((row >> 2) & 7) * 16 + (row >> 5) * 4 + (row & 3)
    wide[...] = lax.dot_general(
        line, spot.astype(line.dtype), (((0,), (0,)), ((), ())), preferred_element_type=jnp.float32
    )
    scores[...] = wide[pl.ds(pl.multiple_of((block & (Y - 1)) * rows, rows), rows)]


def place(owner, blocks):
    rows = blocks.shape[2] // Y
    return pl.pallas_call(
        place_kernel,
        in_specs=[pl.BlockSpec(memory_space=pltpu.SMEM), pl.BlockSpec(memory_space=pltpu.VMEM)],
        out_specs=pl.BlockSpec(memory_space=pltpu.VMEM),
        out_shape=jax.ShapeDtypeStruct((rows, DOCS), jnp.float32),
        scratch_shapes=[pltpu.VMEM((blocks.shape[2], DOCS), jnp.float32)],
        compiler_params=pltpu.CompilerParams(vmem_limit_bytes=16 << 20),
        name="place",
    )(owner, blocks)


def spread_kernel(block, everyone):
    everyone[...] = jnp.broadcast_to(block[...], everyone.shape)


def spread(block, peers):
    return pl.pallas_call(
        spread_kernel,
        out_specs=pl.BlockSpec(memory_space=pltpu.VMEM),
        out_shape=pltpu.VMEM((peers,) + block.shape, block.dtype),
        compiler_params=pltpu.CompilerParams(vmem_limit_bytes=8 << 20),
        name="spread",
    )(block)


def shards(activations, out_grads, proj_in, proj_out, doc_ids, queries, block_owner):
    core0 = (lax.axis_index("tensor") & 1) == 0
    half = TOKENS // 2
    core0, proj_in = lax.optimization_barrier((core0, proj_in))

    keep, got = project(out_grads, activations, proj_out.T, proj_in.T, lambda send: swap(send, 1, 1))
    total = keep + got
    total = total + swap(total, 2, 6)
    more = swap(total, 6, 2)

    columns = queries.shape[1] // 2
    mine, other = pick(core0, queries[:, :columns], queries[:, columns:])
    lines = [jnp.stack([mine, swap(other, 1, 1)])]
    lines += [lax.ppermute(lines[0], "dp", [(i, i ^ step) for i in range(N_DP)]) for step in range(1, Y)]

    ids = jnp.where(core0, doc_ids[:, :half], doc_ids[:, half:])
    here = lax.axis_index("dp")
    owner = lax.dynamic_slice(block_owner, (here,), (1,), allow_negative_indices=False)
    more, lines, owner = lax.optimization_barrier((more, lines, owner))
    feat = features(ids, total, more).reshape(DOCS_DEV, 2, RANK // 2, RANK)
    keep, send = pick(core0, feat[:, 0], feat[:, 1])
    block = (keep + swap(send, 1, 1)).astype(jnp.bfloat16)
    block = block.reshape(DOCS_DEV, 2, columns // 2).transpose(1, 0, 2).reshape(2 * DOCS_DEV, columns // 2)

    peers = N_DP // Y
    groups = [[g * Y + y for g in range(peers)] for y in range(Y)]
    feats = lax.all_to_all(spread(block, peers), "dp", 0, 0, axis_index_groups=groups)
    keep, send = score(feats.reshape(peers * 2 * DOCS_DEV, columns // 2), lines)
    stored = (keep + swap(send, 1, 1)).astype(jnp.bfloat16)

    return place(owner, lax.all_to_all(spread(stored, N_DP), "dp", 0, 0))


def solution(mesh):
    placed = (
        P("dp", "tensor"),
        P("dp", "tensor"),
        P("tensor", None),
        P("tensor", None),
        P("dp", None),
        P(("dp", "tensor"), None),
        P(),
    )
    return jax.shard_map(
        shards, mesh=mesh, in_specs=placed, out_specs=P(("dp", "tensor"), None), check_vma=False
    )
```

time: 67.1 us -> 60.9 us (0.908)
  blocking collectives: 31.6 us -> 25 us
  waiting for transfers between devices: 16.7 us -> 12.2 us
  starting transfers between devices: 9.66 us -> 13.6 us
  Pallas kernels: 6.57 us -> 8.6 us
    ppermute x6, waiting for transfers between devices: 16.7 us -> 9.45 us  [swap(): lax.ppermute(value, 'tensor', [(i, i ^ (odd if i & 1 else even)) for i in...]
    all_to_all x2, blocking collectives: 31.6 us -> 25 us  [the longest x1 14.2 us: shards(): return place(owner, lax.all_to_all(spread(stored, N_DP), 'dp', 0, 0))]
    ppermute x0 -> x3, starting transfers between devices: none -> 3.58 us  [shards(): lax.ppermute(lines[0], 'dp', [(i, i ^ step) for i in range(N_DP)])]
    ppermute x0 -> x3, waiting for transfers between devices: none -> 2.8 us  [shards(): lax.ppermute(lines[0], 'dp', [(i, i ^ step) for i in range(N_DP)])]
    pallas_call x2 -> x4, Pallas kernels: 5.74 us -> 7.82 us  [the longest x1 4.08 us: project(): pl.pallas_call(project_sent_kernel, in_specs=[in_hbm] * 4, out_specs=[in_...]
  transfers between devices with their start and end apart: 6 -> 9, of which waited for: 6 -> 6; matrix products, arithmetic and copies ran while one was open for 1% -> 1% of each run, Pallas kernels for 0% -> 3%
where the time goes in v5:
time: 60.9 us; the launch traced here: 60.5 us
  blocking collectives  25 us (41%)
  starting transfers between devices  13.6 us (22%)
  waiting for transfers between devices  12.2 us (20%)
  Pallas kernels  8.6 us (14%)
  local copies, waits for them, and re-layouts  0.75 us (1%)
    all_to_all x1, blocking collectives, shards(): return place(owner, lax.all_to_all(spread(stored, N_DP), 'dp', 0, 0))  14.2 us
    all_to_all x1, blocking collectives, shards(): lax.all_to_all(spread(block, peers), 'dp', 0, 0, axis_index_groups=groups)  10.8 us
    ppermute x6, starting transfers between devices, swap(): lax.ppermute(value, 'tensor', [(i, i ^ (odd if i & 1 else even)) for i in...  10 us
    ppermute x6, waiting for transfers between devices, swap(): lax.ppermute(value, 'tensor', [(i, i ^ (odd if i & 1 else even)) for i in...  9.45 us
    pallas_call x1, Pallas kernels, project(): pl.pallas_call(project_sent_kernel, in_specs=[in_hbm] * 4, out_specs=[in_...  4.08 us
    ppermute x3, starting transfers between devices, shards(): lax.ppermute(lines[0], 'dp', [(i, i ^ step) for i in range(N_DP)])  3.58 us
    ppermute x3, waiting for transfers between devices, shards(): lax.ppermute(lines[0], 'dp', [(i, i ^ step) for i in range(N_DP)])  2.8 us
    pallas_call x1, Pallas kernels, project(): pl.pallas_call(project_kept_kernel, in_specs=[in_vmem] * 4, out_specs=in_...  1.53 us
  transfers between devices with their start and end apart: 9, of which 6 were waited for; matrix products, arithmetic and copies ran while one was open for 1% of the time, Pallas kernels for 3%

profile of v5, /device:TPU:8, one launch (start us, length us, event | category | flops | bytes accessed | tf_op | source)
XLA Modules:
  0.0 60.5 jit_solution(9136165648529228560)
XLA Ops:
  0.0 0.0 copy-start
  0.0 4.1 %project_sent.1 = (f32[512,128]{1,0:T(8,128)S(1)}, bf16[512,1024]{1,0:T(8,128)(2,1)S(1)}, bf16[512,3584]{1,0:T(8,128)(2,1)S(1)}, bf16[1024,128]{1,0:T(8,128)(2,1)S(1)}, bf16[3584,128]{1,0:T(8,128)(2,1)S(1)}) custom-call(bf16[1024,1024]{1,0:T(8,128)(2,1)} %out_grads.1, bf16[1024,3584]{1,0:T(8,128)(2,1)} %activations.1, bf16[64,1024]{1,0:T(8,128)(2,1)} %bitcast.30, ...), custom_call_target="tpu_custom_call" | custom-call | tf_op jit(solution)/shard_map/project_sent/pallas_call | solution.py:91
  4.1 0.1 collective-permute-start
  4.2 0.0 copy-done
  4.2 0.6 collective-permute-start.3
  4.8 0.0 copy-start.2
  4.8 0.0 copy-start.1
  4.8 1.5 %project_kept.1 = f32[512,128]{1,0:T(8,128)S(1)} custom-call(bf16[512,1024]{1,0:T(8,128)(2,1)S(1)} %get-tuple-element.21.grads, bf16[512,3584]{1,0:T(8,128)(2,1)S(1)} %get-tuple-element.22.acts, bf16[1024,128]{1,0:T(8,128)(2,1)S(1)} %get-tuple-element.23.wide_out, bf16[3584,128]{1,0:T(8,128)(2,1)S(1)} %get-tuple-element.24.wide_in), custom_call_target="tpu_custom_call" | custom-call | flops 603979776 | bytes 4718592 | tf_op jit(solution)/shard_map/project_kept/pallas_call | solution.py:113
  6.3 0.0 collective-permute-done
  6.4 3.4 %collective-permute-start.1 = (f32[512,128]{1,0:T(8,128)S(1)}, f32[512,128]{1,0:T(8,128)S(1)}, u32[]{:S(2)}, u32[]{:S(2)}) collective-permute-start(f32[512,128]{1,0:T(8,128)S(1)} %add.12), channel_id=1, source_target_pairs={{0,2},{1,7},{2,0},{3,5},{4,6},{5,3},{6,4},{7,1},{8,10},{9,15},{10,... | collective-permute-start | bytes 786440 | tf_op jit(solution)/shard_map/ppermute | solution.py:19
  9.7 0.0 collective-permute-done.3
  9.8 0.5 collective-permute-start.4
  10.3 2.6 %collective-permute-start.5 = (bf16[2,32,2048]{2,1,0:T(8,128)(2,1)S(1)}, bf16[2,32,2048]{2,1,0:T(8,128)(2,1)S(1)}, u32[]{:S(2)}, u32[]{:S(2)}) collective-permute-start(bf16[2,32,2048]{2,1,0:T(8,128)(2,1)S(1)} %pad_maximum_fusion.refs_0_), channel_id=1, source_target_pairs={{0,16},{8,24},{16,0},{24,8},{32,48},{40,56},{48,32},{56,40},{64,80... | collective-permute-start | bytes 786440 | tf_op jit(solution)/shard_map/ppermute | solution.py:235
  12.9 0.4 collective-permute-start.6
  13.4 3.7 %collective-permute-done.1 = f32[512,128]{1,0:T(8,128)S(1)} collective-permute-done((f32[512,128]{1,0:T(8,128)S(1)}, f32[512,128]{1,0:T(8,128)S(1)}, u32[]{:S(2)}, u32[]{:S(2)}) %collective-permute-start.1) | collective-permute-done | bytes 262176 | tf_op jit(solution)/shard_map/ppermute | solution.py:19
  17.0 5.9 %collective-permute-start.2 = (f32[512,128]{1,0:T(8,128)S(1)}, f32[512,128]{1,0:T(8,128)S(1)}, u32[]{:S(2)}, u32[]{:S(2)}) collective-permute-start(f32[512,128]{1,0:T(8,128)S(1)} %add.13.total), channel_id=1, source_target_pairs={{0,6},{1,3},{2,4},{3,1},{4,2},{5,7},{6,0},{7,5},{8,14},{9,11},{10,... | collective-permute-start | bytes 786440 | tf_op jit(solution)/shard_map/ppermute | solution.py:19
  23.0 0.0 copy-done.2
  23.0 0.6 %dynamic_slice.3.owner = s32[1]{0:T(128)} dynamic-slice(s32[32]{0:T(128)S(1)} %copy-done.2, s32[]{:T(128)S(6)} %axis_index.25), dynamic_slice_sizes={1} | dynamic-slice | bytes 12 | tf_op jit(solution)/shard_map/dynamic_slice | solution.py:239
  23.6 0.0 copy-done.1
  23.6 0.0 collective-permute-done.4.refs_1_
  23.6 0.3 collective-permute-done.5.refs_2_
  23.9 2.5 %collective-permute-done.6.refs_3_ = bf16[2,32,2048]{2,1,0:T(8,128)(2,1)S(1)} collective-permute-done((bf16[2,32,2048]{2,1,0:T(8,128)(2,1)S(1)}, bf16[2,32,2048]{2,1,0:T(8,128)(2,1)S(1)}, u32[]{:S(2)}, u32[]{:S(2)}) %collective-permute-start.6) | collective-permute-done | bytes 262176 | tf_op jit(solution)/shard_map/ppermute | solution.py:235
  26.4 3.4 %collective-permute-done.2.more = f32[512,128]{1,0:T(8,128)S(1)} collective-permute-done((f32[512,128]{1,0:T(8,128)S(1)}, f32[512,128]{1,0:T(8,128)S(1)}, u32[]{:S(2)}, u32[]{:S(2)}) %collective-permute-start.2) | collective-permute-done | bytes 262176 | tf_op jit(solution)/shard_map/ppermute | solution.py:19
  29.8 0.7 %features.1 = f32[256,64]{1,0:T(8,128)S(1)} custom-call(s32[1,512]{1,0:T(1,128)S(1)} %broadcast_select_fusion.1.ids, f32[512,128]{1,0:T(8,128)S(1)} %add.13.total, f32[512,128]{1,0:T(8,128)S(1)} %collective-permute-done.2.more), custom_call_target="tpu_custom_call" | custom-call | tf_op jit(solution)/shard_map/features/pallas_call | solution.py:137
  30.5 0.1 collective-permute-start.7
  30.6 1.2 %collective-permute-done.7 = f32[4,32,64]{2,1,0:T(8,128)S(1)} collective-permute-done((f32[4,32,64]{2,1,0:T(8,128)S(1)}, f32[4,32,64]{2,1,0:T(8,128)S(1)}, u32[]{:S(2)}, u32[]{:S(2)}) %collective-permute-start.7) | collective-permute-done | bytes 32800 | tf_op jit(solution)/shard_map/ppermute | solution.py:19
  31.9 0.1 reshape.17
  32.0 10.8 %all_to_all.10 = bf16[8,8,1024]{2,1,0:T(8,128)(2,1)S(1)} all-to-all(bf16[8,8,1024]{2,1,0:T(8,128)(2,1)S(1)} %spread.2), channel_id=1, replica_groups={{0,32,64,96,128,160,192,224},{8,40,72,104,136,168,200,232},{16,48,80,11..., dimensions={0} | all-to-all | bytes 262144 | tf_op jit(solution)/shard_map/all_to_all | solution.py:248
  42.8 0.8 %score.1 = (f32[32,128]{1,0:T(8,128)S(1)}, f32[32,128]{1,0:T(8,128)S(1)}) custom-call(bf16[64,1024]{1,0:T(8,128)(2,1)S(1)} %bitcast.28, bf16[2,32,2048]{2,1,0:T(8,128)(2,1)S(1)} %pad_maximum_fusion.refs_0_, bf16[2,32,2048]{2,1,0:T(8,128)(2,1)S(1)} %collective-permute-done.4.refs_1_, bf16[2,32,2048]{2,1,0:T(8,128)(2,1)S(1)} %collective-permute-done.5.refs_2_, ...), custom_call_target="tpu_custom_call" | custom-call | tf_op jit(solution)/shard_map/score/pallas_call | solution.py:173
  43.6 0.0 collective-permute-start.8
  43.6 1.2 %collective-permute-done.8 = f32[32,128]{1,0:T(8,128)S(1)} collective-permute-done((f32[32,128]{1,0:T(8,128)S(1)}, f32[32,128]{1,0:T(8,128)S(1)}, u32[]{:S(2)}, u32[]{:S(2)}) %collective-permute-start.8) | collective-permute-done | bytes 16416 | tf_op jit(solution)/shard_map/ppermute | solution.py:19
  44.9 14.2 %all_to_all.11.blocks = bf16[32,32,128]{2,1,0:T(8,128)(2,1)S(1)} all-to-all(bf16[32,32,128]{2,1,0:T(8,128)(2,1)S(1)} %spread.3), channel_id=1, replica_groups=mesh['dp'=32,'tensor'=8] {'dp'}, dimensions={0} | all-to-all | bytes 524288 | tf_op jit(solution)/shard_map/all_to_all | solution.py:252
  59.1 1.4 %place.1 = f32[32,128]{1,0:T(8,128)} custom-call(s32[1]{0:T(128)} %dynamic_slice.3.owner, bf16[32,32,128]{2,1,0:T(8,128)(2,1)S(1)} %all_to_all.11.blocks), custom_call_target="tpu_custom_call" | custom-call | tf_op jit(solution)/shard_map/place/pallas_call | solution.py:197
  (12 shorter events, 0.2 us)
Async XLA Ops:
  0.0 4.2 %copy-start = (bf16[32,4096]{1,0:T(8,128)(2,1)S(1)}, bf16[32,4096]{1,0:T(8,128)(2,1)}, u32[]{:S(2)}) copy-start(bf16[32,4096]{1,0:T(8,128)(2,1)} %param.12) | copy-start | bytes 786436
  4.1 2.3 %collective-permute-start = (f32[512,128]{1,0:T(8,128)S(1)}, f32[512,128]{1,0:T(8,128)S(1)}, u32[]{:S(2)}, u32[]{:S(2)}) collective-permute-start(f32[512,128]{1,0:T(8,128)S(1)} %get-tuple-element.25), channel_id=1, source_target_pairs={{0,1},{1,0},{2,3},{3,2},{4,5},{5,4},{6,7},{7,6},{8,9},{9,8},{10,11... | collective-permute-start | bytes 786440 | tf_op jit(solution)/shard_map/ppermute | solution.py:19
  4.2 5.5 %collective-permute-start.3 = (bf16[32,2048]{1,0:T(8,128)(2,1)S(1)}, bf16[32,2048]{1,0:T(8,128)(2,1)S(1)}, u32[]{:S(2)}, u32[]{:S(2)}) collective-permute-start(bf16[32,2048]{1,0:T(8,128)(2,1)S(1)} %get-tuple-element.36), channel_id=1, source_target_pairs={{0,1},{1,0},{2,3},{3,2},{4,5},{5,4},{6,7},{7,6},{8,9},{9,8},{10,11... | collective-permute-start | bytes 393224 | tf_op jit(solution)/shard_map/ppermute | solution.py:19
  4.8 18.2 %copy-start.2 = (s32[32]{0:T(128)S(1)}, s32[32]{0:T(128)}, u32[]{:S(2)}) copy-start(s32[32]{0:T(128)} %param.13) | copy-start | bytes 388
  4.8 18.8 %copy-start.1 = (s32[1,1024]{1,0:T(1,128)S(1)}, s32[1,1024]{1,0:T(1,128)}, u32[]{:S(2)}) copy-start(s32[1,1024]{1,0:T(1,128)} %param.11) | copy-start | bytes 12292
  6.4 10.6 %collective-permute-start.1 = (f32[512,128]{1,0:T(8,128)S(1)}, f32[512,128]{1,0:T(8,128)S(1)}, u32[]{:S(2)}, u32[]{:S(2)}) collective-permute-start(f32[512,128]{1,0:T(8,128)S(1)} %add.12), channel_id=1, source_target_pairs={{0,2},{1,7},{2,0},{3,5},{4,6},{5,3},{6,4},{7,1},{8,10},{9,15},{10,... | collective-permute-start | bytes 786440 | tf_op jit(solution)/shard_map/ppermute | solution.py:19
  9.8 13.8 %collective-permute-start.4 = (bf16[2,32,2048]{2,1,0:T(8,128)(2,1)S(1)}, bf16[2,32,2048]{2,1,0:T(8,128)(2,1)S(1)}, u32[]{:S(2)}, u32[]{:S(2)}) collective-permute-start(bf16[2,32,2048]{2,1,0:T(8,128)(2,1)S(1)} %pad_maximum_fusion.refs_0_), channel_id=1, source_target_pairs={{0,8},{8,0},{16,24},{24,16},{32,40},{40,32},{48,56},{56,48},{64,72... | collective-permute-start | bytes 786440 | tf_op jit(solution)/shard_map/ppermute | solution.py:235
  10.3 13.6 %collective-permute-start.5 = (bf16[2,32,2048]{2,1,0:T(8,128)(2,1)S(1)}, bf16[2,32,2048]{2,1,0:T(8,128)(2,1)S(1)}, u32[]{:S(2)}, u32[]{:S(2)}) collective-permute-start(bf16[2,32,2048]{2,1,0:T(8,128)(2,1)S(1)} %pad_maximum_fusion.refs_0_), channel_id=1, source_target_pairs={{0,16},{8,24},{16,0},{24,8},{32,48},{40,56},{48,32},{56,40},{64,80... | collective-permute-start | bytes 786440 | tf_op jit(solution)/shard_map/ppermute | solution.py:235
  12.9 13.5 %collective-permute-start.6 = (bf16[2,32,2048]{2,1,0:T(8,128)(2,1)S(1)}, bf16[2,32,2048]{2,1,0:T(8,128)(2,1)S(1)}, u32[]{:S(2)}, u32[]{:S(2)}) collective-permute-start(bf16[2,32,2048]{2,1,0:T(8,128)(2,1)S(1)} %pad_maximum_fusion.refs_0_), channel_id=1, source_target_pairs={{0,24},{8,16},{16,8},{24,0},{32,56},{40,48},{48,40},{56,32},{64,88... | collective-permute-start | bytes 786440 | tf_op jit(solution)/shard_map/ppermute | solution.py:235
  17.0 12.7 %collective-permute-start.2 = (f32[512,128]{1,0:T(8,128)S(1)}, f32[512,128]{1,0:T(8,128)S(1)}, u32[]{:S(2)}, u32[]{:S(2)}) collective-permute-start(f32[512,128]{1,0:T(8,128)S(1)} %add.13.total), channel_id=1, source_target_pairs={{0,6},{1,3},{2,4},{3,1},{4,2},{5,7},{6,0},{7,5},{8,14},{9,11},{10,... | collective-permute-start | bytes 786440 | tf_op jit(solution)/shard_map/ppermute | solution.py:19
  30.5 1.3 %collective-permute-start.7 = (f32[4,32,64]{2,1,0:T(8,128)S(1)}, f32[4,32,64]{2,1,0:T(8,128)S(1)}, u32[]{:S(2)}, u32[]{:S(2)}) collective-permute-start(f32[4,32,64]{2,1,0:T(8,128)S(1)} %select_bitcast_fusion.1), channel_id=1, source_target_pairs={{0,1},{1,0},{2,3},{3,2},{4,5},{5,4},{6,7},{7,6},{8,9},{9,8},{10,11... | collective-permute-start | bytes 98312 | tf_op jit(solution)/shard_map/ppermute | solution.py:19
  43.6 1.2 %collective-permute-start.8 = (f32[32,128]{1,0:T(8,128)S(1)}, f32[32,128]{1,0:T(8,128)S(1)}, u32[]{:S(2)}, u32[]{:S(2)}) collective-permute-start(f32[32,128]{1,0:T(8,128)S(1)} %get-tuple-element.34), channel_id=1, source_target_pairs={{0,1},{1,0},{2,3},{3,2},{4,5},{5,4},{6,7},{7,6},{8,9},{9,8},{10,11... | collective-permute-start | bytes 49160 | tf_op jit(solution)/shard_map/ppermute | solution.py:19

commit v6 on v5

--- a/solution.py
+++ b/solution.py
@@ -17,10 +17,6 @@
 
 def swap(value, even, odd):
     return lax.ppermute(value, "tensor", [(i, i ^ (odd if i & 1 else even)) for i in range(8)])
-
-
-def pick(first, low, high):
-    return jnp.where(first, low, high), jnp.where(first, high, low)
 
 
 def token_block(ref, block):
@@ -143,15 +139,14 @@
 
 
 def score_kernel(feats, *refs):
-    queries, (keep, send, rows) = refs[:-3], refs[-3:]
+    queries, (everyone, rows) = refs[:-2], refs[-2:]
     half, count = feats.shape[1], feats.shape[0] // 2
-    each = queries[0].shape[1]
+    each = queries[0].shape[0]
     here = lax.axis_index("dp") & (Y - 1)
     for step, q in enumerate(queries):
         for h in range(2):
-            for core in range(2):
-                start = ((2 * h + core) * Y + (here ^ step)) * each
-                rows[pl.ds(pl.multiple_of(start, each), each)] = q[core, :, h * half : (h + 1) * half]
+            start = (h * Y + (here ^ step)) * each
+            rows[pl.ds(pl.multiple_of(start, each), each)] = q[:, h * half : (h + 1) * half]
     every = lax.dot_general(feats[...], rows[...], NT, preferred_element_type=jnp.float32)
     doc = lax.broadcasted_iota(jnp.int32, (count, 2 * count), 0)
     source = lax.broadcasted_iota(jnp.int32, (count, 2 * count), 1)
@@ -164,45 +159,46 @@
         (source == first + 4).astype(jnp.float32), every[:, width:], precision=lax.Precision.HIGHEST,
         preferred_element_type=jnp.float32,
     )
-    keep[...] = scored[:, : width // 2]
-    send[...] = scored[:, width // 2 :]
+    everyone[...] = jnp.broadcast_to(scored.astype(everyone.dtype), everyone.shape)
 
 
 def score(feats, queries):
-    out = jax.ShapeDtypeStruct((feats.shape[0] // 2, len(queries) * queries[0].shape[1]), jnp.float32)
+    docs, rows = feats.shape[0] // 2, len(queries) * queries[0].shape[0]
     return pl.pallas_call(
         score_kernel,
-        out_shape=[out, out],
-        scratch_shapes=[pltpu.VMEM((4 * len(queries) * queries[0].shape[1], feats.shape[1]), feats.dtype)],
+        out_specs=pl.BlockSpec(memory_space=pltpu.VMEM),
+        out_shape=pltpu.VMEM((N_DP, docs, rows), jnp.bfloat16),
+        scratch_shapes=[pltpu.VMEM((2 * rows, feats.shape[1]), feats.dtype)],
         compiler_params=pltpu.CompilerParams(vmem_limit_bytes=16 << 20),
         name="score",
     )(feats, *queries)
 
 
-def place_kernel(owner, blocks, scores, wide):
+def place_kernel(owners, blocks, scores):
     lanes, rows = blocks.shape[2], scores.shape[0]
-    block = owner[0]
-    line = blocks[pl.ds(block & ~(Y - 1), Y)].reshape(DOCS, lanes)
+    here = lax.broadcasted_iota(jnp.int32, owners.shape, 1) == lax.axis_index("dp")
+    owner = jnp.sum(jnp.where(here, owners[...], 0), axis=1, keepdims=True)
+    line = jnp.zeros((DOCS, lanes), jnp.float32)
+    for first in range(0, N_DP, Y):
+        chosen = (owner & ~(Y - 1)) == first
+        line = line + jnp.where(chosen, blocks[first : first + Y].reshape(DOCS, lanes).astype(jnp.float32), 0.0)
     row = lax.broadcasted_iota(jnp.int32, (DOCS, DOCS), 0)
     column = lax.broadcasted_iota(jnp.int32, (DOCS, DOCS), 1)
     spot = column == ((row >> 2) & 7) * 16 + (row >> 5) * 4 + (row & 3)
-    wide[...] = lax.dot_general(
-        line, spot.astype(line.dtype), (((0,), (0,)), ((), ())), preferred_element_type=jnp.float32
-    )
-    scores[...] = wide[pl.ds(pl.multiple_of((block & (Y - 1)) * rows, rows), rows)]
-
-
-def place(owner, blocks):
-    rows = blocks.shape[2] // Y
+    wide = jnp.dot(line.T.astype(blocks.dtype), spot.astype(blocks.dtype), preferred_element_type=jnp.float32)
+    total = jnp.zeros_like(scores)
+    for y in range(Y):
+        total = total + jnp.where((owner & (Y - 1)) == y, wide[y * rows : (y + 1) * rows], 0.0)
+    scores[...] = total
+
+
+def place(owners, blocks):
     return pl.pallas_call(
         place_kernel,
-        in_specs=[pl.BlockSpec(memory_space=pltpu.SMEM), pl.BlockSpec(memory_space=pltpu.VMEM)],
-        out_specs=pl.BlockSpec(memory_space=pltpu.VMEM),
-        out_shape=jax.ShapeDtypeStruct((rows, DOCS), jnp.float32),
-        scratch_shapes=[pltpu.VMEM((blocks.shape[2], DOCS), jnp.float32)],
+        out_shape=jax.ShapeDtypeStruct((blocks.shape[2] // Y, DOCS), jnp.float32),
         compiler_params=pltpu.CompilerParams(vmem_limit_bytes=16 << 20),
         name="place",
-    )(owner, blocks)
+    )(owners, blocks)
 
 
 def spread_kernel(block, everyone):
@@ -229,27 +225,20 @@
     total = total + swap(total, 2, 6)
     more = swap(total, 6, 2)
 
-    columns = queries.shape[1] // 2
-    mine, other = pick(core0, queries[:, :columns], queries[:, columns:])
-    lines = [jnp.stack([mine, swap(other, 1, 1)])]
-    lines += [lax.ppermute(lines[0], "dp", [(i, i ^ step) for i in range(N_DP)]) for step in range(1, Y)]
+    lines = [queries] + [lax.ppermute(queries, "dp", [(i, i ^ step) for i in range(N_DP)]) for step in range(1, Y)]
 
     ids = jnp.where(core0, doc_ids[:, :half], doc_ids[:, half:])
-    here = lax.axis_index("dp")
-    owner = lax.dynamic_slice(block_owner, (here,), (1,), allow_negative_indices=False)
-    more, lines, owner = lax.optimization_barrier((more, lines, owner))
-    feat = features(ids, total, more).reshape(DOCS_DEV, 2, RANK // 2, RANK)
-    keep, send = pick(core0, feat[:, 0], feat[:, 1])
-    block = (keep + swap(send, 1, 1)).astype(jnp.bfloat16)
-    block = block.reshape(DOCS_DEV, 2, columns // 2).transpose(1, 0, 2).reshape(2 * DOCS_DEV, columns // 2)
+    more, lines = lax.optimization_barrier((more, lines))
+    feat = features(ids, total, more)
+    block = (feat + swap(feat, 1, 1)).astype(jnp.bfloat16)
+    block = block.reshape(DOCS_DEV, 2, RANK * RANK // 2).transpose(1, 0, 2).reshape(2 * DOCS_DEV, RANK * RANK // 2)
 
     peers = N_DP // Y
     groups = [[g * Y + y for g in range(peers)] for y in range(Y)]
     feats = lax.all_to_all(spread(block, peers), "dp", 0, 0, axis_index_groups=groups)
-    keep, send = score(feats.reshape(peers * 2 * DOCS_DEV, columns // 2), lines)
-    stored = (keep + swap(send, 1, 1)).astype(jnp.bfloat16)
-
-    return place(owner, lax.all_to_all(spread(stored, N_DP), "dp", 0, 0))
+    blocks = score(feats.reshape(peers * 2 * DOCS_DEV, RANK * RANK // 2), lines)
+
+    return place(block_owner.reshape(1, N_DP), lax.all_to_all(blocks, "dp", 0, 0))
 
 
 def solution(mesh):

time: 60.9 us -> 59.6 us (0.979)
  blocking collectives: 25 us -> 25.7 us
    all_to_all x1, blocking collectives: 10.8 us -> 11.7 us  [shards(): lax.all_to_all(spread(block, peers), 'dp', 0, 0, axis_index_groups=groups)]
    dynamic_slice x1 -> x0, local copies, waits for them, and re-layouts: 0.62 us -> none  [shards(): lax.dynamic_slice(block_owner, (here,), (1,), allow_negative_indices=False)]
    ppermute x6 -> x4, starting transfers between devices: 10 us -> 9.62 us  [swap(): lax.ppermute(value, 'tensor', [(i, i ^ (odd if i & 1 else even)) for i in...]
    ppermute x6 -> x4, waiting for transfers between devices: 9.45 us -> 9.14 us  [swap(): lax.ppermute(value, 'tensor', [(i, i ^ (odd if i & 1 else even)) for i in...]
  transfers between devices with their start and end apart: 9 -> 7, of which waited for: 6 -> 5; matrix products, arithmetic and copies ran while one was open for 1% -> 0% of each run, Pallas kernels for 3% -> 3%
where the time goes in v6:
time: 59.6 us; the launch traced here: 59.4 us
  blocking collectives  25.7 us (43%)
  starting transfers between devices  13.1 us (22%)
  waiting for transfers between devices  12.1 us (20%)
  Pallas kernels  8.08 us (14%)
    all_to_all x1, blocking collectives, shards(): lax.all_to_all(blocks, 'dp', 0, 0)  14 us
    all_to_all x1, blocking collectives, shards(): lax.all_to_all(spread(block, peers), 'dp', 0, 0, axis_index_groups=groups)  11.7 us
    ppermute x4, starting transfers between devices, swap(): lax.ppermute(value, 'tensor', [(i, i ^ (odd if i & 1 else even)) for i in...  9.62 us
    ppermute x4, waiting for transfers between devices, swap(): lax.ppermute(value, 'tensor', [(i, i ^ (odd if i & 1 else even)) for i in...  9.14 us
    pallas_call x1, Pallas kernels, project(): pl.pallas_call(project_sent_kernel, in_specs=[in_hbm] * 4, out_specs=[in_...  4.04 us
    ppermute x3, starting transfers between devices, shards(): lax.ppermute(queries, 'dp', [(i, i ^ step) for i in range(N_DP)])  3.49 us
    ppermute x3, waiting for transfers between devices, shards(): lax.ppermute(queries, 'dp', [(i, i ^ step) for i in range(N_DP)])  3 us
    pallas_call x1, Pallas kernels, project(): pl.pallas_call(project_kept_kernel, in_specs=[in_vmem] * 4, out_specs=in_...  1.53 us
  transfers between devices with their start and end apart: 7, of which 5 were waited for; matrix products, arithmetic and copies ran while one was open for 0% of the time, Pallas kernels for 3%

profile of v6, /device:TPU:8, one launch (start us, length us, event | category | flops | bytes accessed | tf_op | source)
XLA Modules:
  0.0 59.4 jit_solution(18317245700502091711)
XLA Ops:
  0.0 4.0 %project_sent.1 = (f32[512,128]{1,0:T(8,128)S(1)}, bf16[512,1024]{1,0:T(8,128)(2,1)S(1)}, bf16[512,3584]{1,0:T(8,128)(2,1)S(1)}, bf16[1024,128]{1,0:T(8,128)(2,1)S(1)}, bf16[3584,128]{1,0:T(8,128)(2,1)S(1)}) custom-call(bf16[1024,1024]{1,0:T(8,128)(2,1)} %out_grads.1, bf16[1024,3584]{1,0:T(8,128)(2,1)} %activations.1, bf16[64,1024]{1,0:T(8,128)(2,1)} %bitcast.8, ...), custom_call_target="tpu_custom_call" | custom-call | tf_op jit(solution)/shard_map/project_sent/pallas_call | solution.py:87
  4.1 0.0 copy-start
  4.1 0.1 collective-permute-start
  4.2 0.0 copy-start.2
  4.2 1.5 %project_kept.1 = f32[512,128]{1,0:T(8,128)S(1)} custom-call(bf16[512,1024]{1,0:T(8,128)(2,1)S(1)} %get-tuple-element.19.grads, bf16[512,3584]{1,0:T(8,128)(2,1)S(1)} %get-tuple-element.20.acts, bf16[1024,128]{1,0:T(8,128)(2,1)S(1)} %get-tuple-element.21.wide_out, bf16[3584,128]{1,0:T(8,128)(2,1)S(1)} %get-tuple-element.22.wide_in), custom_call_target="tpu_custom_call" | custom-call | flops 603979776 | bytes 4718592 | tf_op jit(solution)/shard_map/project_kept/pallas_call | solution.py:109
  5.7 0.0 copy-start.1
  5.7 0.0 collective-permute-done
  5.8 3.4 %collective-permute-start.1 = (f32[512,128]{1,0:T(8,128)S(1)}, f32[512,128]{1,0:T(8,128)S(1)}, u32[]{:S(2)}, u32[]{:S(2)}) collective-permute-start(f32[512,128]{1,0:T(8,128)S(1)} %add.9), channel_id=1, source_target_pairs={{0,2},{1,7},{2,0},{3,5},{4,6},{5,3},{6,4},{7,1},{8,10},{9,15},{10,... | collective-permute-start | bytes 786440 | tf_op jit(solution)/shard_map/ppermute | solution.py:19
  9.1 0.0 copy-done
  9.1 0.4 collective-permute-start.3
  9.6 2.6 %collective-permute-start.4 = (bf16[32,4096]{1,0:T(8,128)(2,1)S(1)}, bf16[32,4096]{1,0:T(8,128)(2,1)S(1)}, u32[]{:S(2)}, u32[]{:S(2)}) collective-permute-start(bf16[32,4096]{1,0:T(8,128)(2,1)S(1)} %copy-done), channel_id=1, source_target_pairs={{0,16},{8,24},{16,0},{24,8},{32,48},{40,56},{48,32},{56,40},{64,80... | collective-permute-start | bytes 786440 | tf_op jit(solution)/shard_map/ppermute | solution.py:228
  12.2 0.4 collective-permute-start.5
  12.6 3.7 %collective-permute-done.1 = f32[512,128]{1,0:T(8,128)S(1)} collective-permute-done((f32[512,128]{1,0:T(8,128)S(1)}, f32[512,128]{1,0:T(8,128)S(1)}, u32[]{:S(2)}, u32[]{:S(2)}) %collective-permute-start.1) | collective-permute-done | bytes 262176 | tf_op jit(solution)/shard_map/ppermute | solution.py:19
  16.3 6.1 %collective-permute-start.2 = (f32[512,128]{1,0:T(8,128)S(1)}, f32[512,128]{1,0:T(8,128)S(1)}, u32[]{:S(2)}, u32[]{:S(2)}) collective-permute-start(f32[512,128]{1,0:T(8,128)S(1)} %add.10.total), channel_id=1, source_target_pairs={{0,6},{1,3},{2,4},{3,1},{4,2},{5,7},{6,0},{7,5},{8,14},{9,11},{10,... | collective-permute-start | bytes 786440 | tf_op jit(solution)/shard_map/ppermute | solution.py:19
  22.4 0.0 copy-done.2
  22.4 0.0 collective-permute-done.3.refs_1_
  22.4 0.3 collective-permute-done.4.refs_2_
  22.7 2.7 %collective-permute-done.5.refs_3_ = bf16[32,4096]{1,0:T(8,128)(2,1)S(1)} collective-permute-done((bf16[32,4096]{1,0:T(8,128)(2,1)S(1)}, bf16[32,4096]{1,0:T(8,128)(2,1)S(1)}, u32[]{:S(2)}, u32[]{:S(2)}) %collective-permute-start.5) | collective-permute-done | bytes 262176 | tf_op jit(solution)/shard_map/ppermute | solution.py:228
  25.4 4.1 %collective-permute-done.2.more = f32[512,128]{1,0:T(8,128)S(1)} collective-permute-done((f32[512,128]{1,0:T(8,128)S(1)}, f32[512,128]{1,0:T(8,128)S(1)}, u32[]{:S(2)}, u32[]{:S(2)}) %collective-permute-start.2) | collective-permute-done | bytes 262176 | tf_op jit(solution)/shard_map/ppermute | solution.py:19
  29.6 0.7 %features.1 = f32[256,64]{1,0:T(8,128)S(1)} custom-call(s32[1,512]{1,0:T(1,128)S(1)} %broadcast_select_fusion.ids, f32[512,128]{1,0:T(8,128)S(1)} %add.10.total, f32[512,128]{1,0:T(8,128)S(1)} %collective-permute-done.2.more), custom_call_target="tpu_custom_call" | custom-call | tf_op jit(solution)/shard_map/features/pallas_call | solution.py:133
  30.3 0.1 collective-permute-start.6
  30.4 1.3 %collective-permute-done.6 = f32[256,64]{1,0:T(8,128)S(1)} collective-permute-done((f32[256,64]{1,0:T(8,128)S(1)}, f32[256,64]{1,0:T(8,128)S(1)}, u32[]{:S(2)}, u32[]{:S(2)}) %collective-permute-start.6) | collective-permute-done | bytes 65568 | tf_op jit(solution)/shard_map/ppermute | solution.py:19
  31.8 0.1 reshape.13
  31.9 11.7 %all_to_all.10 = bf16[8,8,2048]{2,1,0:T(8,128)(2,1)S(1)} all-to-all(bf16[8,8,2048]{2,1,0:T(8,128)(2,1)S(1)} %spread.1), channel_id=1, replica_groups={{0,32,64,96,128,160,192,224},{8,40,72,104,136,168,200,232},{16,48,80,11..., dimensions={0} | all-to-all | bytes 524288 | tf_op jit(solution)/shard_map/all_to_all | solution.py:238
  43.6 0.8 %score.1 = bf16[32,32,128]{2,1,0:T(8,128)(2,1)S(1)} custom-call(bf16[64,2048]{1,0:T(8,128)(2,1)S(1)} %bitcast.5, bf16[32,4096]{1,0:T(8,128)(2,1)S(1)} %copy-done, bf16[32,4096]{1,0:T(8,128)(2,1)S(1)} %collective-permute-done.3.refs_1_, bf16[32,4096]{1,0:T(8,128)(2,1)S(1)} %collective-permute-done.4.refs_2_, bf16[32,4096]{1,0:T(8,128)(2,1)S(1)} %collective-permute-done.5.refs_3_), custom_call_target="tpu_custom_call" | custom-call | tf_op jit(solution)/shard_map/score/pallas_call | solution.py:167
  44.5 14.0 %all_to_all.11.blocks = bf16[32,32,128]{2,1,0:T(8,128)(2,1)S(1)} all-to-all(bf16[32,32,128]{2,1,0:T(8,128)(2,1)S(1)} %score.1), channel_id=1, replica_groups=mesh['dp'=32,'tensor'=8] {'dp'}, dimensions={0} | all-to-all | bytes 524288 | tf_op jit(solution)/shard_map/all_to_all | solution.py:241
  58.5 0.0 copy-done.1
  58.5 0.9 %place.1 = f32[32,128]{1,0:T(8,128)} custom-call(s32[1,32]{1,0:T(1,128)S(1)} %bitcast.6, bf16[32,32,128]{2,1,0:T(8,128)(2,1)S(1)} %all_to_all.11.blocks), custom_call_target="tpu_custom_call" | custom-call | tf_op jit(solution)/shard_map/place/pallas_call | solution.py:196
  (7 shorter events, 0.1 us)
Async XLA Ops:
  4.1 5.1 %copy-start = (bf16[32,4096]{1,0:T(8,128)(2,1)S(1)}, bf16[32,4096]{1,0:T(8,128)(2,1)}, u32[]{:S(2)}) copy-start(bf16[32,4096]{1,0:T(8,128)(2,1)} %refs_0_) | copy-start | bytes 786436
  4.1 1.7 %collective-permute-start = (f32[512,128]{1,0:T(8,128)S(1)}, f32[512,128]{1,0:T(8,128)S(1)}, u32[]{:S(2)}, u32[]{:S(2)}) collective-permute-start(f32[512,128]{1,0:T(8,128)S(1)} %get-tuple-element.23), channel_id=1, source_target_pairs={{0,1},{1,0},{2,3},{3,2},{4,5},{5,4},{6,7},{7,6},{8,9},{9,8},{10,11... | collective-permute-start | bytes 786440 | tf_op jit(solution)/shard_map/ppermute | solution.py:19
  4.2 18.2 %copy-start.2 = (s32[1,1024]{1,0:T(1,128)S(1)}, s32[1,1024]{1,0:T(1,128)}, u32[]{:S(2)}) copy-start(s32[1,1024]{1,0:T(1,128)} %param.11) | copy-start | bytes 12292
  5.7 52.8 %copy-start.1 = (s32[32]{0:T(128)S(1)}, s32[32]{0:T(128)}, u32[]{:S(2)}) copy-start(s32[32]{0:T(128)} %param.13) | copy-start | bytes 388
  5.8 10.5 %collective-permute-start.1 = (f32[512,128]{1,0:T(8,128)S(1)}, f32[512,128]{1,0:T(8,128)S(1)}, u32[]{:S(2)}, u32[]{:S(2)}) collective-permute-start(f32[512,128]{1,0:T(8,128)S(1)} %add.9), channel_id=1, source_target_pairs={{0,2},{1,7},{2,0},{3,5},{4,6},{5,3},{6,4},{7,1},{8,10},{9,15},{10,... | collective-permute-start | bytes 786440 | tf_op jit(solution)/shard_map/ppermute | solution.py:19
  9.1 13.3 %collective-permute-start.3 = (bf16[32,4096]{1,0:T(8,128)(2,1)S(1)}, bf16[32,4096]{1,0:T(8,128)(2,1)S(1)}, u32[]{:S(2)}, u32[]{:S(2)}) collective-permute-start(bf16[32,4096]{1,0:T(8,128)(2,1)S(1)} %copy-done), channel_id=1, source_target_pairs={{0,8},{8,0},{16,24},{24,16},{32,40},{40,32},{48,56},{56,48},{64,72... | collective-permute-start | bytes 786440 | tf_op jit(solution)/shard_map/ppermute | solution.py:228
  9.6 13.1 %collective-permute-start.4 = (bf16[32,4096]{1,0:T(8,128)(2,1)S(1)}, bf16[32,4096]{1,0:T(8,128)(2,1)S(1)}, u32[]{:S(2)}, u32[]{:S(2)}) collective-permute-start(bf16[32,4096]{1,0:T(8,128)(2,1)S(1)} %copy-done), channel_id=1, source_target_pairs={{0,16},{8,24},{16,0},{24,8},{32,48},{40,56},{48,32},{56,40},{64,80... | collective-permute-start | bytes 786440 | tf_op jit(solution)/shard_map/ppermute | solution.py:228
  12.2 13.2 %collective-permute-start.5 = (bf16[32,4096]{1,0:T(8,128)(2,1)S(1)}, bf16[32,4096]{1,0:T(8,128)(2,1)S(1)}, u32[]{:S(2)}, u32[]{:S(2)}) collective-permute-start(bf16[32,4096]{1,0:T(8,128)(2,1)S(1)} %copy-done), channel_id=1, source_target_pairs={{0,24},{8,16},{16,8},{24,0},{32,56},{40,48},{48,40},{56,32},{64,88... | collective-permute-start | bytes 786440 | tf_op jit(solution)/shard_map/ppermute | solution.py:228
  16.3 13.2 %collective-permute-start.2 = (f32[512,128]{1,0:T(8,128)S(1)}, f32[512,128]{1,0:T(8,128)S(1)}, u32[]{:S(2)}, u32[]{:S(2)}) collective-permute-start(f32[512,128]{1,0:T(8,128)S(1)} %add.10.total), channel_id=1, source_target_pairs={{0,6},{1,3},{2,4},{3,1},{4,2},{5,7},{6,0},{7,5},{8,14},{9,11},{10,... | collective-permute-start | bytes 786440 | tf_op jit(solution)/shard_map/ppermute | solution.py:19
  30.3 1.4 %collective-permute-start.6 = (f32[256,64]{1,0:T(8,128)S(1)}, f32[256,64]{1,0:T(8,128)S(1)}, u32[]{:S(2)}, u32[]{:S(2)}) collective-permute-start(f32[256,64]{1,0:T(8,128)S(1)} %features.1), channel_id=1, source_target_pairs={{0,1},{1,0},{2,3},{3,2},{4,5},{5,4},{6,7},{7,6},{8,9},{9,8},{10,11... | collective-permute-start | bytes 196616 | tf_op jit(solution)/shard_map/ppermute | solution.py:19

commit v7 on v6

--- a/solution.py
+++ b/solution.py
@@ -23,60 +23,67 @@
     return ref.at[pl.ds(pl.multiple_of(block * STEP, STEP), STEP)]
 
 
-def project_block(grads, acts, wide_out, wide_in, block, target):
+def project_block(grads, acts, wide_out, wide_in, block, target, place):
     here = pl.ds(pl.multiple_of(block * STEP, STEP), STEP)
-    target[here] = jnp.dot(grads[here], wide_out[...], preferred_element_type=jnp.float32) + jnp.dot(
+    there = pl.ds(pl.multiple_of(place * STEP, STEP), STEP)
+    target[there] = jnp.dot(grads[here], wide_out[...], preferred_element_type=jnp.float32) + jnp.dot(
         acts[here], wide_in[...], preferred_element_type=jnp.float32
     )
 
 
-def project_sent_kernel(
-    out_grads, activations, proj_out, proj_in, send, grads_kept, acts_kept, wide_out, wide_in, grads, acts, raw_out, raw_in, sem
+def project_early_kernel(
+    out_grads, activations, proj_out, proj_in, send, first, grads_last, acts_last, wide_out, wide_in, grads, acts, raw_out, raw_in, sem
 ):
-    blocks = TOKENS // STEP // 2
+    blocks = TOKENS // STEP
+    half = blocks // 2
     core = lax.axis_index("tensor") & 1
 
-    def copies(half, block, to_grads, to_acts, base):
+    def copies(block, to_grads, to_acts, place):
+        which = jnp.where(block < half, (1 - core) * half, core * half - half) + block
         return (
-            pltpu.make_async_copy(
-                token_block(out_grads, half * blocks + block), token_block(to_grads, block), sem.at[base + 2 * block]
-            ),
-            pltpu.make_async_copy(
-                token_block(activations, half * blocks + block), token_block(to_acts, block), sem.at[base + 2 * block + 1]
-            ),
+            pltpu.make_async_copy(token_block(out_grads, which), token_block(to_grads, place), sem.at[2 + 2 * block]),
+            pltpu.make_async_copy(token_block(activations, which), token_block(to_acts, place), sem.at[3 + 2 * block]),
         )
 
     weights = (
         pltpu.make_async_copy(proj_out, raw_out, sem.at[0]),
         pltpu.make_async_copy(proj_in, raw_in, sem.at[1]),
     )
-    later = [copy for block in range(blocks) for copy in copies(core, block, grads_kept, acts_kept, 2 + 2 * blocks)]
+    last = copies(blocks - 1, grads_last, acts_last, 0)
     for copy in weights:
         copy.start()
-    for block in range(blocks):
-        for copy in copies(1 - core, block, grads, acts, 2):
+    for block in range(blocks - 1):
+        for copy in copies(block, grads, acts, block):
             copy.start()
-    for copy in later:
+    for copy in last:
         copy.start()
     for copy in weights:
         copy.wait()
     wide_out[...] = jnp.concatenate([raw_out[...], jnp.zeros_like(raw_out)], axis=0).T
     wide_in[...] = jnp.concatenate([jnp.zeros_like(raw_in), raw_in[...]], axis=0).T
 
-    @pl.loop(0, blocks)
+    @pl.loop(0, half)
     def _(block):
-        for copy in copies(1 - core, block, grads, acts, 2):
+        for copy in copies(block, grads, acts, block):
             copy.wait()
-        project_block(grads, acts, wide_out, wide_in, block, send)
-
-    for copy in later:
+        project_block(grads, acts, wide_out, wide_in, block, send, block)
+
+    @pl.loop(half, blocks - 1)
+    def _(block):
+        for copy in copies(block, grads, acts, block):
+            copy.wait()
+        project_block(grads, acts, wide_out, wide_in, block, first, block - half)
+
+    for copy in last:
         copy.wait()
 
 
-def project_kept_kernel(grads, acts, wide_out, wide_in, keep):
-    @pl.loop(0, TOKENS // STEP // 2)
+def project_late_kernel(first, grads, acts, wide_out, wide_in, keep):
+    keep[: first.shape[0]] = first[...]
+
+    @pl.loop(0, 1)
     def _(block):
-        project_block(grads, acts, wide_out, wide_in, block, keep)
+        project_block(grads, acts, wide_out, wide_in, block, keep, block + first.shape[0] // STEP)
 
 
 def project(out_grads, activations, proj_out, proj_in, meanwhile):
@@ -85,37 +92,38 @@
     in_vmem, in_hbm = pl.BlockSpec(memory_space=pltpu.VMEM), pl.BlockSpec(memory_space=pltpu.HBM)
     args = [pltpu.with_memory_space_constraint(x, pltpu.HBM) for x in (out_grads, activations, proj_out, proj_in)]
     send, *rest = pl.pallas_call(
-        project_sent_kernel,
+        project_early_kernel,
         in_specs=[in_hbm] * 4,
-        out_specs=[in_vmem] * 5,
+        out_specs=[in_vmem] * 6,
         out_shape=[
             pltpu.VMEM((half, 2 * RANK), jnp.float32),
-            pltpu.VMEM((half, d), jnp.bfloat16),
-            pltpu.VMEM((half, ff), jnp.bfloat16),
+            pltpu.VMEM((half - STEP, 2 * RANK), jnp.float32),
+            pltpu.VMEM((STEP, d), jnp.bfloat16),
+            pltpu.VMEM((STEP, ff), jnp.bfloat16),
             pltpu.VMEM((d, 2 * RANK), jnp.bfloat16),
             pltpu.VMEM((ff, 2 * RANK), jnp.bfloat16),
         ],
         scratch_shapes=[
-            pltpu.VMEM((half, d), jnp.bfloat16),
-            pltpu.VMEM((half, ff), jnp.bfloat16),
+            pltpu.VMEM((TOKENS - STEP, d), jnp.bfloat16),
+            pltpu.VMEM((TOKENS - STEP, ff), jnp.bfloat16),
             pltpu.VMEM((RANK, d), jnp.bfloat16),
             pltpu.VMEM((RANK, ff), jnp.bfloat16),
             pltpu.SemaphoreType.DMA((2 + 2 * (TOKENS // STEP),)),
         ],
         compiler_params=pltpu.CompilerParams(vmem_limit_bytes=24 << 20),
-        name="project_sent",
+        name="project_early",
     )(*args)
     got = meanwhile(send)
     keep = pl.pallas_call(
-        project_kept_kernel,
-        in_specs=[in_vmem] * 4,
+        project_late_kernel,
+        in_specs=[in_vmem] * 5,
         out_specs=in_vmem,
         out_shape=pltpu.VMEM((half, 2 * RANK), jnp.float32),
         compiler_params=pltpu.CompilerParams(vmem_limit_bytes=24 << 20),
         cost_estimate=pl.CostEstimate(
             flops=2 * half * (d + ff) * 2 * RANK, bytes_accessed=2 * half * (d + ff), transcendentals=0
         ),
-        name="project_kept",
+        name="project_late",
     )(*rest)
     return keep, got
 
@@ -138,7 +146,7 @@
     )(ids, total, more)
 
 
-def score_kernel(feats, *refs):
+def score_kernel(owners, feats, *refs):
     queries, (everyone, rows) = refs[:-2], refs[-2:]
     half, count = feats.shape[1], feats.shape[0] // 2
     each = queries[0].shape[0]
@@ -159,43 +167,59 @@
         (source == first + 4).astype(jnp.float32), every[:, width:], precision=lax.Precision.HIGHEST,
         preferred_element_type=jnp.float32,
     )
-    everyone[...] = jnp.broadcast_to(scored.astype(everyone.dtype), everyone.shape)
-
-
-def score(feats, queries):
-    docs, rows = feats.shape[0] // 2, len(queries) * queries[0].shape[0]
+    scored = scored.astype(everyone.dtype).astype(jnp.float32)
+    tiles = [scored[8 * x : 8 * x + 8] for x in range(count // 8)]
+    lane = lax.broadcasted_iota(jnp.int32, tiles[0].shape, 1) >> 5
+    packed = []
+    for y in range(Y):
+        total = jnp.zeros_like(tiles[0])
+        for x, tile in enumerate(tiles):
+            shift = (x - y) % Y * each
+            total = jnp.where(lane == x, pltpu.roll(tile, shift, 1) if shift else tile, total)
+        packed.append(total)
+    for peer in range(N_DP):
+        y = owners[:, peer : peer + 1] & (Y - 1)
+        chosen = jnp.where(y < 2, jnp.where(y == 0, packed[0], packed[1]), jnp.where(y == 2, packed[2], packed[3]))
+        everyone[peer] = chosen.astype(everyone.dtype)
+
+
+def score(owners, feats, queries):
+    rows = len(queries) * queries[0].shape[0]
     return pl.pallas_call(
         score_kernel,
         out_specs=pl.BlockSpec(memory_space=pltpu.VMEM),
-        out_shape=pltpu.VMEM((N_DP, docs, rows), jnp.bfloat16),
+        out_shape=pltpu.VMEM((N_DP, 8, 128), jnp.bfloat16),
         scratch_shapes=[pltpu.VMEM((2 * rows, feats.shape[1]), feats.dtype)],
         compiler_params=pltpu.CompilerParams(vmem_limit_bytes=16 << 20),
         name="score",
-    )(feats, *queries)
+    )(owners, feats, *queries)
 
 
 def place_kernel(owners, blocks, scores):
-    lanes, rows = blocks.shape[2], scores.shape[0]
+    rows = scores.shape[0]
     here = lax.broadcasted_iota(jnp.int32, owners.shape, 1) == lax.axis_index("dp")
     owner = jnp.sum(jnp.where(here, owners[...], 0), axis=1, keepdims=True)
-    line = jnp.zeros((DOCS, lanes), jnp.float32)
+    line = jnp.zeros((Y * 8, blocks.shape[2]), jnp.float32)
     for first in range(0, N_DP, Y):
         chosen = (owner & ~(Y - 1)) == first
-        line = line + jnp.where(chosen, blocks[first : first + Y].reshape(DOCS, lanes).astype(jnp.float32), 0.0)
-    row = lax.broadcasted_iota(jnp.int32, (DOCS, DOCS), 0)
-    column = lax.broadcasted_iota(jnp.int32, (DOCS, DOCS), 1)
-    spot = column == ((row >> 2) & 7) * 16 + (row >> 5) * 4 + (row & 3)
-    wide = jnp.dot(line.T.astype(blocks.dtype), spot.astype(blocks.dtype), preferred_element_type=jnp.float32)
+        line = line + jnp.where(chosen, blocks[first : first + Y].astype(jnp.float32).reshape(line.shape), 0.0)
+    line = line.T.astype(blocks.dtype)
+    row = lax.broadcasted_iota(jnp.int32, (Y * 8, DOCS), 0)
+    column = lax.broadcasted_iota(jnp.int32, (Y * 8, DOCS), 1)
+    spot = ((row >> 2) & 1) * 16 + (row >> 3) * 4 + (row & 3)
     total = jnp.zeros_like(scores)
-    for y in range(Y):
-        total = total + jnp.where((owner & (Y - 1)) == y, wide[y * rows : (y + 1) * rows], 0.0)
+    for x in range(DOCS // 32):
+        total = total + jnp.dot(
+            line[x * rows : (x + 1) * rows], (column == spot + 32 * x).astype(line.dtype),
+            preferred_element_type=jnp.float32,
+        )
     scores[...] = total
 
 
 def place(owners, blocks):
     return pl.pallas_call(
         place_kernel,
-        out_shape=jax.ShapeDtypeStruct((blocks.shape[2] // Y, DOCS), jnp.float32),
+        out_shape=jax.ShapeDtypeStruct((32, DOCS), jnp.float32),
         compiler_params=pltpu.CompilerParams(vmem_limit_bytes=16 << 20),
         name="place",
     )(owners, blocks)
@@ -236,9 +260,10 @@
     peers = N_DP // Y
     groups = [[g * Y + y for g in range(peers)] for y in range(Y)]
     feats = lax.all_to_all(spread(block, peers), "dp", 0, 0, axis_index_groups=groups)
-    blocks = score(feats.reshape(peers * 2 * DOCS_DEV, RANK * RANK // 2), lines)
-
-    return place(block_owner.reshape(1, N_DP), lax.all_to_all(blocks, "dp", 0, 0))
+    owners = block_owner.reshape(1, N_DP)
+    blocks = score(owners, feats.reshape(peers * 2 * DOCS_DEV, RANK * RANK // 2), lines)
+
+    return place(owners, lax.all_to_all(blocks, "dp", 0, 0))
 
 
 def solution(mesh):

time: 59.6 us -> 58.6 us (0.983)
  blocking collectives: 25.7 us -> 24.8 us
  waiting for transfers between devices: 12.1 us -> 12.7 us
    all_to_all x1, blocking collectives: 14 us -> 13.1 us  [shards(): return place(owners, lax.all_to_all(blocks, 'dp', 0, 0))]
  transfers between devices with their start and end apart: 7 -> 7, of which waited for: 5 -> 6; matrix products, arithmetic and copies ran while one was open for 0% -> 0% of each run, Pallas kernels for 3% -> 1%
where the time goes in v7:
time: 58.6 us; the launch traced here: 58.4 us
  blocking collectives  24.8 us (42%)
  starting transfers between devices  13 us (22%)
  waiting for transfers between devices  12.7 us (22%)
  Pallas kernels  7.61 us (13%)
    all_to_all x1, blocking collectives, shards(): return place(owners, lax.all_to_all(blocks, 'dp', 0, 0))  13.1 us
    all_to_all x1, blocking collectives, shards(): lax.all_to_all(spread(block, peers), 'dp', 0, 0, axis_index_groups=groups)  11.7 us
    ppermute x4, waiting for transfers between devices, swap(): lax.ppermute(value, 'tensor', [(i, i ^ (odd if i & 1 else even)) for i in...  9.51 us
    ppermute x4, starting transfers between devices, swap(): lax.ppermute(value, 'tensor', [(i, i ^ (odd if i & 1 else even)) for i in...  9.48 us
    pallas_call x1, Pallas kernels, project(): pl.pallas_call(project_early_kernel, in_specs=[in_hbm] * 4, out_specs=[in...  4.26 us
    ppermute x3, starting transfers between devices, shards(): lax.ppermute(queries, 'dp', [(i, i ^ step) for i in range(N_DP)])  3.49 us
    ppermute x3, waiting for transfers between devices, shards(): lax.ppermute(queries, 'dp', [(i, i ^ step) for i in range(N_DP)])  3.19 us
  transfers between devices with their start and end apart: 7, of which 6 were waited for; matrix products, arithmetic and copies ran while one was open for 0% of the time, Pallas kernels for 1%

profile of v7, /device:TPU:8, one launch (start us, length us, event | category | flops | bytes accessed | tf_op | source)
XLA Modules:
  0.0 58.4 jit_solution(7406382125328762844)
XLA Ops:
  0.0 4.3 %project_early.1 = (f32[512,128]{1,0:T(8,128)S(1)}, f32[256,128]{1,0:T(8,128)S(1)}, bf16[256,1024]{1,0:T(8,128)(2,1)S(1)}, bf16[256,3584]{1,0:T(8,128)(2,1)S(1)}...) custom-call(bf16[1024,1024]{1,0:T(8,128)(2,1)} %out_grads.1, bf16[1024,3584]{1,0:T(8,128)(2,1)} %activations.1, ...), custom_call_target="tpu_custom_call" | custom-call | tf_op jit(solution)/shard_map/project_early/pallas_call | solution.py:94
  4.3 0.1 collective-permute-start
  4.4 0.0 copy-start
  4.4 0.0 copy-start.2
  4.4 0.8 %project_late.1 = f32[512,128]{1,0:T(8,128)S(1)} custom-call(f32[256,128]{1,0:T(8,128)S(1)} %get-tuple-element.20.first, bf16[256,1024]{1,0:T(8,128)(2,1)S(1)} %get-tuple-element.21.grads, bf16[256,3584]{1,0:T(8,128)(2,1)S(1)} %get-tuple-element.22.acts, bf16[1024,128]{1,0:T(8,128)(2,1)S(1)} %get-tuple-element.23.wide_out, ...), custom_call_target="tpu_custom_call" | custom-call | flops 603979776 | bytes 4718592 | tf_op jit(solution)/shard_map/project_late/pallas_call | solution.py:117
  5.2 0.0 copy-start.1
  5.2 0.7 %collective-permute-done = f32[512,128]{1,0:T(8,128)S(1)} collective-permute-done((f32[512,128]{1,0:T(8,128)S(1)}, f32[512,128]{1,0:T(8,128)S(1)}, u32[]{:S(2)}, u32[]{:S(2)}) %collective-permute-start) | collective-permute-done | bytes 262176 | tf_op jit(solution)/shard_map/ppermute | solution.py:19
  5.9 3.4 %collective-permute-start.1 = (f32[512,128]{1,0:T(8,128)S(1)}, f32[512,128]{1,0:T(8,128)S(1)}, u32[]{:S(2)}, u32[]{:S(2)}) collective-permute-start(f32[512,128]{1,0:T(8,128)S(1)} %add.9), channel_id=1, source_target_pairs={{0,2},{1,7},{2,0},{3,5},{4,6},{5,3},{6,4},{7,1},{8,10},{9,15},{10,... | collective-permute-start | bytes 786440 | tf_op jit(solution)/shard_map/ppermute | solution.py:19
  9.3 0.0 copy-done
  9.3 0.4 collective-permute-start.3
  9.7 2.6 %collective-permute-start.4 = (bf16[32,4096]{1,0:T(8,128)(2,1)S(1)}, bf16[32,4096]{1,0:T(8,128)(2,1)S(1)}, u32[]{:S(2)}, u32[]{:S(2)}) collective-permute-start(bf16[32,4096]{1,0:T(8,128)(2,1)S(1)} %copy-done), channel_id=1, source_target_pairs={{0,16},{8,24},{16,0},{24,8},{32,48},{40,56},{48,32},{56,40},{64,80... | collective-permute-start | bytes 786440 | tf_op jit(solution)/shard_map/ppermute | solution.py:252
  12.3 0.5 collective-permute-start.5
  12.8 3.8 %collective-permute-done.1 = f32[512,128]{1,0:T(8,128)S(1)} collective-permute-done((f32[512,128]{1,0:T(8,128)S(1)}, f32[512,128]{1,0:T(8,128)S(1)}, u32[]{:S(2)}, u32[]{:S(2)}) %collective-permute-start.1) | collective-permute-done | bytes 262176 | tf_op jit(solution)/shard_map/ppermute | solution.py:19
  16.6 5.9 %collective-permute-start.2 = (f32[512,128]{1,0:T(8,128)S(1)}, f32[512,128]{1,0:T(8,128)S(1)}, u32[]{:S(2)}, u32[]{:S(2)}) collective-permute-start(f32[512,128]{1,0:T(8,128)S(1)} %add.10.total), channel_id=1, source_target_pairs={{0,6},{1,3},{2,4},{3,1},{4,2},{5,7},{6,0},{7,5},{8,14},{9,11},{10,... | collective-permute-start | bytes 786440 | tf_op jit(solution)/shard_map/ppermute | solution.py:19
  22.5 0.0 copy-done.2
  22.5 0.0 collective-permute-done.3.refs_1_
  22.5 0.7 %collective-permute-done.4.refs_2_ = bf16[32,4096]{1,0:T(8,128)(2,1)S(1)} collective-permute-done((bf16[32,4096]{1,0:T(8,128)(2,1)S(1)}, bf16[32,4096]{1,0:T(8,128)(2,1)S(1)}, u32[]{:S(2)}, u32[]{:S(2)}) %collective-permute-start.4) | collective-permute-done | bytes 262176 | tf_op jit(solution)/shard_map/ppermute | solution.py:252
  23.2 2.5 %collective-permute-done.5.refs_3_ = bf16[32,4096]{1,0:T(8,128)(2,1)S(1)} collective-permute-done((bf16[32,4096]{1,0:T(8,128)(2,1)S(1)}, bf16[32,4096]{1,0:T(8,128)(2,1)S(1)}, u32[]{:S(2)}, u32[]{:S(2)}) %collective-permute-start.5) | collective-permute-done | bytes 262176 | tf_op jit(solution)/shard_map/ppermute | solution.py:252
  25.7 3.7 %collective-permute-done.2.more = f32[512,128]{1,0:T(8,128)S(1)} collective-permute-done((f32[512,128]{1,0:T(8,128)S(1)}, f32[512,128]{1,0:T(8,128)S(1)}, u32[]{:S(2)}, u32[]{:S(2)}) %collective-permute-start.2) | collective-permute-done | bytes 262176 | tf_op jit(solution)/shard_map/ppermute | solution.py:19
  29.4 0.7 %features.1 = f32[256,64]{1,0:T(8,128)S(1)} custom-call(s32[1,512]{1,0:T(1,128)S(1)} %broadcast_select_fusion.ids, f32[512,128]{1,0:T(8,128)S(1)} %add.10.total, f32[512,128]{1,0:T(8,128)S(1)} %collective-permute-done.2.more), custom_call_target="tpu_custom_call" | custom-call | tf_op jit(solution)/shard_map/features/pallas_call | solution.py:141
  30.2 0.1 collective-permute-start.6
  30.3 1.3 %collective-permute-done.6 = f32[256,64]{1,0:T(8,128)S(1)} collective-permute-done((f32[256,64]{1,0:T(8,128)S(1)}, f32[256,64]{1,0:T(8,128)S(1)}, u32[]{:S(2)}, u32[]{:S(2)}) %collective-permute-start.6) | collective-permute-done | bytes 65568 | tf_op jit(solution)/shard_map/ppermute | solution.py:19
  31.6 0.1 reshape.13
  31.8 11.7 %all_to_all.10 = bf16[8,8,2048]{2,1,0:T(8,128)(2,1)S(1)} all-to-all(bf16[8,8,2048]{2,1,0:T(8,128)(2,1)S(1)} %spread.1), channel_id=1, replica_groups={{0,32,64,96,128,160,192,224},{8,40,72,104,136,168,200,232},{16,48,80,11..., dimensions={0} | all-to-all | bytes 524288 | tf_op jit(solution)/shard_map/all_to_all | solution.py:262
  43.5 0.0 copy-done.1
  43.5 0.9 %score.1 = bf16[32,8,128]{2,1,0:T(8,128)(2,1)S(1)} custom-call(s32[1,32]{1,0:T(1,128)S(1)} %bitcast.6, bf16[64,2048]{1,0:T(8,128)(2,1)S(1)} %bitcast.5, bf16[32,4096]{1,0:T(8,128)(2,1)S(1)} %copy-done, bf16[32,4096]{1,0:T(8,128)(2,1)S(1)} %collective-permute-done.3.refs_1_, bf16[32,4096]{1,0:T(8,128)(2,1)S(1)} %collective-permute-done.4.refs_2_, ...), custom_call_target="tpu_custom_call" | custom-call | tf_op jit(solution)/shard_map/score/pallas_call | solution.py:188
  44.4 13.1 %all_to_all.11.blocks = bf16[32,8,128]{2,1,0:T(8,128)(2,1)S(1)} all-to-all(bf16[32,8,128]{2,1,0:T(8,128)(2,1)S(1)} %score.1), channel_id=1, replica_groups=mesh['dp'=32,'tensor'=8] {'dp'}, dimensions={0} | all-to-all | bytes 131072 | tf_op jit(solution)/shard_map/all_to_all | solution.py:266
  57.5 0.9 %place.1 = f32[32,128]{1,0:T(8,128)} custom-call(s32[1,32]{1,0:T(1,128)S(1)} %bitcast.7, bf16[32,8,128]{2,1,0:T(8,128)(2,1)S(1)} %all_to_all.11.blocks), custom_call_target="tpu_custom_call" | custom-call | tf_op jit(solution)/shard_map/place/pallas_call | solution.py:220
  (7 shorter events, 0.1 us)
Async XLA Ops:
  4.3 1.6 %collective-permute-start = (f32[512,128]{1,0:T(8,128)S(1)}, f32[512,128]{1,0:T(8,128)S(1)}, u32[]{:S(2)}, u32[]{:S(2)}) collective-permute-start(f32[512,128]{1,0:T(8,128)S(1)} %get-tuple-element.25), channel_id=1, source_target_pairs={{0,1},{1,0},{2,3},{3,2},{4,5},{5,4},{6,7},{7,6},{8,9},{9,8},{10,11... | collective-permute-start | bytes 786440 | tf_op jit(solution)/shard_map/ppermute | solution.py:19
  4.4 4.9 %copy-start = (bf16[32,4096]{1,0:T(8,128)(2,1)S(1)}, bf16[32,4096]{1,0:T(8,128)(2,1)}, u32[]{:S(2)}) copy-start(bf16[32,4096]{1,0:T(8,128)(2,1)} %refs_0_) | copy-start | bytes 786436
  4.4 18.1 %copy-start.2 = (s32[1,1024]{1,0:T(1,128)S(1)}, s32[1,1024]{1,0:T(1,128)}, u32[]{:S(2)}) copy-start(s32[1,1024]{1,0:T(1,128)} %param.11) | copy-start | bytes 12292
  5.2 38.3 %copy-start.1 = (s32[32]{0:T(128)S(1)}, s32[32]{0:T(128)}, u32[]{:S(2)}) copy-start(s32[32]{0:T(128)} %param.13) | copy-start | bytes 388
  5.9 10.6 %collective-permute-start.1 = (f32[512,128]{1,0:T(8,128)S(1)}, f32[512,128]{1,0:T(8,128)S(1)}, u32[]{:S(2)}, u32[]{:S(2)}) collective-permute-start(f32[512,128]{1,0:T(8,128)S(1)} %add.9), channel_id=1, source_target_pairs={{0,2},{1,7},{2,0},{3,5},{4,6},{5,3},{6,4},{7,1},{8,10},{9,15},{10,... | collective-permute-start | bytes 786440 | tf_op jit(solution)/shard_map/ppermute | solution.py:19
  9.3 13.2 %collective-permute-start.3 = (bf16[32,4096]{1,0:T(8,128)(2,1)S(1)}, bf16[32,4096]{1,0:T(8,128)(2,1)S(1)}, u32[]{:S(2)}, u32[]{:S(2)}) collective-permute-start(bf16[32,4096]{1,0:T(8,128)(2,1)S(1)} %copy-done), channel_id=1, source_target_pairs={{0,8},{8,0},{16,24},{24,16},{32,40},{40,32},{48,56},{56,48},{64,72... | collective-permute-start | bytes 786440 | tf_op jit(solution)/shard_map/ppermute | solution.py:252
  9.7 13.5 %collective-permute-start.4 = (bf16[32,4096]{1,0:T(8,128)(2,1)S(1)}, bf16[32,4096]{1,0:T(8,128)(2,1)S(1)}, u32[]{:S(2)}, u32[]{:S(2)}) collective-permute-start(bf16[32,4096]{1,0:T(8,128)(2,1)S(1)} %copy-done), channel_id=1, source_target_pairs={{0,16},{8,24},{16,0},{24,8},{32,48},{40,56},{48,32},{56,40},{64,80... | collective-permute-start | bytes 786440 | tf_op jit(solution)/shard_map/ppermute | solution.py:252
  12.3 13.4 %collective-permute-start.5 = (bf16[32,4096]{1,0:T(8,128)(2,1)S(1)}, bf16[32,4096]{1,0:T(8,128)(2,1)S(1)}, u32[]{:S(2)}, u32[]{:S(2)}) collective-permute-start(bf16[32,4096]{1,0:T(8,128)(2,1)S(1)} %copy-done), channel_id=1, source_target_pairs={{0,24},{8,16},{16,8},{24,0},{32,56},{40,48},{48,40},{56,32},{64,88... | collective-permute-start | bytes 786440 | tf_op jit(solution)/shard_map/ppermute | solution.py:252
  16.6 12.8 %collective-permute-start.2 = (f32[512,128]{1,0:T(8,128)S(1)}, f32[512,128]{1,0:T(8,128)S(1)}, u32[]{:S(2)}, u32[]{:S(2)}) collective-permute-start(f32[512,128]{1,0:T(8,128)S(1)} %add.10.total), channel_id=1, source_target_pairs={{0,6},{1,3},{2,4},{3,1},{4,2},{5,7},{6,0},{7,5},{8,14},{9,11},{10,... | collective-permute-start | bytes 786440 | tf_op jit(solution)/shard_map/ppermute | solution.py:19
  30.2 1.4 %collective-permute-start.6 = (f32[256,64]{1,0:T(8,128)S(1)}, f32[256,64]{1,0:T(8,128)S(1)}, u32[]{:S(2)}, u32[]{:S(2)}) collective-permute-start(f32[256,64]{1,0:T(8,128)S(1)} %features.1), channel_id=1, source_target_pairs={{0,1},{1,0},{2,3},{3,2},{4,5},{5,4},{6,7},{7,6},{8,9},{9,8},{10,11... | collective-permute-start | bytes 196616 | tf_op jit(solution)/shard_map/ppermute | solution.py:19

commit v8 on v7

--- a/solution.py
+++ b/solution.py
@@ -128,13 +128,27 @@
     return keep, got
 
 
+def thirds(value):
+    high = value.astype(jnp.bfloat16)
+    rest = value - high.astype(jnp.float32)
+    middle = rest.astype(jnp.bfloat16)
+    return high, middle, (rest - middle.astype(jnp.float32)).astype(jnp.bfloat16)
+
+
 def features_kernel(ids, total, more, feat):
-    both = total[...] + more[...]
-    out_t = both.T[:RANK]
-    weighted = jnp.concatenate([jnp.where(ids[...] == d, out_t, 0.0) for d in range(DOCS_DEV)], axis=0)
-    feat[...] = jnp.dot(
-        weighted, both[:, RANK:], precision=lax.Precision.HIGHEST, preferred_element_type=jnp.float32
-    )
+    parts = thirds(total[...] + more[...])
+    right = jnp.concatenate([part[:, RANK:] for part in parts], axis=1)
+
+    def by_document(part):
+        out_t = part.T[:RANK]
+        return jnp.concatenate([jnp.where(ids[...] == d, out_t, jnp.zeros_like(out_t)) for d in range(DOCS_DEV)], axis=0)
+
+    high, middle, low = [
+        jnp.dot(by_document(part), right[:, : (3 - i) * RANK], preferred_element_type=jnp.float32)
+        for i, part in enumerate(parts)
+    ]
+    least = (low + high[:, 2 * RANK :]) + middle[:, RANK:]
+    feat[...] = least + ((middle[:, :RANK] + high[:, RANK : 2 * RANK]) + high[:, :RANK])
 
 
 def features(ids, total, more):
@@ -156,17 +170,16 @@
             start = (h * Y + (here ^ step)) * each
             rows[pl.ds(pl.multiple_of(start, each), each)] = q[:, h * half : (h + 1) * half]
     every = lax.dot_general(feats[...], rows[...], NT, preferred_element_type=jnp.float32)
-    doc = lax.broadcasted_iota(jnp.int32, (count, 2 * count), 0)
-    source = lax.broadcasted_iota(jnp.int32, (count, 2 * count), 1)
+    width = rows.shape[0] // 2
+    halves = jnp.concatenate([every[:, :width], every[:, width:]], axis=0)
+    doc = lax.broadcasted_iota(jnp.int32, (count, 4 * count), 0)
+    source = lax.broadcasted_iota(jnp.int32, (count, 4 * count), 1)
     first = (doc >> 2) * 8 + (doc & 3)
-    width = rows.shape[0] // 2
+    spot = (source == first) | (source == first + 2 * count + 4)
     scored = jnp.dot(
-        (source == first).astype(jnp.float32), every[:, :width], precision=lax.Precision.HIGHEST,
-        preferred_element_type=jnp.float32,
-    ) + jnp.dot(
-        (source == first + 4).astype(jnp.float32), every[:, width:], precision=lax.Precision.HIGHEST,
-        preferred_element_type=jnp.float32,
-    )
+        spot.astype(feats.dtype), jnp.concatenate(thirds(halves), axis=1), preferred_element_type=jnp.float32
+    )
+    scored = (scored[:, 2 * width :] + scored[:, width : 2 * width]) + scored[:, :width]
     scored = scored.astype(everyone.dtype).astype(jnp.float32)
     tiles = [scored[8 * x : 8 * x + 8] for x in range(count // 8)]
     lane = lax.broadcasted_iota(jnp.int32, tiles[0].shape, 1) >> 5

time: 58.6 us -> 58.2 us (level)
  no operation moved by 1% of the time
where the time goes in v8:
time: 58.2 us; the launch traced here: 58 us
  blocking collectives  24.8 us (43%)
  starting transfers between devices  13 us (22%)
  waiting for transfers between devices  12.7 us (22%)
  Pallas kernels  7.22 us (12%)
    all_to_all x1, blocking collectives, shards(): return place(owners, lax.all_to_all(blocks, 'dp', 0, 0))  13.1 us
    all_to_all x1, blocking collectives, shards(): lax.all_to_all(spread(block, peers), 'dp', 0, 0, axis_index_groups=groups)  11.7 us
    ppermute x4, waiting for transfers between devices, swap(): lax.ppermute(value, 'tensor', [(i, i ^ (odd if i & 1 else even)) for i in...  9.51 us
    ppermute x4, starting transfers between devices, swap(): lax.ppermute(value, 'tensor', [(i, i ^ (odd if i & 1 else even)) for i in...  9.48 us
    pallas_call x1, Pallas kernels, project(): pl.pallas_call(project_early_kernel, in_specs=[in_hbm] * 4, out_specs=[in...  4.26 us
    ppermute x3, starting transfers between devices, shards(): lax.ppermute(queries, 'dp', [(i, i ^ step) for i in range(N_DP)])  3.49 us
    ppermute x3, waiting for transfers between devices, shards(): lax.ppermute(queries, 'dp', [(i, i ^ step) for i in range(N_DP)])  3.19 us
  transfers between devices with their start and end apart: 7, of which 6 were waited for; matrix products, arithmetic and copies ran while one was open for 0% of the time, Pallas kernels for 1%

profile of v8, /device:TPU:8, one launch (start us, length us, event | category | flops | bytes accessed | tf_op | source)
XLA Modules:
  0.0 58.0 jit_solution(12245310448476391475)
XLA Ops:
  0.0 4.3 %project_early.1 = (f32[512,128]{1,0:T(8,128)S(1)}, f32[256,128]{1,0:T(8,128)S(1)}, bf16[256,1024]{1,0:T(8,128)(2,1)S(1)}, bf16[256,3584]{1,0:T(8,128)(2,1)S(1)}...) custom-call(bf16[1024,1024]{1,0:T(8,128)(2,1)} %out_grads.1, bf16[1024,3584]{1,0:T(8,128)(2,1)} %activations.1, ...), custom_call_target="tpu_custom_call" | custom-call | tf_op jit(solution)/shard_map/project_early/pallas_call | solution.py:94
  4.3 0.1 collective-permute-start
  4.4 0.0 copy-start
  4.4 0.0 copy-start.2
  4.4 0.8 %project_late.1 = f32[512,128]{1,0:T(8,128)S(1)} custom-call(f32[256,128]{1,0:T(8,128)S(1)} %get-tuple-element.20.first, bf16[256,1024]{1,0:T(8,128)(2,1)S(1)} %get-tuple-element.21.grads, bf16[256,3584]{1,0:T(8,128)(2,1)S(1)} %get-tuple-element.22.acts, bf16[1024,128]{1,0:T(8,128)(2,1)S(1)} %get-tuple-element.23.wide_out, ...), custom_call_target="tpu_custom_call" | custom-call | flops 603979776 | bytes 4718592 | tf_op jit(solution)/shard_map/project_late/pallas_call | solution.py:117
  5.2 0.0 copy-start.1
  5.2 0.7 %collective-permute-done = f32[512,128]{1,0:T(8,128)S(1)} collective-permute-done((f32[512,128]{1,0:T(8,128)S(1)}, f32[512,128]{1,0:T(8,128)S(1)}, u32[]{:S(2)}, u32[]{:S(2)}) %collective-permute-start) | collective-permute-done | bytes 262176 | tf_op jit(solution)/shard_map/ppermute | solution.py:19
  5.9 3.4 %collective-permute-start.1 = (f32[512,128]{1,0:T(8,128)S(1)}, f32[512,128]{1,0:T(8,128)S(1)}, u32[]{:S(2)}, u32[]{:S(2)}) collective-permute-start(f32[512,128]{1,0:T(8,128)S(1)} %add.9), channel_id=1, source_target_pairs={{0,2},{1,7},{2,0},{3,5},{4,6},{5,3},{6,4},{7,1},{8,10},{9,15},{10,... | collective-permute-start | bytes 786440 | tf_op jit(solution)/shard_map/ppermute | solution.py:19
  9.3 0.0 copy-done
  9.3 0.4 collective-permute-start.3
  9.7 2.6 %collective-permute-start.4 = (bf16[32,4096]{1,0:T(8,128)(2,1)S(1)}, bf16[32,4096]{1,0:T(8,128)(2,1)S(1)}, u32[]{:S(2)}, u32[]{:S(2)}) collective-permute-start(bf16[32,4096]{1,0:T(8,128)(2,1)S(1)} %copy-done), channel_id=1, source_target_pairs={{0,16},{8,24},{16,0},{24,8},{32,48},{40,56},{48,32},{56,40},{64,80... | collective-permute-start | bytes 786440 | tf_op jit(solution)/shard_map/ppermute | solution.py:265
  12.3 0.5 collective-permute-start.5
  12.8 3.8 %collective-permute-done.1 = f32[512,128]{1,0:T(8,128)S(1)} collective-permute-done((f32[512,128]{1,0:T(8,128)S(1)}, f32[512,128]{1,0:T(8,128)S(1)}, u32[]{:S(2)}, u32[]{:S(2)}) %collective-permute-start.1) | collective-permute-done | bytes 262176 | tf_op jit(solution)/shard_map/ppermute | solution.py:19
  16.6 5.9 %collective-permute-start.2 = (f32[512,128]{1,0:T(8,128)S(1)}, f32[512,128]{1,0:T(8,128)S(1)}, u32[]{:S(2)}, u32[]{:S(2)}) collective-permute-start(f32[512,128]{1,0:T(8,128)S(1)} %add.10.total), channel_id=1, source_target_pairs={{0,6},{1,3},{2,4},{3,1},{4,2},{5,7},{6,0},{7,5},{8,14},{9,11},{10,... | collective-permute-start | bytes 786440 | tf_op jit(solution)/shard_map/ppermute | solution.py:19
  22.5 0.0 copy-done.2
  22.5 0.0 collective-permute-done.3.refs_1_
  22.5 0.7 %collective-permute-done.4.refs_2_ = bf16[32,4096]{1,0:T(8,128)(2,1)S(1)} collective-permute-done((bf16[32,4096]{1,0:T(8,128)(2,1)S(1)}, bf16[32,4096]{1,0:T(8,128)(2,1)S(1)}, u32[]{:S(2)}, u32[]{:S(2)}) %collective-permute-start.4) | collective-permute-done | bytes 262176 | tf_op jit(solution)/shard_map/ppermute | solution.py:265
  23.2 2.5 %collective-permute-done.5.refs_3_ = bf16[32,4096]{1,0:T(8,128)(2,1)S(1)} collective-permute-done((bf16[32,4096]{1,0:T(8,128)(2,1)S(1)}, bf16[32,4096]{1,0:T(8,128)(2,1)S(1)}, u32[]{:S(2)}, u32[]{:S(2)}) %collective-permute-start.5) | collective-permute-done | bytes 262176 | tf_op jit(solution)/shard_map/ppermute | solution.py:265
  25.7 3.7 %collective-permute-done.2.more = f32[512,128]{1,0:T(8,128)S(1)} collective-permute-done((f32[512,128]{1,0:T(8,128)S(1)}, f32[512,128]{1,0:T(8,128)S(1)}, u32[]{:S(2)}, u32[]{:S(2)}) %collective-permute-start.2) | collective-permute-done | bytes 262176 | tf_op jit(solution)/shard_map/ppermute | solution.py:19
  29.4 0.5 features.1
  29.9 0.1 collective-permute-start.6
  30.0 1.3 %collective-permute-done.6 = f32[256,64]{1,0:T(8,128)S(1)} collective-permute-done((f32[256,64]{1,0:T(8,128)S(1)}, f32[256,64]{1,0:T(8,128)S(1)}, u32[]{:S(2)}, u32[]{:S(2)}) %collective-permute-start.6) | collective-permute-done | bytes 65568 | tf_op jit(solution)/shard_map/ppermute | solution.py:19
  31.4 0.1 reshape.13
  31.5 11.7 %all_to_all.10 = bf16[8,8,2048]{2,1,0:T(8,128)(2,1)S(1)} all-to-all(bf16[8,8,2048]{2,1,0:T(8,128)(2,1)S(1)} %spread.1), channel_id=1, replica_groups={{0,32,64,96,128,160,192,224},{8,40,72,104,136,168,200,232},{16,48,80,11..., dimensions={0} | all-to-all | bytes 524288 | tf_op jit(solution)/shard_map/all_to_all | solution.py:275
  43.2 0.0 copy-done.1
  43.2 0.8 %score.1 = bf16[32,8,128]{2,1,0:T(8,128)(2,1)S(1)} custom-call(s32[1,32]{1,0:T(1,128)S(1)} %bitcast.6, bf16[64,2048]{1,0:T(8,128)(2,1)S(1)} %bitcast.5, bf16[32,4096]{1,0:T(8,128)(2,1)S(1)} %copy-done, bf16[32,4096]{1,0:T(8,128)(2,1)S(1)} %collective-permute-done.3.refs_1_, bf16[32,4096]{1,0:T(8,128)(2,1)S(1)} %collective-permute-done.4.refs_2_, ...), custom_call_target="tpu_custom_call" | custom-call | tf_op jit(solution)/shard_map/score/pallas_call | solution.py:201
  44.0 13.1 %all_to_all.11.blocks = bf16[32,8,128]{2,1,0:T(8,128)(2,1)S(1)} all-to-all(bf16[32,8,128]{2,1,0:T(8,128)(2,1)S(1)} %score.1), channel_id=1, replica_groups=mesh['dp'=32,'tensor'=8] {'dp'}, dimensions={0} | all-to-all | bytes 131072 | tf_op jit(solution)/shard_map/all_to_all | solution.py:279
  57.1 0.9 %place.1 = f32[32,128]{1,0:T(8,128)} custom-call(s32[1,32]{1,0:T(1,128)S(1)} %bitcast.7, bf16[32,8,128]{2,1,0:T(8,128)(2,1)S(1)} %all_to_all.11.blocks), custom_call_target="tpu_custom_call" | custom-call | tf_op jit(solution)/shard_map/place/pallas_call | solution.py:233
  (7 shorter events, 0.1 us)
Async XLA Ops:
  4.3 1.6 %collective-permute-start = (f32[512,128]{1,0:T(8,128)S(1)}, f32[512,128]{1,0:T(8,128)S(1)}, u32[]{:S(2)}, u32[]{:S(2)}) collective-permute-start(f32[512,128]{1,0:T(8,128)S(1)} %get-tuple-element.25), channel_id=1, source_target_pairs={{0,1},{1,0},{2,3},{3,2},{4,5},{5,4},{6,7},{7,6},{8,9},{9,8},{10,11... | collective-permute-start | bytes 786440 | tf_op jit(solution)/shard_map/ppermute | solution.py:19
  4.4 4.9 %copy-start = (bf16[32,4096]{1,0:T(8,128)(2,1)S(1)}, bf16[32,4096]{1,0:T(8,128)(2,1)}, u32[]{:S(2)}) copy-start(bf16[32,4096]{1,0:T(8,128)(2,1)} %refs_0_) | copy-start | bytes 786436
  4.4 18.1 %copy-start.2 = (s32[1,1024]{1,0:T(1,128)S(1)}, s32[1,1024]{1,0:T(1,128)}, u32[]{:S(2)}) copy-start(s32[1,1024]{1,0:T(1,128)} %param.11) | copy-start | bytes 12292
  5.2 38.1 %copy-start.1 = (s32[32]{0:T(128)S(1)}, s32[32]{0:T(128)}, u32[]{:S(2)}) copy-start(s32[32]{0:T(128)} %param.13) | copy-start | bytes 388
  5.9 10.6 %collective-permute-start.1 = (f32[512,128]{1,0:T(8,128)S(1)}, f32[512,128]{1,0:T(8,128)S(1)}, u32[]{:S(2)}, u32[]{:S(2)}) collective-permute-start(f32[512,128]{1,0:T(8,128)S(1)} %add.9), channel_id=1, source_target_pairs={{0,2},{1,7},{2,0},{3,5},{4,6},{5,3},{6,4},{7,1},{8,10},{9,15},{10,... | collective-permute-start | bytes 786440 | tf_op jit(solution)/shard_map/ppermute | solution.py:19
  9.3 13.2 %collective-permute-start.3 = (bf16[32,4096]{1,0:T(8,128)(2,1)S(1)}, bf16[32,4096]{1,0:T(8,128)(2,1)S(1)}, u32[]{:S(2)}, u32[]{:S(2)}) collective-permute-start(bf16[32,4096]{1,0:T(8,128)(2,1)S(1)} %copy-done), channel_id=1, source_target_pairs={{0,8},{8,0},{16,24},{24,16},{32,40},{40,32},{48,56},{56,48},{64,72... | collective-permute-start | bytes 786440 | tf_op jit(solution)/shard_map/ppermute | solution.py:265
  9.7 13.5 %collective-permute-start.4 = (bf16[32,4096]{1,0:T(8,128)(2,1)S(1)}, bf16[32,4096]{1,0:T(8,128)(2,1)S(1)}, u32[]{:S(2)}, u32[]{:S(2)}) collective-permute-start(bf16[32,4096]{1,0:T(8,128)(2,1)S(1)} %copy-done), channel_id=1, source_target_pairs={{0,16},{8,24},{16,0},{24,8},{32,48},{40,56},{48,32},{56,40},{64,80... | collective-permute-start | bytes 786440 | tf_op jit(solution)/shard_map/ppermute | solution.py:265
  12.3 13.4 %collective-permute-start.5 = (bf16[32,4096]{1,0:T(8,128)(2,1)S(1)}, bf16[32,4096]{1,0:T(8,128)(2,1)S(1)}, u32[]{:S(2)}, u32[]{:S(2)}) collective-permute-start(bf16[32,4096]{1,0:T(8,128)(2,1)S(1)} %copy-done), channel_id=1, source_target_pairs={{0,24},{8,16},{16,8},{24,0},{32,56},{40,48},{48,40},{56,32},{64,88... | collective-permute-start | bytes 786440 | tf_op jit(solution)/shard_map/ppermute | solution.py:265
  16.6 12.8 %collective-permute-start.2 = (f32[512,128]{1,0:T(8,128)S(1)}, f32[512,128]{1,0:T(8,128)S(1)}, u32[]{:S(2)}, u32[]{:S(2)}) collective-permute-start(f32[512,128]{1,0:T(8,128)S(1)} %add.10.total), channel_id=1, source_target_pairs={{0,6},{1,3},{2,4},{3,1},{4,2},{5,7},{6,0},{7,5},{8,14},{9,11},{10,... | collective-permute-start | bytes 786440 | tf_op jit(solution)/shard_map/ppermute | solution.py:19
  29.9 1.4 %collective-permute-start.6 = (f32[256,64]{1,0:T(8,128)S(1)}, f32[256,64]{1,0:T(8,128)S(1)}, u32[]{:S(2)}, u32[]{:S(2)}) collective-permute-start(f32[256,64]{1,0:T(8,128)S(1)} %features.1), channel_id=1, source_target_pairs={{0,1},{1,0},{2,3},{3,2},{4,5},{5,4},{6,7},{7,6},{8,9},{9,8},{10,11... | collective-permute-start | bytes 196616 | tf_op jit(solution)/shard_map/ppermute | solution.py:19

commit v9 on v8

--- a/solution.py
+++ b/solution.py
@@ -12,6 +12,7 @@
 Y = 4
 TOKENS = 1024
 STEP = 256
+EARLY = 128
 NT = (((1,), (1,)), ((), ()))
 
 
@@ -19,14 +20,13 @@
     return lax.ppermute(value, "tensor", [(i, i ^ (odd if i & 1 else even)) for i in range(8)])
 
 
-def token_block(ref, block):
-    return ref.at[pl.ds(pl.multiple_of(block * STEP, STEP), STEP)]
-
-
-def project_block(grads, acts, wide_out, wide_in, block, target, place):
-    here = pl.ds(pl.multiple_of(block * STEP, STEP), STEP)
-    there = pl.ds(pl.multiple_of(place * STEP, STEP), STEP)
-    target[there] = jnp.dot(grads[here], wide_out[...], preferred_element_type=jnp.float32) + jnp.dot(
+def tokens(ref, start, count):
+    return ref.at[pl.ds(pl.multiple_of(start, EARLY), count)]
+
+
+def project_rows(grads, acts, wide_out, wide_in, start, count):
+    here = pl.ds(start, count)
+    return jnp.dot(grads[here], wide_out[...], preferred_element_type=jnp.float32) + jnp.dot(
         acts[here], wide_in[...], preferred_element_type=jnp.float32
     )
 
@@ -34,56 +34,58 @@
 def project_early_kernel(
     out_grads, activations, proj_out, proj_in, send, first, grads_last, acts_last, wide_out, wide_in, grads, acts, raw_out, raw_in, sem
 ):
-    blocks = TOKENS // STEP
-    half = blocks // 2
+    half = TOKENS // 2
     core = lax.axis_index("tensor") & 1
-
-    def copies(block, to_grads, to_acts, place):
-        which = jnp.where(block < half, (1 - core) * half, core * half - half) + block
+    kept, sent = core * half, (1 - core) * half
+
+    def copies(slot, start, count, to_grads, to_acts, place):
         return (
-            pltpu.make_async_copy(token_block(out_grads, which), token_block(to_grads, place), sem.at[2 + 2 * block]),
-            pltpu.make_async_copy(token_block(activations, which), token_block(to_acts, place), sem.at[3 + 2 * block]),
+            pltpu.make_async_copy(tokens(out_grads, start, count), tokens(to_grads, place, count), sem.at[2 * slot]),
+            pltpu.make_async_copy(tokens(activations, start, count), tokens(to_acts, place, count), sem.at[2 * slot + 1]),
         )
 
+    def sent_copies(block):
+        return copies(1 + block, sent + block * STEP, STEP, grads, acts, block * STEP)
+
+    blocks = half // STEP
     weights = (
         pltpu.make_async_copy(proj_out, raw_out, sem.at[0]),
         pltpu.make_async_copy(proj_in, raw_in, sem.at[1]),
     )
-    last = copies(blocks - 1, grads_last, acts_last, 0)
+    near = copies(1 + blocks, kept, EARLY, grads, acts, half)
+    last = copies(2 + blocks, kept + EARLY, half - EARLY, grads_last, acts_last, 0)
     for copy in weights:
         copy.start()
-    for block in range(blocks - 1):
-        for copy in copies(block, grads, acts, block):
+    for block in range(blocks):
+        for copy in sent_copies(block):
             copy.start()
-    for copy in last:
+    for copy in near + last:
         copy.start()
     for copy in weights:
         copy.wait()
     wide_out[...] = jnp.concatenate([raw_out[...], jnp.zeros_like(raw_out)], axis=0).T
     wide_in[...] = jnp.concatenate([jnp.zeros_like(raw_in), raw_in[...]], axis=0).T
 
-    @pl.loop(0, half)
+    @pl.loop(0, blocks)
     def _(block):
-        for copy in copies(block, grads, acts, block):
+        for copy in sent_copies(block):
             copy.wait()
-        project_block(grads, acts, wide_out, wide_in, block, send, block)
-
-    @pl.loop(half, blocks - 1)
-    def _(block):
-        for copy in copies(block, grads, acts, block):
+        start = pl.multiple_of(block * STEP, STEP)
+        send[pl.ds(start, STEP)] = project_rows(grads, acts, wide_out, wide_in, start, STEP)
+
+    @pl.loop(0, 1)
+    def _(_):
+        for copy in near:
             copy.wait()
-        project_block(grads, acts, wide_out, wide_in, block, first, block - half)
+        first[...] = project_rows(grads, acts, wide_out, wide_in, half, EARLY)
 
     for copy in last:
         copy.wait()
 
 
 def project_late_kernel(first, grads, acts, wide_out, wide_in, keep):
-    keep[: first.shape[0]] = first[...]
-
-    @pl.loop(0, 1)
-    def _(block):
-        project_block(grads, acts, wide_out, wide_in, block, keep, block + first.shape[0] // STEP)
+    keep[:EARLY] = first[...]
+    keep[EARLY:] = project_rows(grads, acts, wide_out, wide_in, 0, grads.shape[0])
 
 
 def project(out_grads, activations, proj_out, proj_in, meanwhile):
@@ -97,18 +99,18 @@
         out_specs=[in_vmem] * 6,
         out_shape=[
             pltpu.VMEM((half, 2 * RANK), jnp.float32),
-            pltpu.VMEM((half - STEP, 2 * RANK), jnp.float32),
-            pltpu.VMEM((STEP, d), jnp.bfloat16),
-            pltpu.VMEM((STEP, ff), jnp.bfloat16),
+            pltpu.VMEM((EARLY, 2 * RANK), jnp.float32),
+            pltpu.VMEM((half - EARLY, d), jnp.bfloat16),
+            pltpu.VMEM((half - EARLY, ff), jnp.bfloat16),
             pltpu.VMEM((d, 2 * RANK), jnp.bfloat16),
             pltpu.VMEM((ff, 2 * RANK), jnp.bfloat16),
         ],
         scratch_shapes=[
-            pltpu.VMEM((TOKENS - STEP, d), jnp.bfloat16),
-            pltpu.VMEM((TOKENS - STEP, ff), jnp.bfloat16),
+            pltpu.VMEM((half + EARLY, d), jnp.bfloat16),
+            pltpu.VMEM((half + EARLY, ff), jnp.bfloat16),
             pltpu.VMEM((RANK, d), jnp.bfloat16),
             pltpu.VMEM((RANK, ff), jnp.bfloat16),
-            pltpu.SemaphoreType.DMA((2 + 2 * (TOKENS // STEP),)),
+            pltpu.SemaphoreType.DMA((2 * (half // STEP + 3),)),
         ],
         compiler_params=pltpu.CompilerParams(vmem_limit_bytes=24 << 20),
         name="project_early",
@@ -215,17 +217,15 @@
     line = jnp.zeros((Y * 8, blocks.shape[2]), jnp.float32)
     for first in range(0, N_DP, Y):
         chosen = (owner & ~(Y - 1)) == first
-        line = line + jnp.where(chosen, blocks[first : first + Y].astype(jnp.float32).reshape(line.shape), 0.0)
-    line = line.T.astype(blocks.dtype)
+        line = jnp.where(chosen, blocks[first : first + Y].astype(jnp.float32).reshape(line.shape), line)
     row = lax.broadcasted_iota(jnp.int32, (Y * 8, DOCS), 0)
     column = lax.broadcasted_iota(jnp.int32, (Y * 8, DOCS), 1)
-    spot = ((row >> 2) & 1) * 16 + (row >> 3) * 4 + (row & 3)
-    total = jnp.zeros_like(scores)
-    for x in range(DOCS // 32):
-        total = total + jnp.dot(
-            line[x * rows : (x + 1) * rows], (column == spot + 32 * x).astype(line.dtype),
-            preferred_element_type=jnp.float32,
-        )
+    spot = (column & 31) == ((row >> 2) & 1) * 16 + (row >> 3) * 4 + (row & 3)
+    wide = jnp.dot(line.T.astype(blocks.dtype), spot.astype(blocks.dtype), preferred_element_type=jnp.float32)
+    group = lax.broadcasted_iota(jnp.int32, scores.shape, 1) >> 5
+    total = wide[:rows]
+    for x in range(1, DOCS // 32):
+        total = jnp.where(group == x, wide[x * rows : (x + 1) * rows], total)
     scores[...] = total
 
 

time: 58.2 us -> 58 us (level)
  transfers between devices with their start and end apart: 7 -> 7, of which waited for: 6 -> 6; matrix products, arithmetic and copies ran while one was open for 0% -> 0% of each run, Pallas kernels for 1% -> 2%
where the time goes in v9:
time: 58 us; the launch traced here: 57.8 us
  blocking collectives  24.8 us (43%)
  starting transfers between devices  13 us (22%)
  waiting for transfers between devices  12.4 us (21%)
  Pallas kernels  7.33 us (13%)
    all_to_all x1, blocking collectives, shards(): return place(owners, lax.all_to_all(blocks, 'dp', 0, 0))  13.1 us
    all_to_all x1, blocking collectives, shards(): lax.all_to_all(spread(block, peers), 'dp', 0, 0, axis_index_groups=groups)  11.7 us
    ppermute x4, starting transfers between devices, swap(): lax.ppermute(value, 'tensor', [(i, i ^ (odd if i & 1 else even)) for i in...  9.48 us
    ppermute x4, waiting for transfers between devices, swap(): lax.ppermute(value, 'tensor', [(i, i ^ (odd if i & 1 else even)) for i in...  9.2 us
    pallas_call x1, Pallas kernels, project(): pl.pallas_call(project_early_kernel, in_specs=[in_hbm] * 4, out_specs=[in...  4.07 us
    ppermute x3, starting transfers between devices, shards(): lax.ppermute(queries, 'dp', [(i, i ^ step) for i in range(N_DP)])  3.49 us
    ppermute x3, waiting for transfers between devices, shards(): lax.ppermute(queries, 'dp', [(i, i ^ step) for i in range(N_DP)])  3.19 us
  transfers between devices with their start and end apart: 7, of which 6 were waited for; matrix products, arithmetic and copies ran while one was open for 0% of the time, Pallas kernels for 2%

profile of v9, /device:TPU:8, one launch (start us, length us, event | category | flops | bytes accessed | tf_op | source)
XLA Modules:
  0.0 57.8 jit_solution(3984914149608324800)
XLA Ops:
  0.0 4.1 %project_early.1 = (f32[512,128]{1,0:T(8,128)S(1)}, f32[128,128]{1,0:T(8,128)S(1)}, bf16[384,1024]{1,0:T(8,128)(2,1)S(1)}, bf16[384,3584]{1,0:T(8,128)(2,1)S(1)}...) custom-call(bf16[1024,1024]{1,0:T(8,128)(2,1)} %out_grads.1, bf16[1024,3584]{1,0:T(8,128)(2,1)} %activations.1, ...), custom_call_target="tpu_custom_call" | custom-call | tf_op jit(solution)/shard_map/project_early/pallas_call | solution.py:96
  4.1 0.1 collective-permute-start
  4.2 0.0 copy-start
  4.2 0.0 copy-start.2
  4.2 1.1 %project_late.1 = f32[512,128]{1,0:T(8,128)S(1)} custom-call(f32[128,128]{1,0:T(8,128)S(1)} %get-tuple-element.20.first, bf16[384,1024]{1,0:T(8,128)(2,1)S(1)} %get-tuple-element.21.grads, bf16[384,3584]{1,0:T(8,128)(2,1)S(1)} %get-tuple-element.22.acts, bf16[1024,128]{1,0:T(8,128)(2,1)S(1)} %get-tuple-element.23.wide_out, ...), custom_call_target="tpu_custom_call" | custom-call | flops 603979776 | bytes 4718592 | tf_op jit(solution)/shard_map/project_late/pallas_call | solution.py:119
  5.3 0.0 copy-start.1
  5.3 0.4 collective-permute-done
  5.7 3.4 %collective-permute-start.1 = (f32[512,128]{1,0:T(8,128)S(1)}, f32[512,128]{1,0:T(8,128)S(1)}, u32[]{:S(2)}, u32[]{:S(2)}) collective-permute-start(f32[512,128]{1,0:T(8,128)S(1)} %add.9), channel_id=1, source_target_pairs={{0,2},{1,7},{2,0},{3,5},{4,6},{5,3},{6,4},{7,1},{8,10},{9,15},{10,... | collective-permute-start | bytes 786440 | tf_op jit(solution)/shard_map/ppermute | solution.py:20
  9.1 0.0 copy-done
  9.1 0.4 collective-permute-start.3
  9.5 2.6 %collective-permute-start.4 = (bf16[32,4096]{1,0:T(8,128)(2,1)S(1)}, bf16[32,4096]{1,0:T(8,128)(2,1)S(1)}, u32[]{:S(2)}, u32[]{:S(2)}) collective-permute-start(bf16[32,4096]{1,0:T(8,128)(2,1)S(1)} %copy-done), channel_id=1, source_target_pairs={{0,16},{8,24},{16,0},{24,8},{32,48},{40,56},{48,32},{56,40},{64,80... | collective-permute-start | bytes 786440 | tf_op jit(solution)/shard_map/ppermute | solution.py:265
  12.1 0.5 collective-permute-start.5
  12.6 3.8 %collective-permute-done.1 = f32[512,128]{1,0:T(8,128)S(1)} collective-permute-done((f32[512,128]{1,0:T(8,128)S(1)}, f32[512,128]{1,0:T(8,128)S(1)}, u32[]{:S(2)}, u32[]{:S(2)}) %collective-permute-start.1) | collective-permute-done | bytes 262176 | tf_op jit(solution)/shard_map/ppermute | solution.py:20
  16.4 5.9 %collective-permute-start.2 = (f32[512,128]{1,0:T(8,128)S(1)}, f32[512,128]{1,0:T(8,128)S(1)}, u32[]{:S(2)}, u32[]{:S(2)}) collective-permute-start(f32[512,128]{1,0:T(8,128)S(1)} %add.10.total), channel_id=1, source_target_pairs={{0,6},{1,3},{2,4},{3,1},{4,2},{5,7},{6,0},{7,5},{8,14},{9,11},{10,... | collective-permute-start | bytes 786440 | tf_op jit(solution)/shard_map/ppermute | solution.py:20
  22.3 0.0 copy-done.2
  22.3 0.0 collective-permute-done.3.refs_1_
  22.3 0.7 %collective-permute-done.4.refs_2_ = bf16[32,4096]{1,0:T(8,128)(2,1)S(1)} collective-permute-done((bf16[32,4096]{1,0:T(8,128)(2,1)S(1)}, bf16[32,4096]{1,0:T(8,128)(2,1)S(1)}, u32[]{:S(2)}, u32[]{:S(2)}) %collective-permute-start.4) | collective-permute-done | bytes 262176 | tf_op jit(solution)/shard_map/ppermute | solution.py:265
  23.0 2.5 %collective-permute-done.5.refs_3_ = bf16[32,4096]{1,0:T(8,128)(2,1)S(1)} collective-permute-done((bf16[32,4096]{1,0:T(8,128)(2,1)S(1)}, bf16[32,4096]{1,0:T(8,128)(2,1)S(1)}, u32[]{:S(2)}, u32[]{:S(2)}) %collective-permute-start.5) | collective-permute-done | bytes 262176 | tf_op jit(solution)/shard_map/ppermute | solution.py:265
  25.5 3.7 %collective-permute-done.2.more = f32[512,128]{1,0:T(8,128)S(1)} collective-permute-done((f32[512,128]{1,0:T(8,128)S(1)}, f32[512,128]{1,0:T(8,128)S(1)}, u32[]{:S(2)}, u32[]{:S(2)}) %collective-permute-start.2) | collective-permute-done | bytes 262176 | tf_op jit(solution)/shard_map/ppermute | solution.py:20
  29.2 0.5 features.1
  29.7 0.1 collective-permute-start.6
  29.8 1.3 %collective-permute-done.6 = f32[256,64]{1,0:T(8,128)S(1)} collective-permute-done((f32[256,64]{1,0:T(8,128)S(1)}, f32[256,64]{1,0:T(8,128)S(1)}, u32[]{:S(2)}, u32[]{:S(2)}) %collective-permute-start.6) | collective-permute-done | bytes 65568 | tf_op jit(solution)/shard_map/ppermute | solution.py:20
  31.2 0.1 reshape.13
  31.3 11.7 %all_to_all.10 = bf16[8,8,2048]{2,1,0:T(8,128)(2,1)S(1)} all-to-all(bf16[8,8,2048]{2,1,0:T(8,128)(2,1)S(1)} %spread.1), channel_id=1, replica_groups={{0,32,64,96,128,160,192,224},{8,40,72,104,136,168,200,232},{16,48,80,11..., dimensions={0} | all-to-all | bytes 524288 | tf_op jit(solution)/shard_map/all_to_all | solution.py:275
  43.0 0.0 copy-done.1
  43.0 0.8 %score.1 = bf16[32,8,128]{2,1,0:T(8,128)(2,1)S(1)} custom-call(s32[1,32]{1,0:T(1,128)S(1)} %bitcast.6, bf16[64,2048]{1,0:T(8,128)(2,1)S(1)} %bitcast.5, bf16[32,4096]{1,0:T(8,128)(2,1)S(1)} %copy-done, bf16[32,4096]{1,0:T(8,128)(2,1)S(1)} %collective-permute-done.3.refs_1_, bf16[32,4096]{1,0:T(8,128)(2,1)S(1)} %collective-permute-done.4.refs_2_, ...), custom_call_target="tpu_custom_call" | custom-call | tf_op jit(solution)/shard_map/score/pallas_call | solution.py:203
  43.8 13.1 %all_to_all.11.blocks = bf16[32,8,128]{2,1,0:T(8,128)(2,1)S(1)} all-to-all(bf16[32,8,128]{2,1,0:T(8,128)(2,1)S(1)} %score.1), channel_id=1, replica_groups=mesh['dp'=32,'tensor'=8] {'dp'}, dimensions={0} | all-to-all | bytes 131072 | tf_op jit(solution)/shard_map/all_to_all | solution.py:279
  56.9 0.9 %place.1 = f32[32,128]{1,0:T(8,128)} custom-call(s32[1,32]{1,0:T(1,128)S(1)} %bitcast.7, bf16[32,8,128]{2,1,0:T(8,128)(2,1)S(1)} %all_to_all.11.blocks), custom_call_target="tpu_custom_call" | custom-call | tf_op jit(solution)/shard_map/place/pallas_call | solution.py:233
  (7 shorter events, 0.1 us)
Async XLA Ops:
  4.1 1.6 %collective-permute-start = (f32[512,128]{1,0:T(8,128)S(1)}, f32[512,128]{1,0:T(8,128)S(1)}, u32[]{:S(2)}, u32[]{:S(2)}) collective-permute-start(f32[512,128]{1,0:T(8,128)S(1)} %get-tuple-element.25), channel_id=1, source_target_pairs={{0,1},{1,0},{2,3},{3,2},{4,5},{5,4},{6,7},{7,6},{8,9},{9,8},{10,11... | collective-permute-start | bytes 786440 | tf_op jit(solution)/shard_map/ppermute | solution.py:20
  4.2 4.9 %copy-start = (bf16[32,4096]{1,0:T(8,128)(2,1)S(1)}, bf16[32,4096]{1,0:T(8,128)(2,1)}, u32[]{:S(2)}) copy-start(bf16[32,4096]{1,0:T(8,128)(2,1)} %refs_0_) | copy-start | bytes 786436
  4.2 18.1 %copy-start.2 = (s32[1,1024]{1,0:T(1,128)S(1)}, s32[1,1024]{1,0:T(1,128)}, u32[]{:S(2)}) copy-start(s32[1,1024]{1,0:T(1,128)} %param.11) | copy-start | bytes 12292
  5.3 37.7 %copy-start.1 = (s32[32]{0:T(128)S(1)}, s32[32]{0:T(128)}, u32[]{:S(2)}) copy-start(s32[32]{0:T(128)} %param.13) | copy-start | bytes 388
  5.7 10.6 %collective-permute-start.1 = (f32[512,128]{1,0:T(8,128)S(1)}, f32[512,128]{1,0:T(8,128)S(1)}, u32[]{:S(2)}, u32[]{:S(2)}) collective-permute-start(f32[512,128]{1,0:T(8,128)S(1)} %add.9), channel_id=1, source_target_pairs={{0,2},{1,7},{2,0},{3,5},{4,6},{5,3},{6,4},{7,1},{8,10},{9,15},{10,... | collective-permute-start | bytes 786440 | tf_op jit(solution)/shard_map/ppermute | solution.py:20
  9.1 13.2 %collective-permute-start.3 = (bf16[32,4096]{1,0:T(8,128)(2,1)S(1)}, bf16[32,4096]{1,0:T(8,128)(2,1)S(1)}, u32[]{:S(2)}, u32[]{:S(2)}) collective-permute-start(bf16[32,4096]{1,0:T(8,128)(2,1)S(1)} %copy-done), channel_id=1, source_target_pairs={{0,8},{8,0},{16,24},{24,16},{32,40},{40,32},{48,56},{56,48},{64,72... | collective-permute-start | bytes 786440 | tf_op jit(solution)/shard_map/ppermute | solution.py:265
  9.5 13.5 %collective-permute-start.4 = (bf16[32,4096]{1,0:T(8,128)(2,1)S(1)}, bf16[32,4096]{1,0:T(8,128)(2,1)S(1)}, u32[]{:S(2)}, u32[]{:S(2)}) collective-permute-start(bf16[32,4096]{1,0:T(8,128)(2,1)S(1)} %copy-done), channel_id=1, source_target_pairs={{0,16},{8,24},{16,0},{24,8},{32,48},{40,56},{48,32},{56,40},{64,80... | collective-permute-start | bytes 786440 | tf_op jit(solution)/shard_map/ppermute | solution.py:265
  12.1 13.4 %collective-permute-start.5 = (bf16[32,4096]{1,0:T(8,128)(2,1)S(1)}, bf16[32,4096]{1,0:T(8,128)(2,1)S(1)}, u32[]{:S(2)}, u32[]{:S(2)}) collective-permute-start(bf16[32,4096]{1,0:T(8,128)(2,1)S(1)} %copy-done), channel_id=1, source_target_pairs={{0,24},{8,16},{16,8},{24,0},{32,56},{40,48},{48,40},{56,32},{64,88... | collective-permute-start | bytes 786440 | tf_op jit(solution)/shard_map/ppermute | solution.py:265
  16.4 12.8 %collective-permute-start.2 = (f32[512,128]{1,0:T(8,128)S(1)}, f32[512,128]{1,0:T(8,128)S(1)}, u32[]{:S(2)}, u32[]{:S(2)}) collective-permute-start(f32[512,128]{1,0:T(8,128)S(1)} %add.10.total), channel_id=1, source_target_pairs={{0,6},{1,3},{2,4},{3,1},{4,2},{5,7},{6,0},{7,5},{8,14},{9,11},{10,... | collective-permute-start | bytes 786440 | tf_op jit(solution)/shard_map/ppermute | solution.py:20
  29.7 1.4 %collective-permute-start.6 = (f32[256,64]{1,0:T(8,128)S(1)}, f32[256,64]{1,0:T(8,128)S(1)}, u32[]{:S(2)}, u32[]{:S(2)}) collective-permute-start(f32[256,64]{1,0:T(8,128)S(1)} %features.1), channel_id=1, source_target_pairs={{0,1},{1,0},{2,3},{3,2},{4,5},{5,4},{6,7},{7,6},{8,9},{9,8},{10,11... | collective-permute-start | bytes 196616 | tf_op jit(solution)/shard_map/ppermute | solution.py:20

commit v10 on v9

--- a/solution.py
+++ b/solution.py
@@ -137,7 +137,7 @@
     return high, middle, (rest - middle.astype(jnp.float32)).astype(jnp.bfloat16)
 
 
-def features_kernel(ids, total, more, feat):
+def features_kernel(ids, total, more, feat, wide):
     parts = thirds(total[...] + more[...])
     right = jnp.concatenate([part[:, RANK:] for part in parts], axis=1)
 
@@ -150,13 +150,16 @@
         for i, part in enumerate(parts)
     ]
     least = (low + high[:, 2 * RANK :]) + middle[:, RANK:]
-    feat[...] = least + ((middle[:, :RANK] + high[:, RANK : 2 * RANK]) + high[:, :RANK])
+    wide[...] = least + ((middle[:, :RANK] + high[:, RANK : 2 * RANK]) + high[:, :RANK])
+    count = feat.shape[0]
+    feat[...] = jnp.concatenate([wide[pl.ds(0, count, stride=2)], wide[pl.ds(1, count, stride=2)]], axis=1)
 
 
 def features(ids, total, more):
     return pl.pallas_call(
         features_kernel,
-        out_shape=jax.ShapeDtypeStruct((DOCS_DEV * RANK, RANK), jnp.float32),
+        out_shape=jax.ShapeDtypeStruct((DOCS_DEV * RANK // 2, 2 * RANK), jnp.float32),
+        scratch_shapes=[pltpu.VMEM((DOCS_DEV * RANK, RANK), jnp.float32)],
         compiler_params=pltpu.CompilerParams(vmem_limit_bytes=16 << 20),
         name="features",
     )(ids, total, more)

time: 58 us -> 57.9 us (level)
  no operation moved by 1% of the time
where the time goes in v10:
time: 57.9 us; the launch traced here: 57.7 us
  blocking collectives  24.8 us (43%)
  starting transfers between devices  13 us (22%)
  waiting for transfers between devices  12.3 us (21%)
  Pallas kernels  7.43 us (13%)
    all_to_all x1, blocking collectives, shards(): return place(owners, lax.all_to_all(blocks, 'dp', 0, 0))  13.1 us
    all_to_all x1, blocking collectives, shards(): lax.all_to_all(spread(block, peers), 'dp', 0, 0, axis_index_groups=groups)  11.7 us
    ppermute x4, starting transfers between devices, swap(): lax.ppermute(value, 'tensor', [(i, i ^ (odd if i & 1 else even)) for i in...  9.47 us
    ppermute x4, waiting for transfers between devices, swap(): lax.ppermute(value, 'tensor', [(i, i ^ (odd if i & 1 else even)) for i in...  9.1 us
    pallas_call x1, Pallas kernels, project(): pl.pallas_call(project_early_kernel, in_specs=[in_hbm] * 4, out_specs=[in...  4.07 us
    ppermute x3, starting transfers between devices, shards(): lax.ppermute(queries, 'dp', [(i, i ^ step) for i in range(N_DP)])  3.49 us
    ppermute x3, waiting for transfers between devices, shards(): lax.ppermute(queries, 'dp', [(i, i ^ step) for i in range(N_DP)])  3.19 us
  transfers between devices with their start and end apart: 7, of which 6 were waited for; matrix products, arithmetic and copies ran while one was open for 0% of the time, Pallas kernels for 2%

profile of v10, /device:TPU:8, one launch (start us, length us, event | category | flops | bytes accessed | tf_op | source)
XLA Modules:
  0.0 57.7 jit_solution(2331805608376705629)
XLA Ops:
  0.0 4.1 %project_early.1 = (f32[512,128]{1,0:T(8,128)S(1)}, f32[128,128]{1,0:T(8,128)S(1)}, bf16[384,1024]{1,0:T(8,128)(2,1)S(1)}, bf16[384,3584]{1,0:T(8,128)(2,1)S(1)}...) custom-call(bf16[1024,1024]{1,0:T(8,128)(2,1)} %out_grads.1, bf16[1024,3584]{1,0:T(8,128)(2,1)} %activations.1, ...), custom_call_target="tpu_custom_call" | custom-call | tf_op jit(solution)/shard_map/project_early/pallas_call | solution.py:96
  4.1 0.1 collective-permute-start
  4.2 0.0 copy-start
  4.2 0.0 copy-start.2
  4.2 1.1 %project_late.1 = f32[512,128]{1,0:T(8,128)S(1)} custom-call(f32[128,128]{1,0:T(8,128)S(1)} %get-tuple-element.20.first, bf16[384,1024]{1,0:T(8,128)(2,1)S(1)} %get-tuple-element.21.grads, bf16[384,3584]{1,0:T(8,128)(2,1)S(1)} %get-tuple-element.22.acts, bf16[1024,128]{1,0:T(8,128)(2,1)S(1)} %get-tuple-element.23.wide_out, ...), custom_call_target="tpu_custom_call" | custom-call | flops 603979776 | bytes 4718592 | tf_op jit(solution)/shard_map/project_late/pallas_call | solution.py:119
  5.3 0.0 copy-start.1
  5.3 0.4 collective-permute-done
  5.7 3.4 %collective-permute-start.1 = (f32[512,128]{1,0:T(8,128)S(1)}, f32[512,128]{1,0:T(8,128)S(1)}, u32[]{:S(2)}, u32[]{:S(2)}) collective-permute-start(f32[512,128]{1,0:T(8,128)S(1)} %add.9), channel_id=1, source_target_pairs={{0,2},{1,7},{2,0},{3,5},{4,6},{5,3},{6,4},{7,1},{8,10},{9,15},{10,... | collective-permute-start | bytes 786440 | tf_op jit(solution)/shard_map/ppermute | solution.py:20
  9.1 0.0 copy-done
  9.1 0.4 collective-permute-start.3
  9.5 2.6 %collective-permute-start.4 = (bf16[32,4096]{1,0:T(8,128)(2,1)S(1)}, bf16[32,4096]{1,0:T(8,128)(2,1)S(1)}, u32[]{:S(2)}, u32[]{:S(2)}) collective-permute-start(bf16[32,4096]{1,0:T(8,128)(2,1)S(1)} %copy-done), channel_id=1, source_target_pairs={{0,16},{8,24},{16,0},{24,8},{32,48},{40,56},{48,32},{56,40},{64,80... | collective-permute-start | bytes 786440 | tf_op jit(solution)/shard_map/ppermute | solution.py:268
  12.1 0.5 collective-permute-start.5
  12.6 3.8 %collective-permute-done.1 = f32[512,128]{1,0:T(8,128)S(1)} collective-permute-done((f32[512,128]{1,0:T(8,128)S(1)}, f32[512,128]{1,0:T(8,128)S(1)}, u32[]{:S(2)}, u32[]{:S(2)}) %collective-permute-start.1) | collective-permute-done | bytes 262176 | tf_op jit(solution)/shard_map/ppermute | solution.py:20
  16.4 5.9 %collective-permute-start.2 = (f32[512,128]{1,0:T(8,128)S(1)}, f32[512,128]{1,0:T(8,128)S(1)}, u32[]{:S(2)}, u32[]{:S(2)}) collective-permute-start(f32[512,128]{1,0:T(8,128)S(1)} %add.10.total), channel_id=1, source_target_pairs={{0,6},{1,3},{2,4},{3,1},{4,2},{5,7},{6,0},{7,5},{8,14},{9,11},{10,... | collective-permute-start | bytes 786440 | tf_op jit(solution)/shard_map/ppermute | solution.py:20
  22.3 0.0 copy-done.2
  22.3 0.0 collective-permute-done.3.refs_1_
  22.3 0.7 %collective-permute-done.4.refs_2_ = bf16[32,4096]{1,0:T(8,128)(2,1)S(1)} collective-permute-done((bf16[32,4096]{1,0:T(8,128)(2,1)S(1)}, bf16[32,4096]{1,0:T(8,128)(2,1)S(1)}, u32[]{:S(2)}, u32[]{:S(2)}) %collective-permute-start.4) | collective-permute-done | bytes 262176 | tf_op jit(solution)/shard_map/ppermute | solution.py:268
  23.0 2.5 %collective-permute-done.5.refs_3_ = bf16[32,4096]{1,0:T(8,128)(2,1)S(1)} collective-permute-done((bf16[32,4096]{1,0:T(8,128)(2,1)S(1)}, bf16[32,4096]{1,0:T(8,128)(2,1)S(1)}, u32[]{:S(2)}, u32[]{:S(2)}) %collective-permute-start.5) | collective-permute-done | bytes 262176 | tf_op jit(solution)/shard_map/ppermute | solution.py:268
  25.5 3.7 %collective-permute-done.2.more = f32[512,128]{1,0:T(8,128)S(1)} collective-permute-done((f32[512,128]{1,0:T(8,128)S(1)}, f32[512,128]{1,0:T(8,128)S(1)}, u32[]{:S(2)}, u32[]{:S(2)}) %collective-permute-start.2) | collective-permute-done | bytes 262176 | tf_op jit(solution)/shard_map/ppermute | solution.py:20
  29.2 0.6 %features.1 = f32[128,128]{1,0:T(8,128)S(1)} custom-call(s32[1,512]{1,0:T(1,128)S(1)} %broadcast_select_fusion.ids, f32[512,128]{1,0:T(8,128)S(1)} %add.10.total, f32[512,128]{1,0:T(8,128)S(1)} %collective-permute-done.2.more), custom_call_target="tpu_custom_call" | custom-call | tf_op jit(solution)/shard_map/features/pallas_call | solution.py:159
  29.8 0.1 collective-permute-start.6
  29.9 1.2 %collective-permute-done.6 = f32[128,128]{1,0:T(8,128)S(1)} collective-permute-done((f32[128,128]{1,0:T(8,128)S(1)}, f32[128,128]{1,0:T(8,128)S(1)}, u32[]{:S(2)}, u32[]{:S(2)}) %collective-permute-start.6) | collective-permute-done | bytes 65568 | tf_op jit(solution)/shard_map/ppermute | solution.py:20
  31.2 11.7 %all_to_all.10 = bf16[8,8,2048]{2,1,0:T(8,128)(2,1)S(1)} all-to-all(bf16[8,8,2048]{2,1,0:T(8,128)(2,1)S(1)} %spread.1), channel_id=1, replica_groups={{0,32,64,96,128,160,192,224},{8,40,72,104,136,168,200,232},{16,48,80,11..., dimensions={0} | all-to-all | bytes 524288 | tf_op jit(solution)/shard_map/all_to_all | solution.py:278
  42.9 0.0 copy-done.1
  42.9 0.8 %score.1 = bf16[32,8,128]{2,1,0:T(8,128)(2,1)S(1)} custom-call(s32[1,32]{1,0:T(1,128)S(1)} %bitcast.8, bf16[64,2048]{1,0:T(8,128)(2,1)S(1)} %bitcast.7, bf16[32,4096]{1,0:T(8,128)(2,1)S(1)} %copy-done, bf16[32,4096]{1,0:T(8,128)(2,1)S(1)} %collective-permute-done.3.refs_1_, bf16[32,4096]{1,0:T(8,128)(2,1)S(1)} %collective-permute-done.4.refs_2_, ...), custom_call_target="tpu_custom_call" | custom-call | tf_op jit(solution)/shard_map/score/pallas_call | solution.py:206
  43.7 13.1 %all_to_all.11.blocks = bf16[32,8,128]{2,1,0:T(8,128)(2,1)S(1)} all-to-all(bf16[32,8,128]{2,1,0:T(8,128)(2,1)S(1)} %score.1), channel_id=1, replica_groups=mesh['dp'=32,'tensor'=8] {'dp'}, dimensions={0} | all-to-all | bytes 131072 | tf_op jit(solution)/shard_map/all_to_all | solution.py:282
  56.8 0.9 %place.1 = f32[32,128]{1,0:T(8,128)} custom-call(s32[1,32]{1,0:T(1,128)S(1)} %bitcast.9, bf16[32,8,128]{2,1,0:T(8,128)(2,1)S(1)} %all_to_all.11.blocks), custom_call_target="tpu_custom_call" | custom-call | tf_op jit(solution)/shard_map/place/pallas_call | solution.py:236
  (8 shorter events, 0.1 us)
Async XLA Ops:
  4.1 1.6 %collective-permute-start = (f32[512,128]{1,0:T(8,128)S(1)}, f32[512,128]{1,0:T(8,128)S(1)}, u32[]{:S(2)}, u32[]{:S(2)}) collective-permute-start(f32[512,128]{1,0:T(8,128)S(1)} %get-tuple-element.25), channel_id=1, source_target_pairs={{0,1},{1,0},{2,3},{3,2},{4,5},{5,4},{6,7},{7,6},{8,9},{9,8},{10,11... | collective-permute-start | bytes 786440 | tf_op jit(solution)/shard_map/ppermute | solution.py:20
  4.2 4.9 %copy-start = (bf16[32,4096]{1,0:T(8,128)(2,1)S(1)}, bf16[32,4096]{1,0:T(8,128)(2,1)}, u32[]{:S(2)}) copy-start(bf16[32,4096]{1,0:T(8,128)(2,1)} %refs_0_) | copy-start | bytes 786436
  4.2 18.1 %copy-start.2 = (s32[1,1024]{1,0:T(1,128)S(1)}, s32[1,1024]{1,0:T(1,128)}, u32[]{:S(2)}) copy-start(s32[1,1024]{1,0:T(1,128)} %param.11) | copy-start | bytes 12292
  5.3 37.6 %copy-start.1 = (s32[32]{0:T(128)S(1)}, s32[32]{0:T(128)}, u32[]{:S(2)}) copy-start(s32[32]{0:T(128)} %param.13) | copy-start | bytes 388
  5.7 10.6 %collective-permute-start.1 = (f32[512,128]{1,0:T(8,128)S(1)}, f32[512,128]{1,0:T(8,128)S(1)}, u32[]{:S(2)}, u32[]{:S(2)}) collective-permute-start(f32[512,128]{1,0:T(8,128)S(1)} %add.9), channel_id=1, source_target_pairs={{0,2},{1,7},{2,0},{3,5},{4,6},{5,3},{6,4},{7,1},{8,10},{9,15},{10,... | collective-permute-start | bytes 786440 | tf_op jit(solution)/shard_map/ppermute | solution.py:20
  9.1 13.2 %collective-permute-start.3 = (bf16[32,4096]{1,0:T(8,128)(2,1)S(1)}, bf16[32,4096]{1,0:T(8,128)(2,1)S(1)}, u32[]{:S(2)}, u32[]{:S(2)}) collective-permute-start(bf16[32,4096]{1,0:T(8,128)(2,1)S(1)} %copy-done), channel_id=1, source_target_pairs={{0,8},{8,0},{16,24},{24,16},{32,40},{40,32},{48,56},{56,48},{64,72... | collective-permute-start | bytes 786440 | tf_op jit(solution)/shard_map/ppermute | solution.py:268
  9.5 13.5 %collective-permute-start.4 = (bf16[32,4096]{1,0:T(8,128)(2,1)S(1)}, bf16[32,4096]{1,0:T(8,128)(2,1)S(1)}, u32[]{:S(2)}, u32[]{:S(2)}) collective-permute-start(bf16[32,4096]{1,0:T(8,128)(2,1)S(1)} %copy-done), channel_id=1, source_target_pairs={{0,16},{8,24},{16,0},{24,8},{32,48},{40,56},{48,32},{56,40},{64,80... | collective-permute-start | bytes 786440 | tf_op jit(solution)/shard_map/ppermute | solution.py:268
  12.1 13.4 %collective-permute-start.5 = (bf16[32,4096]{1,0:T(8,128)(2,1)S(1)}, bf16[32,4096]{1,0:T(8,128)(2,1)S(1)}, u32[]{:S(2)}, u32[]{:S(2)}) collective-permute-start(bf16[32,4096]{1,0:T(8,128)(2,1)S(1)} %copy-done), channel_id=1, source_target_pairs={{0,24},{8,16},{16,8},{24,0},{32,56},{40,48},{48,40},{56,32},{64,88... | collective-permute-start | bytes 786440 | tf_op jit(solution)/shard_map/ppermute | solution.py:268
  16.4 12.8 %collective-permute-start.2 = (f32[512,128]{1,0:T(8,128)S(1)}, f32[512,128]{1,0:T(8,128)S(1)}, u32[]{:S(2)}, u32[]{:S(2)}) collective-permute-start(f32[512,128]{1,0:T(8,128)S(1)} %add.10.total), channel_id=1, source_target_pairs={{0,6},{1,3},{2,4},{3,1},{4,2},{5,7},{6,0},{7,5},{8,14},{9,11},{10,... | collective-permute-start | bytes 786440 | tf_op jit(solution)/shard_map/ppermute | solution.py:20
  29.8 1.3 %collective-permute-start.6 = (f32[128,128]{1,0:T(8,128)S(1)}, f32[128,128]{1,0:T(8,128)S(1)}, u32[]{:S(2)}, u32[]{:S(2)}) collective-permute-start(f32[128,128]{1,0:T(8,128)S(1)} %features.1), channel_id=1, source_target_pairs={{0,1},{1,0},{2,3},{3,2},{4,5},{5,4},{6,7},{7,6},{8,9},{9,8},{10,11... | collective-permute-start | bytes 196616 | tf_op jit(solution)/shard_map/ppermute | solution.py:20
